TPU v7x, 32 devices: a whole 2x2x4 slice. The times are simulated.
32 devices in a mesh: dp: 8 (over y, x, core), mp: 4 (over z).
Axes of the slice: x: 2, y: 2, z: 4, core: 2. Of those that a mesh axis runs over, the one named last changes fastest.
Arguments:
- inputs: bfloat16 [8192, 2560], P('dp'), may hold values from -6 to 6
- cotangent: bfloat16 [8192, 2560], P('dp'), may hold values from -6 to 6
- norm_gains: float32 [6144], P('dp'), may hold values from 0.5 to 1.5
- norm_gains_first: float32 [6144], P('dp'), may hold values from -96 to 96
- norm_gains_second: float32 [6144], P('dp'), may hold values from 969.5232 to 3870.72
- query_down: float32 [2560, 768], P(('dp', 'mp')), may hold values from -0.125 to 0.125
- query_down_first: float32 [2560, 768], P(('dp', 'mp')), may hold values from -40 to 40
- query_down_second: float32 [2560, 768], P(('dp', 'mp')), may hold values from 211.14061 to 842.9568
- latent_down: float32 [2560, 288], P(('dp', 'mp')), may hold values from -0.125 to 0.125
- latent_down_first: float32 [2560, 288], P(('dp', 'mp')), may hold values from -128 to 128
- latent_down_second: float32 [2560, 288], P(('dp', 'mp')), may hold values from 1723.5968 to 6881.28
- query_up: float32 [768, 3840], P('dp', 'mp'), may hold values from -0.21875 to 0.21875
- query_up_first: float32 [768, 3840], P('dp', 'mp'), may hold values from -16 to 16
- query_up_second: float32 [768, 3840], P('dp', 'mp'), may hold values from 38.78093 to 154.8288
- latent_up: float32 [256, 5120], P('dp', 'mp'), may hold values from -0.375 to 0.375
- latent_up_first: float32 [256, 5120], P('dp', 'mp'), may hold values from -32 to 32
- latent_up_second: float32 [256, 5120], P('dp', 'mp'), may hold values from 155.12372 to 619.3152
- out_proj: float32 [2560, 2560], P('mp', 'dp'), may hold values from -4 to 4
- out_proj_first: float32 [2560, 2560], P('mp', 'dp'), may hold values from -2.5 to 2.5
- out_proj_second: float32 [2560, 2560], P('mp', 'dp'), may hold values from 0.6894387 to 2.752512
- ffn_gate: float32 [2560, 6400], P('dp', 'mp'), may hold values from -0.125 to 0.125
- ffn_gate_first: float32 [2560, 6400], P('dp', 'mp'), may hold values from -48 to 48
- ffn_gate_second: float32 [2560, 6400], P('dp', 'mp'), may hold values from 275.77548 to 1101.0048
- ffn_up: float32 [2560, 6400], P('dp', 'mp'), may hold values from -0.125 to 0.125
- ffn_up_first: float32 [2560, 6400], P('dp', 'mp'), may hold values from -48 to 48
- ffn_up_second: float32 [2560, 6400], P('dp', 'mp'), may hold values from 275.77548 to 1101.0048
- ffn_down: float32 [6400, 2560], P('mp', 'dp'), may hold values from -0.875 to 0.875
- ffn_down_first: float32 [6400, 2560], P('mp', 'dp'), may hold values from -6 to 6
- ffn_down_second: float32 [6400, 2560], P('mp', 'dp'), may hold values from 4.308992 to 17.2032
Outputs:
- output: bfloat16 [8192, 2560], P('dp')
- input_grad: float32 [8192, 2560], P('dp')
- norm_gains_first_new: float32 [6144], P('dp')
- norm_gains_second_new: float32 [6144], P('dp')
- norm_gains_new: float32 [6144], P('dp')
- query_down_first_new: float32 [2560, 768], P(('dp', 'mp'))
- query_down_second_new: float32 [2560, 768], P(('dp', 'mp'))
- query_down_new: float32 [2560, 768], P(('dp', 'mp'))
- latent_down_first_new: float32 [2560, 288], P(('dp', 'mp'))
- latent_down_second_new: float32 [2560, 288], P(('dp', 'mp'))
- latent_down_new: float32 [2560, 288], P(('dp', 'mp'))
- query_up_first_new: float32 [768, 3840], P('dp', 'mp')
- query_up_second_new: float32 [768, 3840], P('dp', 'mp')
- query_up_new: float32 [768, 3840], P('dp', 'mp')
- latent_up_first_new: float32 [256, 5120], P('dp', 'mp')
- latent_up_second_new: float32 [256, 5120], P('dp', 'mp')
- latent_up_new: float32 [256, 5120], P('dp', 'mp')
- out_proj_first_new: float32 [2560, 2560], P('mp', 'dp')
- out_proj_second_new: float32 [2560, 2560], P('mp', 'dp')
- out_proj_new: float32 [2560, 2560], P('mp', 'dp')
- ffn_gate_first_new: float32 [2560, 6400], P('dp', 'mp')
- ffn_gate_second_new: float32 [2560, 6400], P('dp', 'mp')
- ffn_gate_new: float32 [2560, 6400], P('dp', 'mp')
- ffn_up_first_new: float32 [2560, 6400], P('dp', 'mp')
- ffn_up_second_new: float32 [2560, 6400], P('dp', 'mp')
- ffn_up_new: float32 [2560, 6400], P('dp', 'mp')
- ffn_down_first_new: float32 [6400, 2560], P('mp', 'dp')
- ffn_down_second_new: float32 [6400, 2560], P('mp', 'dp')
- ffn_down_new: float32 [6400, 2560], P('mp', 'dp')
All inputs are finite; a program needn't handle non-finite values.
Results may differ from a plain program's by a relative error of at most 0.019.
Values may be sent and summed in bfloat16 or wider, within the bound.
No kernel may reach another device: no remote copies, remote signals or barrier semaphores. Data moves between devices by JAX's collectives and lax.ppermute only.
A program may use at most 320 MiB of HBM per device.

v0:
```python
import functools
import math

import jax
import jax.numpy as jnp
from jax import lax
from jax.experimental import pallas as pl
from jax.experimental.pallas import tpu as pltpu
from jax.sharding import PartitionSpec as P

D = 2560
QR = 768
KVR = 256
HD = 64
RD = 32
LEN = 1024
STEP = 5


NORM_EPS = 1e-05
RESID_SCALE = 1.4 / math.sqrt(62.0)
ROPE_BASE = 10000.0
BETA_ONE = 0.9
BETA_TWO = 0.95
ADAM_EPS = 1e-08
DECAY_RATE = 0.1


def normalize(vector, gain_vec):
    return (
        vector * lax.rsqrt(jnp.mean(vector * vector, axis=-1, keepdims=True) + NORM_EPS) * gain_vec
    )


def norm_back(vector, gain_vec, gradient):
    unused, pull_back = jax.vjp(normalize, vector, gain_vec)
    return pull_back(gradient)


def tables(length):
    positions = jnp.arange(length).astype(jnp.float32)
    frequency = jnp.exp(jnp.arange(RD // 2).astype(jnp.float32) * (-2.0 * math.log(ROPE_BASE) / RD))
    angles = positions[:, None] * frequency[None, :]
    return (jnp.cos(angles), jnp.sin(angles))


def product(left, right):
    return jnp.dot(left, right, preferred_element_type=jnp.float32)


def contract(spec, left, right):
    return jnp.einsum(spec, left, right, preferred_element_type=jnp.float32)


BLK = 256
ROWS = 512
LIGHT = 100000
VMEM_CAP = 56 * 1024 * 1024


def dot_nn(left, right):
    return lax.dot_general(left, right, (((1,), (0,)), ((), ())), preferred_element_type=jnp.float32)


def dot_nt(left, right):
    return lax.dot_general(left, right, (((1,), (1,)), ((), ())), preferred_element_type=jnp.float32)


def dot_tn(left, right):
    return lax.dot_general(left, right, (((0,), (0,)), ((), ())), preferred_element_type=jnp.float32)


def kernel_params():
    return pltpu.CompilerParams(vmem_limit_bytes=VMEM_CAP)


def light(flops):
    return pl.CostEstimate(flops=flops // LIGHT, bytes_accessed=1024, transcendentals=0)


def causal_tile():
    keys = lax.broadcasted_iota(jnp.int32, (BLK, BLK), 0)
    rows = lax.broadcasted_iota(jnp.int32, (BLK, BLK), 1)
    return keys <= rows


def forward_kernel(first, q_ref, k_ref, v_ref, mixed_ref, lse_ref, score_ref):
    scale_val = (HD + RD) ** (-0.5)
    key_rows = k_ref[0].T
    keep = causal_tile()
    for i in range(q_ref.shape[2] // BLK):
        cols = slice(i * BLK, (i + 1) * BLK)
        q_blk = q_ref[0, :, cols]
        last = first + i
        top = None
        for c in range(last + 1):
            part = slice(c * BLK, (c + 1) * BLK)
            scores = scale_val * dot_nn(key_rows[part], q_blk)
            if c == last:
                scores = jnp.where(keep, scores, -1e30)
            score_ref[part, :] = scores
            peak = jnp.max(scores, axis=0, keepdims=True)
            top = peak if top is None else jnp.maximum(top, peak)
        total = jnp.zeros((1, BLK), jnp.float32)
        mixed = jnp.zeros((HD, BLK), jnp.float32)
        for c in range(last + 1):
            part = slice(c * BLK, (c + 1) * BLK)
            weights = jnp.exp(score_ref[part, :] - top)
            total = total + jnp.sum(weights, axis=0, keepdims=True)
            mixed = mixed + dot_nn(v_ref[0, :, part], weights.astype(jnp.bfloat16))
        mixed_ref[0, :, cols] = (mixed / total).astype(jnp.bfloat16)
        lse_ref[0, :, cols] = top + jnp.log(total)


def attend_forward(queries, keys, values, half):
    heads, unused, length = queries.shape
    size = length // 2
    seen = size * (half + 1)
    spec = lambda rows, cols, place: pl.BlockSpec((1, rows, cols), lambda h: (h, 0, place))
    return pl.pallas_call(
        functools.partial(forward_kernel, half * size // BLK),
        grid=(heads,),
        in_specs=[spec(HD + RD, size, half), spec(HD + RD, seen, 0), spec(HD, seen, 0)],
        out_specs=[spec(HD, size, 0), spec(1, size, 0)],
        out_shape=[
            jax.ShapeDtypeStruct((heads, HD, size), jnp.bfloat16),
            jax.ShapeDtypeStruct((heads, 1, size), jnp.float32),
        ],
        scratch_shapes=[pltpu.VMEM((seen, BLK), jnp.float32)],
        compiler_params=kernel_params(),
        cost_estimate=light(heads * size * seen * 1400),
        name="attend_forward",
    )(queries, keys, values)


def backward_kernel(first, seeded, *refs):
    q_ref, k_ref, v_ref, grad_ref, lse_ref, cos_ref, sin_ref = refs[:7]
    refs = refs[7:]
    if seeded:
        dk_seed, dv_seed = refs[:2]
        dq_ref, dkv_ref, rope_ref = refs[2:5]
        refs = refs[5:]
    else:
        dq_ref, dkv_ref, rope_ref, dk_out, dv_out = refs[:5]
        refs = refs[5:]
    prob_ref, gp_ref, dk_ref, dv_ref = refs
    scale_val = (HD + RD) ** (-0.5)
    half = RD // 2
    key_rows = k_ref[0].T
    value_rows = v_ref[0].T
    keep = causal_tile()
    size = q_ref.shape[2]
    if seeded:
        dk_ref[...] = dk_seed[0]
        dv_ref[...] = dv_seed[0]
    final = size // BLK - 1
    for i in range(final, -1, -1):
        cols = slice(i * BLK, (i + 1) * BLK)
        q_blk = q_ref[0, :, cols]
        grad_blk = grad_ref[0, :, cols]
        lse_blk = lse_ref[0, :, cols]
        last = first + i
        delta = jnp.zeros((1, BLK), jnp.float32)
        for c in range(last + 1):
            part = slice(c * BLK, (c + 1) * BLK)
            scores = scale_val * dot_nn(key_rows[part], q_blk)
            if c == last:
                scores = jnp.where(keep, scores, -1e30)
            probs = jnp.exp(scores - lse_blk)
            grad_probs = dot_nn(value_rows[part], grad_blk)
            prob_ref[part, :] = probs
            gp_ref[part, :] = grad_probs
            delta = delta + jnp.sum(probs * grad_probs, axis=0, keepdims=True)
        dq = jnp.zeros((HD + RD, BLK), jnp.float32)
        for c in range(last + 1):
            part = slice(c * BLK, (c + 1) * BLK)
            probs = prob_ref[part, :]
            grad_scores = (probs * (gp_ref[part, :] - delta)).astype(jnp.bfloat16)
            dq = dq + dot_nn(k_ref[0, :, part], grad_scores)
            dk_part = dot_nt(q_blk, grad_scores)
            dv_part = dot_nt(grad_blk, probs.astype(jnp.bfloat16))
            if i == final and not seeded:
                dk_ref[:, part] = dk_part
                dv_ref[:, part] = dv_part
            else:
                dk_ref[:, part] += dk_part
                dv_ref[:, part] += dv_part
        dq = scale_val * dq
        low = dq[HD : HD + half]
        high = dq[HD + half :]
        cos_blk = cos_ref[:, cols]
        sin_blk = sin_ref[:, cols]
        dq_ref[0, :HD, cols] = dq[:HD].astype(jnp.bfloat16)
        dq_ref[0, HD : HD + half, cols] = (low * cos_blk + high * sin_blk).astype(jnp.bfloat16)
        dq_ref[0, HD + half :, cols] = (high * cos_blk - low * sin_blk).astype(jnp.bfloat16)
    own = slice(first * BLK, first * BLK + size)
    dkv_ref[0, :HD, :] = (scale_val * dk_ref[:HD, own]).astype(jnp.bfloat16)
    dkv_ref[0, HD:, :] = dv_ref[:, own].astype(jnp.bfloat16)
    if not seeded:
        dk_out[0] = dk_ref[:, : first * BLK]
        dv_out[0] = dv_ref[:, : first * BLK]

    @pl.when(pl.program_id(0) == 0)
    def _():
        rope_ref[...] = scale_val * dk_ref[HD:, own]

    @pl.when(pl.program_id(0) != 0)
    def _():
        rope_ref[...] += scale_val * dk_ref[HD:, own]


def attend_backward(queries, keys, values, grad_mixed, lse, cosines, sines, half, seeds):
    heads, unused, length = queries.shape
    size = length // 2
    seen = size * (half + 1)
    spec = lambda rows, cols, place: pl.BlockSpec((1, rows, cols), lambda h: (h, 0, place))
    flat = lambda rows, place: pl.BlockSpec((rows, size), lambda h: (0, place))
    in_specs = [
        spec(HD + RD, size, half),
        spec(HD + RD, seen, 0),
        spec(HD, seen, 0),
        spec(HD, size, 0),
        spec(1, size, 0),
        flat(RD // 2, half),
        flat(RD // 2, half),
    ]
    out_specs = [spec(HD + RD, size, 0), spec(2 * HD, size, 0), flat(RD, 0)]
    out_shape = [
        jax.ShapeDtypeStruct((heads, HD + RD, size), jnp.bfloat16),
        jax.ShapeDtypeStruct((heads, 2 * HD, size), jnp.bfloat16),
        jax.ShapeDtypeStruct((RD, size), jnp.float32),
    ]
    pair = [spec(HD + RD, size, 0), spec(HD, size, 0)]
    if half == 0:
        in_specs = in_specs + pair
    else:
        out_specs = out_specs + pair
        out_shape = out_shape + [
            jax.ShapeDtypeStruct((heads, HD + RD, size), jnp.float32),
            jax.ShapeDtypeStruct((heads, HD, size), jnp.float32),
        ]
    return pl.pallas_call(
        functools.partial(backward_kernel, half * size // BLK, half == 0),
        grid=(heads,),
        in_specs=in_specs,
        out_specs=out_specs,
        out_shape=out_shape,
        scratch_shapes=[
            pltpu.VMEM((seen, BLK), jnp.float32),
            pltpu.VMEM((seen, BLK), jnp.float32),
            pltpu.VMEM((HD + RD, seen), jnp.float32),
            pltpu.VMEM((HD, seen), jnp.float32),
        ],
        compiler_params=kernel_params(),
        cost_estimate=light(heads * size * seen * 3000),
        name="attend_backward",
    )(queries, keys, values, grad_mixed, lse, cosines, sines, *seeds)


def hidden_kernel(grad_ref, weight_ref, out_ref):
    weight = weight_ref[...].reshape(-1, weight_ref.shape[3])

    @pl.when(pl.program_id(1) == 0)
    def _():
        out_ref[...] = dot_nn(grad_ref[...], weight)

    @pl.when(pl.program_id(1) != 0)
    def _():
        out_ref[...] += dot_nn(grad_ref[...], weight)


def hidden_back(grad_out, weights):
    tokens, model = grad_out.shape
    blocks, unused, rows, units = weights.shape
    return pl.pallas_call(
        hidden_kernel,
        grid=(tokens // ROWS, 2),
        in_specs=[
            pl.BlockSpec((ROWS, model // 2), lambda i, k: (i, k)),
            pl.BlockSpec((blocks // 2, 1, rows, units), lambda i, k: (k, 2, 0, 0)),
        ],
        out_specs=pl.BlockSpec((ROWS, units), lambda i, k: (i, 0)),
        out_shape=jax.ShapeDtypeStruct((tokens, units), jnp.float32),
        compiler_params=kernel_params(),
        cost_estimate=light(2 * tokens * model * units),
        name="hidden_back",
    )(grad_out, weights)


def inner_kernel(normed_ref, grad_ref, weight_ref, hidden_ref, gate_ref, up_ref, sum_ref):
    which = pl.program_id(1)
    step = pl.program_id(2)
    weight = weight_ref[...].reshape(-1, weight_ref.shape[3])

    @pl.when(step == 0)
    def _():
        sum_ref[which] = dot_nn(normed_ref[...], weight)

    @pl.when(step != 0)
    def _():
        sum_ref[which] += dot_nn(normed_ref[...], weight)

    @pl.when((which == 1) & (step == pl.num_programs(2) - 1))
    def _():
        gate_val = sum_ref[0]
        up_val = sum_ref[1]
        grad_hidden = grad_ref[...]
        sigmoid_gate = jax.nn.sigmoid(gate_val)
        silu_gate = gate_val * sigmoid_gate
        hidden_ref[...] = (silu_gate * up_val).astype(jnp.bfloat16)
        gate_ref[...] = (
            grad_hidden * up_val * sigmoid_gate * (1.0 + gate_val * (1.0 - sigmoid_gate))
        ).astype(jnp.bfloat16)
        up_ref[...] = (grad_hidden * silu_gate).astype(jnp.bfloat16)


def ffn_inner(normed, grad_hidden, weights, place):
    tokens, model = normed.shape
    blocks, unused, rows, units = weights.shape
    steps = tokens // ROWS
    out = jax.ShapeDtypeStruct((tokens, units), jnp.bfloat16)
    result = pl.BlockSpec((ROWS, units), lambda i, w, k: (i, 0))
    return pl.pallas_call(
        inner_kernel,
        grid=(steps, 2, 2),
        in_specs=[
            pl.BlockSpec((ROWS, model // 2), lambda i, w, k: (i, k)),
            pl.BlockSpec((ROWS, units), lambda i, w, k: (i + place * steps, 0)),
            pl.BlockSpec((blocks // 2, 1, rows, units), lambda i, w, k: (k, w, 0, 0)),
        ],
        out_specs=[result, result, result],
        out_shape=[out, out, out],
        scratch_shapes=[pltpu.VMEM((2, ROWS, units), jnp.float32)],
        compiler_params=kernel_params(),
        cost_estimate=light(4 * tokens * model * units),
        name="ffn_inner",
    )(normed, grad_hidden, weights)


def back_kernel(count, *refs):
    lefts = refs[:count]
    weight_ref = refs[count]
    out_ref = refs[count + 1]
    units = weight_ref.shape[3]
    total = None
    for number in range(count):
        term = dot_nt(lefts[number][...], weight_ref[:, number].reshape(-1, units))
        total = term if total is None else total + term
    out_ref[...] = total.astype(jnp.bfloat16)


def ffn_back(lefts, weights, first):
    tokens, units = lefts[0].shape
    blocks, unused, rows, unused_units = weights.shape
    count = len(lefts)
    model = blocks * rows
    return pl.pallas_call(
        functools.partial(back_kernel, count),
        grid=(2, tokens // ROWS),
        in_specs=[pl.BlockSpec((ROWS, units), lambda k, i: (i, 0)) for unused_left in lefts]
        + [pl.BlockSpec((blocks // 2, count, rows, units), lambda k, i: (k, first, 0, 0))],
        out_specs=pl.BlockSpec((ROWS, model // 2), lambda k, i: (i, k)),
        out_shape=jax.ShapeDtypeStruct((tokens, model), jnp.bfloat16),
        compiler_params=kernel_params(),
        cost_estimate=light(4 * count * tokens * model * units),
        name="ffn_back",
    )(*lefts, weights)


def outer_kernel(count, *refs):
    out_ref = refs[-1]
    total = dot_tn(refs[0][...], refs[count][...])
    for number in range(1, count):
        total = total + dot_tn(refs[number][...], refs[count + number][...])
    out_ref[...] = total.astype(jnp.bfloat16).reshape(out_ref.shape)


def ffn_outer(lefts, places, rights, blocks, slot, held):
    tokens, units = rights[0].shape
    model = lefts[0].shape[1]
    rows = model // blocks
    extra = [] if held is None else [held]
    count = len(lefts)
    left_spec = lambda place: pl.BlockSpec((tokens, model // 2), lambda k: (place, k))
    return pl.pallas_call(
        functools.partial(outer_kernel, count),
        grid=(2,),
        in_specs=[left_spec(place) for place in places]
        + [pl.BlockSpec((tokens, units), lambda k: (0, 0)) for unused in rights]
        + [pl.BlockSpec(memory_space=pl.ANY) for unused in extra],
        out_specs=pl.BlockSpec((blocks // 2, 1, rows, units), lambda k: (k, slot, 0, 0)),
        out_shape=jax.ShapeDtypeStruct((blocks, 3, rows, units), jnp.bfloat16),
        input_output_aliases={} if held is None else {2 * count: 0},
        compiler_params=kernel_params(),
        cost_estimate=light(4 * count * tokens * model * units),
        name="ffn_outer",
    )(*lefts, *rights, *extra)


def down_kernel(normed_ref, grad_ref, weight_ref, gain_ref, out_ref, part_ref):
    total = dot_tn(normed_ref[...], grad_ref[...])
    out_ref[...] = total.astype(jnp.bfloat16)
    summed = jnp.sum(total * weight_ref[...].astype(jnp.float32), axis=1, keepdims=True)
    part_ref[...] = summed / gain_ref[...]


def down_outer(normed, grads, weights, gains):
    tokens, model = normed.shape
    width = grads.shape[1]
    block = model // 4
    row_spec = lambda cols: pl.BlockSpec((block, cols), lambda k: (k, 0))
    return pl.pallas_call(
        down_kernel,
        grid=(4,),
        in_specs=[
            pl.BlockSpec((tokens, block), lambda k: (0, k)),
            pl.BlockSpec((tokens, width), lambda k: (0, 0)),
            row_spec(width),
            row_spec(1),
        ],
        out_specs=[row_spec(width), row_spec(1)],
        out_shape=[
            jax.ShapeDtypeStruct((model, width), jnp.bfloat16),
            jax.ShapeDtypeStruct((model, 1), jnp.float32),
        ],
        compiler_params=kernel_params(),
        cost_estimate=light(4 * tokens * model * width),
        name="down_outer",
    )(normed, grads, weights, gains)


def input_kernel(grad_ref, weight_ref, inputs_ref, cot_ref, mid_ref, gain_ref, out_ref):
    value = inputs_ref[...].astype(jnp.float32)
    scaled = dot_nt(grad_ref[...], weight_ref[...]) * gain_ref[...]
    rate = lax.rsqrt(jnp.mean(value * value, axis=1, keepdims=True) + NORM_EPS)
    dotted = jnp.mean(scaled * value, axis=1, keepdims=True)
    residual = cot_ref[...].astype(jnp.float32) + mid_ref[...].astype(jnp.float32)
    out_ref[...] = residual + rate * (scaled - value * (rate * rate * dotted))


def input_back(grads, weights, inputs, cotangent, mid_norm, gains):
    tokens, width = grads.shape
    model = inputs.shape[1]
    row_spec = lambda cols: pl.BlockSpec((BLK, cols), lambda i: (i, 0))
    return pl.pallas_call(
        input_kernel,
        grid=(tokens // BLK,),
        in_specs=[
            row_spec(width),
            pl.BlockSpec((model, width), lambda i: (0, 0)),
            row_spec(model),
            row_spec(model),
            row_spec(model),
            pl.BlockSpec((1, model), lambda i: (0, 0)),
        ],
        out_specs=row_spec(model),
        out_shape=jax.ShapeDtypeStruct((tokens, model), jnp.float32),
        compiler_params=kernel_params(),
        cost_estimate=light(4 * tokens * model * width),
        name="input_back",
    )(grads, weights, inputs, cotangent, mid_norm, gains)


def latent_kernel(count, *refs):
    out_ref = refs[-1]
    query_up, latent_up = refs[3 * count], refs[3 * count + 1]
    size = refs[0].shape[1]
    for number in range(count):
        grad_q, grad_kv, rope = refs[number], refs[count + number], refs[2 * count + number]
        rows = slice(number * size, (number + 1) * size)
        out_ref[rows, :QR] = dot_nt(grad_q[...].T, query_up[...]).astype(jnp.bfloat16)
        out_ref[rows, QR : QR + KVR] = dot_nt(grad_kv[...].T, latent_up[...]).astype(jnp.bfloat16)
        out_ref[rows, QR + KVR :] = rope[...].T.astype(jnp.bfloat16)


def latent_back(grads_q, grads_kv, ropes, query_up, latent_up):
    count = len(grads_q)
    tokens = count * grads_q[0].shape[1]
    return pl.pallas_call(
        functools.partial(latent_kernel, count),
        out_shape=jax.ShapeDtypeStruct((tokens, QR + KVR + RD), jnp.bfloat16),
        compiler_params=kernel_params(),
        cost_estimate=light(tokens * (QR + KVR) * 4000),
        name="latent_back",
    )(*grads_q, *grads_kv, *ropes, query_up, latent_up)


def heads_kernel(count, *refs):
    out_ref = refs[-1]
    q_normed, kv_normed = refs[4 * count], refs[4 * count + 1]
    blocks = out_ref.shape[0]
    size = refs[0].shape[0]
    outer = query_outer = latent_outer = None
    for number in range(count):
        grad_attn, mixed = refs[number], refs[count + number]
        grad_q, grad_kv = refs[2 * count + number], refs[3 * count + number]
        rows = slice(number * size, (number + 1) * size)
        terms = (
            dot_nt(grad_attn[...].T, mixed[...]),
            dot_nt(q_normed[rows].T, grad_q[...]),
            dot_nt(kv_normed[rows].T, grad_kv[...]),
        )
        outer = terms[0] if outer is None else outer + terms[0]
        query_outer = terms[1] if query_outer is None else query_outer + terms[1]
        latent_outer = terms[2] if latent_outer is None else latent_outer + terms[2]
    side = outer.shape[1]
    low = outer.astype(jnp.bfloat16).reshape(blocks, -1, side)
    spread = low.shape[1] // 2
    out_ref[:, :spread, :side] = low[:, :spread]
    out_ref[:, :spread, side:] = low[:, spread:]
    query_rows = query_outer.shape[0] // blocks
    columns = query_outer.shape[1]
    middle = slice(spread, spread + query_rows)
    out_ref[:, middle, :columns] = query_outer.astype(jnp.bfloat16).reshape(blocks, query_rows, columns)
    out_ref[:, middle, columns:] = jnp.zeros(
        (blocks, query_rows, out_ref.shape[2] - columns), jnp.bfloat16
    )
    out_ref[:, spread + query_rows :] = latent_outer.astype(jnp.bfloat16).reshape(
        blocks, -1, out_ref.shape[2]
    )


def heads_outer(grads_attn, mixed, grads_q, grads_kv, q_normed, kv_normed, blocks):
    count = len(mixed)
    size = grads_attn[0].shape[0]
    wide_cols = grads_kv[0].shape[0]
    rows = D // blocks // 2 + QR // blocks + KVR // blocks
    whole = lambda value: pl.BlockSpec(value.shape, lambda k: (0, 0))
    return pl.pallas_call(
        functools.partial(heads_kernel, count),
        grid=(2,),
        in_specs=[pl.BlockSpec((size, D // 2), lambda k: (0, k)) for unused in grads_attn]
        + [whole(value) for value in (*mixed, *grads_q, *grads_kv)]
        + [
            pl.BlockSpec((q_normed.shape[0], QR // 2), lambda k: (0, k)),
            pl.BlockSpec((kv_normed.shape[0], KVR // 2), lambda k: (0, k)),
        ],
        out_specs=pl.BlockSpec((blocks // 2, rows, wide_cols), lambda k: (k, 0, 0)),
        out_shape=jax.ShapeDtypeStruct((blocks, rows, wide_cols), jnp.bfloat16),
        compiler_params=kernel_params(),
        cost_estimate=light(count * size * D * wide_cols * 2),
        name="heads_outer",
    )(*grads_attn, *mixed, *grads_q, *grads_kv, q_normed, kv_normed)


def update_rates():
    return [
        (0.25, 0.0),
        (2.5 / math.sqrt(D), DECAY_RATE),
        (2.5 / math.sqrt(D), DECAY_RATE),
        (2.5 / math.sqrt(QR), DECAY_RATE),
        (2.5 / math.sqrt(KVR), DECAY_RATE),
        (1.75, DECAY_RATE),
        (2.5 / math.sqrt(D), DECAY_RATE),
        (2.5 / math.sqrt(D), DECAY_RATE),
        (0.375, DECAY_RATE),
    ]


def adam_step(weight, gradient, first, second, rate_pair):
    first_new = BETA_ONE * first + (1.0 - BETA_ONE) * gradient
    second_new = BETA_TWO * second + (1.0 - BETA_TWO) * gradient * gradient
    first_hat = first_new / (1.0 - BETA_ONE**STEP)
    second_hat = second_new / (1.0 - BETA_TWO**STEP)
    weight_new = weight - rate_pair[0] * (
        first_hat / (jnp.sqrt(second_hat) + ADAM_EPS) + rate_pair[1] * weight
    )
    return (first_new, second_new, weight_new)


def wide(value):
    return value.astype(jnp.float32)


def tie(*values):
    return lax.optimization_barrier(values)


def after(value, *others):
    return lax.optimization_barrier((value, *others))[0]


def chunk_of(stacked, place):
    return lax.dynamic_index_in_dim(stacked, place, axis=0, keepdims=False)


class Gather:
    def __init__(self, own, count, axis):
        self.own, self.count, self.axis = own, count, axis
        self.below, self.above = [own], [own]

    def advance(self, gate):
        step = len(self.below)
        if step == self.count:
            return []
        up, down = gate(self.below[-1], self.above[-1])
        ups = [(k, k + 1) for k in range(step - 1, self.count - 1)]
        downs = [(k + 1, k) for k in range(self.count - step)]
        self.below.append(lax.ppermute(up, "mp", ups))
        self.above.append(lax.ppermute(down, "mp", downs))
        return [self.below[-1], self.above[-1]]

    def result(self):
        while self.advance(tie):
            pass
        place = lax.axis_index("mp")
        blocks = []
        for slot in range(self.count):
            block = self.own
            for step in range(1, self.count):
                if slot + step < self.count:
                    block = jnp.where(place - step == slot, self.below[step], block)
                if slot - step >= 0:
                    block = jnp.where(place + step == slot, self.above[step], block)
            blocks.append(block)
        return jnp.concatenate(blocks, axis=self.axis)


class Scatter:
    def __init__(self, partial, count):
        self.stacked = partial.reshape(count, partial.shape[0] // count, partial.shape[1])
        self.count, self.step = count, 0
        self.below = self.above = None

    def advance(self, gate):
        count = self.count
        if self.step == count - 1:
            return []
        self.step = step = self.step + 1
        place = lax.axis_index("mp")
        up = chunk_of(self.stacked, jnp.clip(count - step + place, 0, count - 1))
        down = chunk_of(self.stacked, jnp.clip(step - count + place, 0, count - 1))
        if step > 1:
            up = (wide(up) + wide(self.below)).astype(up.dtype)
            down = (wide(down) + wide(self.above)).astype(down.dtype)
        up, down = gate(up, down)
        self.below = lax.ppermute(up, "mp", [(k, k + 1) for k in range(step)])
        downs = [(count - 1 - k, count - 2 - k) for k in range(step)]
        self.above = lax.ppermute(down, "mp", downs)
        return [self.below, self.above]

    def result(self):
        while self.advance(tie):
            pass
        own = chunk_of(self.stacked, lax.axis_index("mp"))
        return wide(own) + wide(self.below) + wide(self.above)


class Plane:
    def __init__(self, block, count):
        rows = block.shape[0] // 2
        bits = [1 << k for k in range(1, count.bit_length() - 1)]
        self.count, self.step = count, 0
        self.orders = [bits + [1], bits[::-1] + [1]]
        self.held = [block[None, :rows], block[None, rows:]]

    def advance(self, gate):
        if self.step == len(self.orders[0]):
            return []
        held = gate(*self.held)
        came = []
        for part, order in zip(held, self.orders):
            pairs = [(k, k ^ order[self.step]) for k in range(self.count)]
            came.append(lax.ppermute(part, "dp", pairs))
        self.held = [jnp.concatenate([part, other], axis=0) for part, other in zip(self.held, came)]
        self.step += 1
        return came

    def result(self):
        while self.advance(tie):
            pass
        place = lax.axis_index("dp")
        blocks = []
        for number in range(self.count):
            apart = jnp.bitwise_xor(place, number)
            for part, order in zip(self.held, self.orders):
                spot = sum(
                    jnp.where(jnp.bitwise_and(apart, bit) != 0, 1 << step, 0)
                    for step, bit in enumerate(order)
                )
                blocks.append(chunk_of(part, spot))
        return jnp.concatenate(blocks, axis=0)


class Clock:
    def __init__(self):
        self.past, self.present = (), []

    def gate(self, *values):
        return lax.optimization_barrier((*values, *self.past))[: len(values)]

    def wait(self, value):
        return self.gate(value)[0]

    def move(self, *flows):
        for flow in flows:
            self.present += flow.advance(self.gate)

    def tick(self, *values):
        if self.present or values:
            self.past = (*self.present, *values)
            self.present = []


def sum_rows(stacked):
    flat = stacked.reshape(-1, stacked.shape[-1])
    return wide(lax.psum_scatter(flat, "dp", scatter_dimension=0, tiled=True))


def turn(low, high, cosines, sines, direction):
    return (low * cosines - direction * high * sines, high * cosines + direction * low * sines)


def local(
    inputs,
    cotangent,
    norm_gains,
    norm_gains_first,
    norm_gains_second,
    query_down,
    query_down_first,
    query_down_second,
    latent_down,
    latent_down_first,
    latent_down_second,
    query_up,
    query_up_first,
    query_up_second,
    latent_up,
    latent_up_first,
    latent_up_second,
    out_proj,
    out_proj_first,
    out_proj_second,
    ffn_gate,
    ffn_gate_first,
    ffn_gate_second,
    ffn_up,
    ffn_up_first,
    ffn_up_second,
    ffn_down,
    ffn_down_first,
    ffn_down_second,
):
    low_type = jnp.bfloat16
    tokens_dev = inputs.shape[0]
    n_data = lax.axis_size("dp")
    n_model = lax.axis_size("mp")
    place = lax.axis_index("mp")
    heads_dev = query_up.shape[1] // (HD + RD)
    half_tokens = tokens_dev // 2
    own_tokens = half_tokens // n_model
    hidden_dev = ffn_gate.shape[1]
    out_width = heads_dev * HD
    down_rows = query_down.shape[0]
    width = QR + KVR + RD
    gain_rows = 16
    order = (1, 0)

    def own_rows(value):
        return lax.dynamic_slice_in_dim(value, place * own_tokens, own_tokens, 0)

    def half_of(value, half):
        return value[half * half_tokens : (half + 1) * half_tokens]

    up_rows = query_up.shape[0]
    kv_rows = latent_up.shape[0]
    up_width = latent_up.shape[1]
    gains_high = lax.reduce_precision(norm_gains, 8, 7)
    up_pack = jnp.concatenate(
        [
            jnp.pad(query_up.astype(low_type), ((0, 0), (0, up_width - query_up.shape[1]))),
            latent_up.astype(low_type),
            jnp.pad(
                jnp.stack([gains_high, norm_gains - gains_high]).astype(low_type),
                ((0, gain_rows - 2), (0, up_width - norm_gains.shape[0])),
            ),
        ],
        axis=0,
    )
    down_own = jnp.concatenate([query_down, latent_down], axis=1).astype(low_type)
    up_flow = Plane(up_pack, n_data)
    down_flow = Gather(down_own, n_model, 0)
    out_flow = Gather(out_proj.T.astype(low_type), n_model, 1)
    clock = Clock()
    for unused in range(3):
        clock.move(down_flow)
        clock.tick()
    down_flow = Plane(down_flow.result(), n_data)
    for unused in range(3):
        clock.move(down_flow, up_flow, out_flow)
        clock.tick()
    up_all = up_flow.result().reshape(n_data, -1, up_width)
    down_all = down_flow.result()
    out_all = lax.all_gather(out_flow.result(), "dp", axis=0, tiled=True)
    out_own = lax.dynamic_slice_in_dim(out_all, place * out_width, out_width, 1)
    ffn_pack = jnp.stack([ffn_gate, ffn_up, ffn_down.T]).astype(low_type)
    ffn_all = lax.all_gather(ffn_pack, "dp", axis=0, tiled=False)
    query_up_all = up_all[:, :up_rows, : query_up.shape[1]].reshape(QR, query_up.shape[1])
    latent_up_all = up_all[:, up_rows : up_rows + kv_rows].reshape(KVR, up_width)
    gains_sent = wide(up_all[:, up_rows + kv_rows : up_rows + kv_rows + 2, : norm_gains.shape[0]])
    gains_all = (gains_sent[:, 0] + gains_sent[:, 1]).reshape(-1)
    gain_in = gains_all[:D]
    gain_query = gains_all[D : D + QR]
    gain_latent = gains_all[D + QR : D + QR + KVR]
    gain_mid = gains_all[D + QR + KVR :]
    cosines, sines = tables(LEN)
    cos_tok = cosines
    sin_tok = sines
    cosines = cosines.T
    sines = sines.T

    inputs_wide = wide(inputs)
    cot_wide = wide(cotangent)
    normed_in = normalize(inputs_wide, gain_in).astype(low_type)
    latents = product(normed_in, down_all)
    q_latent = latents[:, :QR]
    kv_latent = latents[:, QR : QR + KVR]
    q_normed = normalize(q_latent, gain_query).astype(low_type)
    kv_normed = normalize(kv_latent, gain_latent).astype(low_type)
    q_heads = contract("rc,tr->ct", query_up_all, q_normed).reshape(heads_dev, HD + RD, tokens_dev)
    turned = turn(q_heads[:, HD : HD + RD // 2], q_heads[:, HD + RD // 2 :], cosines, sines, 1.0)
    queries = jnp.concatenate([q_heads[:, :HD], turned[0], turned[1]], axis=1).astype(low_type)
    kv_heads = contract("rc,tr->ct", latent_up_all, kv_normed).astype(low_type)
    kv_heads = kv_heads.reshape(heads_dev, 2 * HD, tokens_dev)
    rope_in = latents[:, QR + KVR :].T
    turned = turn(rope_in[: RD // 2], rope_in[RD // 2 :], cosines, sines, 1.0)
    key_rope = jnp.concatenate(turned, axis=0).astype(low_type)
    keys = jnp.concatenate(
        [kv_heads[:, :HD], jnp.broadcast_to(key_rope[None], (heads_dev, RD, tokens_dev))], axis=1
    )
    values = kv_heads[:, HD:]
    mixed = {}
    log_sums = {}
    resid_mid = {}
    normed_mid = {}
    grad_ffn = (RESID_SCALE * cot_wide).astype(low_type)
    mixed_flow = {}
    for half in order:
        asked = queries if half == 1 else clock.wait(queries)
        mixed[half], log_sums[half] = attend_forward(asked, keys, values, half)
        mixed[half] = mixed[half].reshape(out_width, half_tokens)
        mixed_flow[half] = Gather(mixed[half], n_model, 0)
        clock.tick(mixed[half])
        clock.move(mixed_flow[1])
    clock.move(mixed_flow[0])
    clock.tick()
    clock.move(mixed_flow[1], mixed_flow[0])
    grad_hidden = hidden_back(clock.wait(grad_ffn), ffn_all)
    clock.tick(grad_hidden)
    clock.move(mixed_flow[0])

    def middle(half):
        mixed_all = clock.wait(mixed_flow[half].result())
        attn_out = contract("ht,dh->td", mixed_all, out_all)
        resid_mid[half] = half_of(inputs_wide, half) + RESID_SCALE * attn_out
        normed_mid[half] = normalize(resid_mid[half], gain_mid).astype(low_type)
        clock.tick(normed_mid[half])

    hidden = {}
    grad_gate = {}
    grad_up = {}
    part_mid = {}
    mid_own = {}
    for half in order:
        middle(half)
        hidden[half], grad_gate[half], grad_up[half] = ffn_inner(
            clock.wait(normed_mid[half]), grad_hidden, ffn_all, half
        )
        clock.tick(grad_up[half])
        part_mid[half] = ffn_back([clock.wait(grad_gate[half]), grad_up[half]], ffn_all, 0)
        clock.tick(part_mid[half])
        sent_mid = part_mid[half] if half == 1 else after(part_mid[half], mid_own[1])
        mid_own[half] = wide(lax.psum_scatter(sent_mid, "mp", scatter_dimension=0, tiled=True))
    pairs = lambda values: [values[half] for half in order]
    both = lambda values: [values[half] for half in (0, 1)]
    mid_norm = {}
    mid_flow = {}
    gain_mid_part = {}
    grad_attn = {}
    grad_mixed = {}

    def mid_back(half):
        own, gain_mid_part[half] = norm_back(own_rows(resid_mid[half]), gain_mid, mid_own[half])
        mid_flow[half] = Gather(own.astype(low_type), n_model, 0)

    def mixed_back(half):
        mid_norm[half] = clock.wait(mid_flow[half].result())
        grad_mid = half_of(cot_wide, half) + wide(mid_norm[half])
        grad_attn[half] = (RESID_SCALE * grad_mid).astype(low_type)
        grad_mixed[half] = contract("td,dh->ht", grad_attn[half], out_own).astype(low_type)

    mid_back(1)
    clock.move(mid_flow[1])
    grad_gate[1] = clock.wait(grad_gate[1])
    ffn_grads = ffn_outer(pairs(normed_mid), (0, 0), pairs(grad_gate), n_data, 0, None)
    clock.tick(ffn_grads[0, 0, :16, :128])
    clock.move(mid_flow[1])
    grad_up[1] = clock.wait(grad_up[1])
    ffn_grads = ffn_outer(pairs(normed_mid), (0, 0), pairs(grad_up), n_data, 1, ffn_grads)
    clock.tick(ffn_grads[0, 1, :16, :128])
    clock.move(mid_flow[1])
    hidden_late = clock.wait(hidden[1])
    ffn_grads = ffn_outer([grad_ffn, grad_ffn], order, [hidden_late, hidden[0]], n_data, 2, ffn_grads)
    clock.tick(ffn_grads[0, 2, :16, :128])
    mid_own[0] = clock.wait(mid_own[0])
    ffn_grads = after(ffn_grads, mid_own[0])
    ffn_sum = sum_rows(ffn_grads).reshape(3, -1, hidden_dev)
    mid_back(0)
    clock.move(mid_flow[0])
    ffn_term = [ffn_back([clock.wait(hidden[half])], ffn_all, 2) for half in (0, 1)]
    ffn_term = jnp.concatenate(ffn_term, axis=0)
    clock.tick(ffn_term)
    resid_all = jnp.concatenate([resid_mid[0], resid_mid[1]], axis=0)

    seeds = ()
    grad_q_heads = {}
    grad_kv_heads = {}
    grad_rope = {}

    def heads_back(half):
        back = attend_backward(
            queries,
            keys,
            values,
            grad_mixed[half].reshape(heads_dev, HD, half_tokens),
            log_sums[half],
            cosines,
            sines,
            half,
            seeds,
        )
        grad_q_heads[half] = back[0].reshape(heads_dev * (HD + RD), half_tokens)
        grad_kv_heads[half] = back[1].reshape(heads_dev * 2 * HD, half_tokens)
        grad_rope[half] = back[2]
        return back[3:]

    out_flow = Scatter(ffn_term, n_model)
    clock.move(mid_flow[0], out_flow)
    mixed_back(1)
    seeds = heads_back(1)
    clock.tick(grad_rope[1])
    clock.move(mid_flow[0])
    clock.tick()
    clock.move(out_flow)
    mixed_back(0)
    seeds = heads_back(0)
    part_latents = latent_back(
        both(grad_q_heads), both(grad_kv_heads), both(grad_rope), query_up_all, latent_up_all
    )
    clock.tick(part_latents)
    lat_flow = Scatter(part_latents, n_model)
    clock.move(lat_flow, out_flow)
    head_grads = heads_outer(
        both(grad_attn),
        both(mixed),
        both(grad_q_heads),
        both(grad_kv_heads),
        clock.wait(q_normed),
        kv_normed,
        n_data,
    )
    clock.tick(head_grads[0, :16, :128])
    clock.move(lat_flow)
    clock.tick()
    clock.move(lat_flow)
    rows = lat_flow.result()
    ffn_own = out_flow.result()
    clock.tick()

    spread = 2 * own_tokens

    def wide_rows(value):
        return lax.dynamic_slice_in_dim(value, place * spread, spread, 0)

    grad_q_own, gain_query_part = norm_back(wide_rows(q_latent), gain_query, rows[:, :QR])
    grad_kv_own, gain_latent_part = norm_back(
        wide_rows(kv_latent), gain_latent, rows[:, QR : QR + KVR]
    )
    turned = turn(
        rows[:, QR + KVR : QR + KVR + RD // 2],
        rows[:, QR + KVR + RD // 2 :],
        wide_rows(cos_tok),
        wide_rows(sin_tok),
        -1.0,
    )
    gain_parts = jnp.concatenate(
        [gain_query_part, gain_latent_part, gain_mid_part[0] + gain_mid_part[1]]
    )
    gain_parts = jnp.pad(gain_parts, (0, gain_rows * width - gain_parts.shape[0]))
    sent_own = jnp.concatenate(
        [
            jnp.concatenate([grad_q_own, grad_kv_own, turned[0], turned[1]], axis=1),
            gain_parts.reshape(gain_rows, width),
        ],
        axis=0,
    ).astype(low_type)
    sent_flow = Gather(sent_own, n_model, 0)
    clock.move(sent_flow)
    clock.tick()
    clock.move(sent_flow)
    clock.tick()
    output_own = (wide_rows(resid_all) + RESID_SCALE * ffn_own).astype(low_type)
    output_flow = Gather(output_own, n_model, 0)
    clock.move(sent_flow, output_flow)
    sent = sent_flow.result().reshape(n_model, spread + gain_rows, width)
    head_grads, ffn_sum = tie(head_grads, ffn_sum)
    head_sum = sum_rows(head_grads)
    out_rows = D // n_data // 2
    clock.tick()
    clock.move(output_flow)
    grad_latents = sent[:, :spread].reshape(tokens_dev, width)
    gain_rest = jnp.sum(wide(sent[:, spread:]), axis=0).reshape(-1)[: QR + KVR + D]

    grad_down, gain_in_part = down_outer(clock.wait(normed_in), grad_latents, down_all, gain_in[:, None])
    gain_grad = jnp.concatenate([gain_in_part[:, 0], gain_rest]).reshape(n_data, 1, -1)
    gain_count = gain_grad.shape[2]
    gain_grad = jnp.pad(gain_grad, ((0, 0), (0, gain_rows - 1), (0, width - gain_count)))
    down_mine = lax.dynamic_index_in_dim(
        grad_down.reshape(n_data, n_model, down_rows, width), place, axis=1, keepdims=False
    )
    down_sent = jnp.concatenate([down_mine, gain_grad.astype(low_type)], axis=1)
    down_sent, head_sum = tie(down_sent, head_sum)
    down_sum = sum_rows(down_sent)
    clock.tick(grad_down)
    clock.move(output_flow)
    output = output_flow.result()
    input_grad = input_back(
        clock.wait(grad_latents),
        down_all,
        inputs,
        cotangent,
        jnp.concatenate([mid_norm[0], mid_norm[1]], axis=0),
        gain_in[None],
    )
    reduced = (
        down_sum[down_rows, :gain_count],
        down_sum[:down_rows, :QR],
        down_sum[:down_rows, QR:],
        head_sum[out_rows : out_rows + up_rows, : query_up.shape[1]],
        head_sum[out_rows + up_rows :],
        jnp.concatenate([head_sum[:out_rows, :out_width], head_sum[:out_rows, out_width:]], axis=0).T,
        ffn_sum[0],
        ffn_sum[1],
        ffn_sum[2].T,
    )
    weights = (
        norm_gains,
        query_down,
        latent_down,
        query_up,
        latent_up,
        out_proj,
        ffn_gate,
        ffn_up,
        ffn_down,
    )
    firsts = (
        norm_gains_first,
        query_down_first,
        latent_down_first,
        query_up_first,
        latent_up_first,
        out_proj_first,
        ffn_gate_first,
        ffn_up_first,
        ffn_down_first,
    )
    seconds = (
        norm_gains_second,
        query_down_second,
        latent_down_second,
        query_up_second,
        latent_up_second,
        out_proj_second,
        ffn_gate_second,
        ffn_up_second,
        ffn_down_second,
    )
    rates = update_rates()
    updated = [
        adam_step(weights[number], reduced[number], firsts[number], seconds[number], rates[number])
        for number in range(9)
    ]
    return (
        output,
        input_grad,
        updated[0][0],
        updated[0][1],
        updated[0][2],
        updated[1][0],
        updated[1][1],
        updated[1][2],
        updated[2][0],
        updated[2][1],
        updated[2][2],
        updated[3][0],
        updated[3][1],
        updated[3][2],
        updated[4][0],
        updated[4][1],
        updated[4][2],
        updated[5][0],
        updated[5][1],
        updated[5][2],
        updated[6][0],
        updated[6][1],
        updated[6][2],
        updated[7][0],
        updated[7][1],
        updated[7][2],
        updated[8][0],
        updated[8][1],
        updated[8][2],
    )


def solution(mesh):
    placed = (
        P("dp", None),
        P("dp", None),
        P("dp"),
        P("dp"),
        P("dp"),
        P(("dp", "mp"), None),
        P(("dp", "mp"), None),
        P(("dp", "mp"), None),
        P(("dp", "mp"), None),
        P(("dp", "mp"), None),
        P(("dp", "mp"), None),
        P("dp", "mp"),
        P("dp", "mp"),
        P("dp", "mp"),
        P("dp", "mp"),
        P("dp", "mp"),
        P("dp", "mp"),
        P("mp", "dp"),
        P("mp", "dp"),
        P("mp", "dp"),
        P("dp", "mp"),
        P("dp", "mp"),
        P("dp", "mp"),
        P("dp", "mp"),
        P("dp", "mp"),
        P("dp", "mp"),
        P("mp", "dp"),
        P("mp", "dp"),
        P("mp", "dp"),
    )
    return jax.shard_map(
        local,
        mesh=mesh,
        in_specs=placed,
        out_specs=(
            P("dp", None),
            P("dp", None),
            P("dp"),
            P("dp"),
            P("dp"),
            P(("dp", "mp"), None),
            P(("dp", "mp"), None),
            P(("dp", "mp"), None),
            P(("dp", "mp"), None),
            P(("dp", "mp"), None),
            P(("dp", "mp"), None),
            P("dp", "mp"),
            P("dp", "mp"),
            P("dp", "mp"),
            P("dp", "mp"),
            P("dp", "mp"),
            P("dp", "mp"),
            P("mp", "dp"),
            P("mp", "dp"),
            P("mp", "dp"),
            P("dp", "mp"),
            P("dp", "mp"),
            P("dp", "mp"),
            P("dp", "mp"),
            P("dp", "mp"),
            P("dp", "mp"),
            P("mp", "dp"),
            P("mp", "dp"),
            P("mp", "dp"),
        ),
        check_vma=False,
    )
```

profile of v0, /device:TPU:0, one launch (start us, length us, event | category | flops | bytes accessed | tf_op | source)
XLA Modules:
  0.0 950.9 jit_solution(6407267579390673732)
XLA Ops:
  14.4 4.9 collective-permute-start
  23.2 4.1 collective-permute-done.1
  29.4 8.5 collective-permute-done.3
  40.0 6.0 collective-permute-done.5
  51.8 5.6 collective-permute-done.7
  58.7 15.0 %collective-permute-done.6 = bf16[1,72,1280]{2,1,0:T(8,128)(2,1)S(1)} collective-permute-done((bf16[1,72,1280]{2,1,0:T(8,128)(2,1)S(1)}, bf16[1,72,1280]{2,1,0:T(8,128)(2,1)S(1)}, u32[]{:S(2)}, u32[]{:S(2)}) %collective-permute-start.6) | collective-permute-done | bytes 184352 | tf_op jit(solution)/shard_map/ppermute | solution.py:664
  79.6 5.9 collective-permute-done.12
  86.9 25.6 %collective-permute-done.13 = bf16[2,72,1280]{2,1,0:T(8,128)(2,1)S(1)} collective-permute-done((bf16[2,72,1280]{2,1,0:T(8,128)(2,1)S(1)}, bf16[2,72,1280]{2,1,0:T(8,128)(2,1)S(1)}, u32[]{:S(2)}, u32[]{:S(2)}) %collective-permute-start.13) | collective-permute-done | bytes 368672 | tf_op jit(solution)/shard_map/ppermute | solution.py:664
  114.6 8.5 collective-permute-done.35
  151.3 6.0 fusion.82
  177.1 15.1 %attend_forward.2 = (bf16[10,64,512]{2,1,0:T(8,128)(2,1)}, f32[10,1,512]{2,1,0:T(1,128)}) custom-call(bf16[10,96,1024]{2,1,0:T(8,128)(2,1)} %pad_maximum_fusion.11.q_ref.refs_0_, bf16[10,96,1024]{2,1,0:T(8,128)(2,1)} %pad_maximum_fusion.12.k_ref.refs_1_, bf16[10,64,1024]{2,1,0:T(8,128)(2,1)} %get-tuple-element.313.v_ref.refs_2_), custom_call_target="tpu_custom_call" | custom-call | flops 73400 | bytes 1024 | tf_op jit(solution)/shard_map/attend_forward/pallas_call | solution.py:120
  195.0 10.1 %attend_forward.3 = (bf16[10,64,512]{2,1,0:T(8,128)(2,1)}, f32[10,1,512]{2,1,0:T(1,128)}) custom-call(bf16[10,96,1024]{2,1,0:T(8,128)(2,1)} %pad_maximum_fusion.11.q_ref.refs_0_, bf16[10,96,1024]{2,1,0:T(8,128)(2,1)} %pad_maximum_fusion.12.k_ref.refs_1_, bf16[10,64,1024]{2,1,0:T(8,128)(2,1)} %get-tuple-element.313.v_ref.refs_2_), custom_call_target="tpu_custom_call" | custom-call | flops 36700 | bytes 1024 | tf_op jit(solution)/shard_map/attend_forward/pallas_call | solution.py:120
  208.4 4.0 collective-permute-done.23
  214.8 6.1 collective-permute-start.24
  222.2 5.5 convert_element_type.297
  227.8 6.8 collective-permute-done.27
  234.6 12.2 %collective-permute-done.25 = bf16[640,512]{1,0:T(8,128)(2,1)} collective-permute-done((bf16[640,512]{1,0:T(8,128)(2,1)}, bf16[640,512]{1,0:T(8,128)(2,1)}, u32[]{:S(2)}, u32[]{:S(2)}) %collective-permute-start.25) | collective-permute-done | bytes 655392 | tf_op jit(solution)/shard_map/ppermute | solution.py:600
  254.9 12.1 %collective-permute-done.31 = bf16[640,512]{1,0:T(8,128)(2,1)S(1)} collective-permute-done((bf16[640,512]{1,0:T(8,128)(2,1)S(1)}, bf16[640,512]{1,0:T(8,128)(2,1)S(1)}, u32[]{:S(2)}, u32[]{:S(2)}) %collective-permute-start.31) | collective-permute-done | bytes 655392 | tf_op jit(solution)/shard_map/ppermute | solution.py:600
  268.0 16.7 %hidden_back.1.grad_ref = f32[1024,1600]{1,0:T(8,128)} custom-call(bf16[1024,2560]{1,0:T(8,128)(2,1)} %multiply_convert_fusion.grad_ref.refs_0_.refs_1_, bf16[8,3,320,1600]{3,2,1,0:T(8,128)(2,1)} %all-gather.3.cloned.1.call-done.weight_ref.refs_2_.refs_1_), custom_call_target="tpu_custom_call" | custom-call | flops 83886 | bytes 1024 | tf_op jit(solution)/shard_map/hidden_back/pallas_call | solution.py:275
  284.8 12.5 %multiply_reduce_fusion.2 = (f32[512]{0:T(512)S(1)}, f32[512,2560]{1,0:T(8,128)}) fusion(bf16[2560,512]{1,0:T(8,128)(2,1)S(1)} %pad_maximum_fusion.7, bf16[2560,2560]{1,0:T(8,128)(2,1)} %all-gather.5.cloned.1.call-done, f32[1024,2560]{1,0:T(8,128)} %convert_element_type.297), kind=kOutput, calls=%fused_computation.19 | convolution fusion | flops 6716128768 | bytes 26216448 | tf_op jit(solution)/shard_map/ht,dh->td/dot_general | solution.py:52
  299.3 4.5 multiply_convert_fusion.3.normed_ref.refs_0_
  303.8 7.4 collective-permute-done.33
  311.2 19.7 %ffn_inner.2 = (bf16[512,1600]{1,0:T(8,128)(2,1)}, bf16[512,1600]{1,0:T(8,128)(2,1)}, bf16[512,1600]{1,0:T(8,128)(2,1)}) custom-call(bf16[512,2560]{1,0:T(8,128)(2,1)} %multiply_convert_fusion.3.normed_ref.refs_0_, f32[1024,1600]{1,0:T(8,128)} %hidden_back.1.grad_ref, bf16[8,3,320,1600]{3,2,1,0:T(8,128)(2,1)} %all-gather.3.cloned.1.call-done.weight_ref.refs_2_.refs_1_), custom_call_target="tpu_custom_call" | custom-call | flops 83886 | bytes 1024 | tf_op jit(solution)/shard_map/ffn_inner/pallas_call | solution.py:323
  330.8 15.3 %ffn_back.4 = bf16[512,2560]{1,0:T(8,128)(2,1)} custom-call(bf16[512,1600]{1,0:T(8,128)(2,1)} %get-tuple-element.199.refs_0_.refs_2_, bf16[512,1600]{1,0:T(8,128)(2,1)} %get-tuple-element.202.refs_1_.refs_2_, bf16[8,3,320,1600]{3,2,1,0:T(8,128)(2,1)} %all-gather.3.cloned.1.call-done.weight_ref.refs_2_.refs_1_), custom_call_target="tpu_custom_call" | custom-call | flops 167772 | bytes 1024 | tf_op jit(solution)/shard_map/ffn_back/pallas_call | solution.py:357
  349.5 12.7 %multiply_reduce_fusion.1 = (f32[512]{0:T(512)S(1)}, f32[512,2560]{1,0:T(8,128)}) fusion(bf16[2560,512]{1,0:T(8,128)(2,1)S(1)} %pad_maximum_fusion.6, bf16[2560,2560]{1,0:T(8,128)(2,1)} %all-gather.5.cloned.1.call-done, f32[1024,2560]{1,0:T(8,128)} %convert_element_type.297), kind=kOutput, calls=%fused_computation.17 | convolution fusion | flops 6716128768 | bytes 26216448 | tf_op jit(solution)/shard_map/ht,dh->td/dot_general | solution.py:52
  362.2 4.5 multiply_convert_fusion.2.normed_ref.refs_1_
  366.7 19.6 %ffn_inner.3 = (bf16[512,1600]{1,0:T(8,128)(2,1)}, bf16[512,1600]{1,0:T(8,128)(2,1)}, bf16[512,1600]{1,0:T(8,128)(2,1)}) custom-call(bf16[512,2560]{1,0:T(8,128)(2,1)} %multiply_convert_fusion.2.normed_ref.refs_1_, f32[1024,1600]{1,0:T(8,128)} %hidden_back.1.grad_ref, bf16[8,3,320,1600]{3,2,1,0:T(8,128)(2,1)} %all-gather.3.cloned.1.call-done.weight_ref.refs_2_.refs_1_), custom_call_target="tpu_custom_call" | custom-call | flops 83886 | bytes 1024 | tf_op jit(solution)/shard_map/ffn_inner/pallas_call | solution.py:323
  386.2 15.8 %ffn_back.5 = bf16[512,2560]{1,0:T(8,128)(2,1)} custom-call(bf16[512,1600]{1,0:T(8,128)(2,1)} %get-tuple-element.196.refs_0_.refs_3_, bf16[512,1600]{1,0:T(8,128)(2,1)} %get-tuple-element.195.refs_1_.refs_3_, bf16[8,3,320,1600]{3,2,1,0:T(8,128)(2,1)} %all-gather.3.cloned.1.call-done.weight_ref.refs_2_.refs_1_), custom_call_target="tpu_custom_call" | custom-call | flops 167772 | bytes 1024 | tf_op jit(solution)/shard_map/ffn_back/pallas_call | solution.py:357
  410.7 14.7 %ffn_outer.3.refs_4_ = bf16[8,3,320,1600]{3,2,1,0:T(8,128)(2,1)} custom-call(bf16[512,2560]{1,0:T(8,128)(2,1)} %multiply_convert_fusion.3.normed_ref.refs_0_, bf16[512,2560]{1,0:T(8,128)(2,1)} %multiply_convert_fusion.2.normed_ref.refs_1_, bf16[512,1600]{1,0:T(8,128)(2,1)} %get-tuple-element.199.refs_0_.refs_2_, ...), custom_call_target="tpu_custom_call" | custom-call | flops 167772 | bytes 1024 | tf_op jit(solution)/shard_map/ffn_outer/pallas_call | solution.py:385
  425.4 8.2 collective-permute-done.36
  433.6 23.2 %collective-permute-done.37 = bf16[128,2560]{1,0:T(8,128)(2,1)S(1)} collective-permute-done((bf16[128,2560]{1,0:T(8,128)(2,1)S(1)}, bf16[128,2560]{1,0:T(8,128)(2,1)S(1)}, u32[]{:S(2)}, u32[]{:S(2)}) %collective-permute-start.37) | collective-permute-done | bytes 655392 | tf_op jit(solution)/shard_map/ppermute | solution.py:600
  458.8 14.9 %ffn_outer.4.refs_4_ = bf16[8,3,320,1600]{3,2,1,0:T(8,128)(2,1)} custom-call(bf16[512,2560]{1,0:T(8,128)(2,1)} %multiply_convert_fusion.3.normed_ref.refs_0_, bf16[512,2560]{1,0:T(8,128)(2,1)} %multiply_convert_fusion.2.normed_ref.refs_1_, bf16[512,1600]{1,0:T(8,128)(2,1)} %get-tuple-element.202.refs_1_.refs_2_, ...), custom_call_target="tpu_custom_call", output_to_operand_aliasing={{}: (4, {})} | custom-call | flops 167772 | bytes 1024 | tf_op jit(solution)/shard_map/ffn_outer/pallas_call | solution.py:385
  480.3 14.7 %ffn_outer.5 = bf16[8,3,320,1600]{3,2,1,0:T(8,128)(2,1)} custom-call(bf16[1024,2560]{1,0:T(8,128)(2,1)} %multiply_convert_fusion.grad_ref.refs_0_.refs_1_, bf16[1024,2560]{1,0:T(8,128)(2,1)} %multiply_convert_fusion.grad_ref.refs_0_.refs_1_, bf16[512,1600]{1,0:T(8,128)(2,1)} %get-tuple-element.208.refs_2_.refs_0_, ...), custom_call_target="tpu_custom_call", output_to_operand_aliasing={{}: (4, {})} | custom-call | flops 167772 | bytes 1024 | tf_op jit(solution)/shard_map/ffn_outer/pallas_call | solution.py:385
  495.9 9.2 convert_element_type.309
  511.8 6.4 collective-permute-start.42
  519.5 10.7 %ffn_back.6 = bf16[512,2560]{1,0:T(8,128)(2,1)} custom-call(bf16[512,1600]{1,0:T(8,128)(2,1)} %get-tuple-element.207.refs_3_.refs_0_, bf16[8,3,320,1600]{3,2,1,0:T(8,128)(2,1)} %all-gather.3.cloned.1.call-done.weight_ref.refs_2_.refs_1_), custom_call_target="tpu_custom_call" | custom-call | flops 83886 | bytes 1024 | tf_op jit(solution)/shard_map/ffn_back/pallas_call | solution.py:357
  530.3 9.4 ffn_back.7
  542.4 4.3 select_select_fusion.11
  550.2 7.3 collective-permute-start.44
  560.1 5.7 fusion.27
  565.8 22.4 %attend_backward.2 = (bf16[10,96,512]{2,1,0:T(8,128)(2,1)}, bf16[10,128,512]{2,1,0:T(8,128)(2,1)}, f32[32,512]{1,0:T(8,128)}, f32[10,96,512]{2,1,0:T(8,128)}, f32[10,64,512]{2,1,0:T(8,128)}) custom-call(bf16[10,96,1024]{2,1,0:T(8,128)(2,1)} %pad_maximum_fusion.11.q_ref.refs_0_, bf16[10,96,1024]{2,1,0:T(8,128)(2,1)} %pad_maximum_fusion.12.k_ref.refs_1_, ...), custom_call_target="tpu_custom_call" | custom-call | flops 157286 | bytes 1024 | tf_op jit(solution)/shard_map/attend_backward/pallas_call | solution.py:242
  590.3 4.1 fusion.13
  594.3 9.7 %collective-permute-done.49 = bf16[128,2560]{1,0:T(8,128)(2,1)S(1)} collective-permute-done((bf16[128,2560]{1,0:T(8,128)(2,1)}, bf16[128,2560]{1,0:T(8,128)(2,1)S(1)}, u32[]{:S(2)}, u32[]{:S(2)}) %collective-permute-start.49) | collective-permute-done | bytes 655392 | tf_op jit(solution)/shard_map/ppermute | solution.py:600
  612.4 5.6 fusion.30
  618.0 13.9 %attend_backward.3 = (bf16[10,96,512]{2,1,0:T(8,128)(2,1)}, bf16[10,128,512]{2,1,0:T(8,128)(2,1)}, f32[32,512]{1,0:T(8,128)}) custom-call(bf16[10,96,1024]{2,1,0:T(8,128)(2,1)} %pad_maximum_fusion.11.q_ref.refs_0_, bf16[10,96,1024]{2,1,0:T(8,128)(2,1)} %pad_maximum_fusion.12.k_ref.refs_1_, bf16[10,64,1024]{2,1,0:T(8,128)(2,1)} %get-tuple-element.313.v_ref.refs_2_, ...), custom_call_target="tpu_custom_call" | custom-call | flops 78643 | bytes 1024 | tf_op jit(solution)/shard_map/attend_backward/pallas_call | solution.py:242
  632.0 7.3 latent_back.1
  651.9 5.4 collective-permute-start.54
  658.0 22.4 %collective-permute-done.54 = bf16[256,1056]{0,1:T(8,128)(2,1)} collective-permute-done((bf16[256,1056]{0,1:T(8,128)(2,1)}, bf16[256,1056]{0,1:T(8,128)(2,1)}, u32[]{:S(2)}, u32[]{:S(2)}) %collective-permute-start.54) | collective-permute-done | bytes 540704 | tf_op jit(solution)/shard_map/ppermute | solution.py:637
  687.2 4.4 collective-permute-start.56
  705.7 9.2 collective-permute-start.58
  718.6 13.6 %heads_outer.1 = bf16[8,288,1280]{2,1,0:T(8,128)(2,1)} custom-call(bf16[512,2560]{1,0:T(8,128)(2,1)} %copy-done.15, bf16[512,2560]{1,0:T(8,128)(2,1)} %copy-done.14, bf16[640,512]{1,0:T(8,128)(2,1)} %bitcast.251, bf16[640,512]{1,0:T(8,128)(2,1)} %bitcast.248, bf16[960,512]{1,0:T(8,128)(2,1)} %bitcast.244, bf16[960,512]{1,0:T(8,128)(2,1)} %bitcast.242, ...), custom_call_target="tpu_custom_call" | custom-call | flops 67108 | bytes 1024 | tf_op jit(solution)/shard_map/heads_outer/pallas_call | solution.py:529
  739.7 5.0 convert.124
  752.9 4.7 collective-permute-start.60
  758.9 6.4 collective-permute-done.60
  765.3 8.8 collective-permute-done.61
  780.2 9.9 %collective-permute-done.63 = bf16[272,1056]{1,0:T(8,128)(2,1)S(1)} collective-permute-done((bf16[272,1056]{1,0:T(8,128)(2,1)S(1)}, bf16[272,1056]{1,0:T(8,128)(2,1)S(1)}, u32[]{:S(2)}, u32[]{:S(2)}) %collective-permute-start.63) | collective-permute-done | bytes 574496 | tf_op jit(solution)/shard_map/ppermute | solution.py:600
  790.1 4.1 collective-permute-start.64
  800.1 34.4 %collective-permute-done.67 = bf16[272,1056]{1,0:T(8,128)(2,1)S(1)} collective-permute-done((bf16[272,1056]{1,0:T(8,128)(2,1)S(1)}, bf16[272,1056]{1,0:T(8,128)(2,1)S(1)}, u32[]{:S(2)}, u32[]{:S(2)}) %collective-permute-start.67) | collective-permute-done | bytes 574496 | tf_op jit(solution)/shard_map/ppermute | solution.py:600
  839.9 12.8 %down_outer.1 = (bf16[2560,1056]{1,0:T(8,128)(2,1)}, f32[2560,1]{1,0:T(8,128)}) custom-call(bf16[1024,2560]{1,0:T(8,128)(2,1)} %copy-done.8, bf16[1024,1056]{1,0:T(8,128)(2,1)} %bitcast.223, bf16[2560,1056]{1,0:T(8,128)(2,1)} %copy-done.3, f32[2560,1]{1,0:T(8,128)} %broadcast_in_dim.33.gain_ref), custom_call_target="tpu_custom_call" | custom-call | flops 110729 | bytes 1024 | tf_op jit(solution)/shard_map/down_outer/pallas_call | solution.py:412
  852.7 10.8 %collective-permute-done.69 = bf16[256,2560]{1,0:T(8,128)(2,1)} collective-permute-done((bf16[256,2560]{1,0:T(8,128)(2,1)}, bf16[256,2560]{1,0:T(8,128)(2,1)}, u32[]{:S(2)}, u32[]{:S(2)}) %collective-permute-start.69) | collective-permute-done | bytes 1310752 | tf_op jit(solution)/shard_map/ppermute | solution.py:600
  874.3 17.2 %input_back.1 = f32[1024,2560]{1,0:T(8,128)} custom-call(bf16[1024,1056]{1,0:T(8,128)(2,1)} %bitcast.224, bf16[2560,1056]{1,0:T(8,128)(2,1)} %copy-done.3, bf16[1024,2560]{1,0:T(8,128)(2,1)} %inputs_ref.1, bf16[1024,2560]{1,0:T(8,128)(2,1)} %cot_ref.1, bf16[1024,2560]{1,0:T(8,128)(2,1)} %pad_maximum_fusion.2.mid_ref, f32[1,2560]{1,0:T(1,128)} %broadcast_in_dim.32.gain_ref), custom_call_target="tpu_custom_call" | custom-call | flops 110729 | bytes 1024 | tf_op jit(solution)/shard_map/input_back/pallas_call | solution.py:445
  900.7 11.0 %multiply_subtract_fusion.1 = (f32[320,1600]{1,0:T(8,128)}, f32[320,1600]{1,0:T(8,128)}, f32[320,1600]{1,0:T(8,128)}, f32[320,1600]{1,0:T(8,128)}, f32[320,1600]{1,0:T(8,128)}, /*index=5*/f32[320,1600]{1,0:T(8,128)}) fusion(f32[320,1600]{1,0:T(8,128)S(1)} %copy-done.17, f32[3,320,1600]{2,1,0:T(8,128)} %convert.124, f32[320,1600]{1,0:T(8,128)} %param.54, ...), kind=kLoop, calls=%fused_computation.65 | loop fusion | flops 15360000 | bytes 28672000 | tf_op jit(solution)/shard_map/sub | solution.py:565
  912.8 5.5 multiply_subtract_fusion
  923.2 17.2 %reduce-scatter.14.cloned.1.call-done = bf16[96,1056]{1,0:T(8,128)(2,1)} async-done(((bf16[768,1056]{1,0:T(8,128)(2,1)}), bf16[96,1056]{1,0:T(8,128)(2,1)}) %reduce-scatter.14.cloned.1.call-update) | async-done | bytes 202768 | tf_op jit(solution)/shard_map/reduce_scatter | solution.py:707
  (506 shorter events, 248.6 us)
Async XLA Ops:
  7.2 260.8 %all-gather.3.cloned.1.call-start = ((), (), s32[]{:S(2)}) async-start(), calls=%async_computation.5 | async-start | bytes 28753920 | tf_op jit(solution)/shard_map/all_gather | solution.py:798
  13.4 271.4 %all-gather.5.cloned.1.call-start = ((), (), s32[]{:S(2)}) async-start(), calls=%async_computation.6 | async-start | bytes 14745600 | tf_op jit(solution)/shard_map/all_gather | solution.py:795
  28.0 9.8 %collective-permute-start.3 = (bf16[80,1056]{1,0:T(8,128)(2,1)S(1)}, bf16[80,1056]{1,0:T(8,128)(2,1)S(1)}, u32[]{:S(2)}, u32[]{:S(2)}) collective-permute-start(bf16[80,1056]{1,0:T(8,128)(2,1)S(1)} %collective-permute-done.1), channel_id=1, source_target_pairs={{1,0},{2,1},{5,4},{6,5},{9,8},{10,9},{13,12},{14,13},{17,16},{18,1... | collective-permute-start | bytes 506888 | tf_op jit(solution)/shard_map/ppermute | solution.py:600
  45.9 11.4 %collective-permute-start.7 = (bf16[1,72,1280]{2,1,0:T(8,128)(2,1)S(1)}, bf16[1,72,1280]{2,1,0:T(8,128)(2,1)S(1)}, u32[]{:S(2)}, u32[]{:S(2)}) collective-permute-start(bf16[1,72,1280]{2,1,0:T(8,128)(2,1)S(1)} %get-tuple-element.153), channel_id=1, source_target_pairs={{0,16},{4,20},{8,24},{12,28},{16,0},{20,4},{24,8},{28,12},{1,17},{... | collective-permute-start | bytes 552968 | tf_op jit(solution)/shard_map/ppermute | solution.py:664
  47.7 26.1 %collective-permute-start.8 = (bf16[1,160,1056]{2,1,0:T(8,128)(2,1)S(1)}, bf16[1,160,1056]{2,1,0:T(8,128)(2,1)S(1)}, u32[]{:S(2)}, u32[]{:S(2)}) collective-permute-start(bf16[1,160,1056]{2,1,0:T(8,128)(2,1)S(1)} %get-tuple-element.154), channel_id=1, source_target_pairs={{0,8},{4,12},{8,0},{12,4},{16,24},{20,28},{24,16},{28,20},{1,9},{5... | collective-permute-start | bytes 1013768 | tf_op jit(solution)/shard_map/ppermute | solution.py:664
  49.3 24.4 %collective-permute-start.9 = (bf16[1,160,1056]{2,1,0:T(8,128)(2,1)S(1)}, bf16[1,160,1056]{2,1,0:T(8,128)(2,1)S(1)}, u32[]{:S(2)}, u32[]{:S(2)}) collective-permute-start(bf16[1,160,1056]{2,1,0:T(8,128)(2,1)S(1)} %get-tuple-element.155), channel_id=1, source_target_pairs={{0,16},{4,20},{8,24},{12,28},{16,0},{20,4},{24,8},{28,12},{1,17},{... | collective-permute-start | bytes 1013768 | tf_op jit(solution)/shard_map/ppermute | solution.py:664
  49.8 23.9 %collective-permute-start.6 = (bf16[1,72,1280]{2,1,0:T(8,128)(2,1)S(1)}, bf16[1,72,1280]{2,1,0:T(8,128)(2,1)S(1)}, u32[]{:S(2)}, u32[]{:S(2)}) collective-permute-start(bf16[1,72,1280]{2,1,0:T(8,128)(2,1)S(1)} %get-tuple-element.152), channel_id=1, source_target_pairs={{0,8},{4,12},{8,0},{12,4},{16,24},{20,28},{24,16},{28,20},{1,9},{5... | collective-permute-start | bytes 552968 | tf_op jit(solution)/shard_map/ppermute | solution.py:664
  50.3 23.5 %collective-permute-start.10 = (bf16[320,640]{1,0:T(8,128)(2,1)S(1)}, bf16[320,640]{1,0:T(8,128)(2,1)S(1)}, u32[]{:S(2)}, u32[]{:S(2)}) collective-permute-start(bf16[320,640]{1,0:T(8,128)(2,1)S(1)} %convert_bitcast_fusion.3), channel_id=1, source_target_pairs={{0,1},{1,2},{2,3},{4,5},{5,6},{6,7},{8,9},{9,10},{10,11},{12,13},{... | collective-permute-start | bytes 1228808 | tf_op jit(solution)/shard_map/ppermute | solution.py:599
  57.4 16.5 %collective-permute-start.11 = (bf16[320,640]{1,0:T(8,128)(2,1)S(1)}, bf16[320,640]{1,0:T(8,128)(2,1)S(1)}, u32[]{:S(2)}, u32[]{:S(2)}) collective-permute-start(bf16[320,640]{1,0:T(8,128)(2,1)S(1)} %convert_bitcast_fusion.3), channel_id=1, source_target_pairs={{1,0},{2,1},{3,2},{5,4},{6,5},{7,6},{9,8},{10,9},{11,10},{13,12},{... | collective-permute-start | bytes 1228808 | tf_op jit(solution)/shard_map/ppermute | solution.py:600
  73.8 11.6 %collective-permute-start.12 = (bf16[2,72,1280]{2,1,0:T(8,128)(2,1)S(1)}, bf16[2,72,1280]{2,1,0:T(8,128)(2,1)S(1)}, u32[]{:S(2)}, u32[]{:S(2)}) collective-permute-start(bf16[2,72,1280]{2,1,0:T(8,128)(2,1)S(1)} %pad_maximum_fusion.23), channel_id=1, source_target_pairs={{0,16},{4,20},{8,24},{12,28},{16,0},{20,4},{24,8},{28,12},{1,17},{... | collective-permute-start | bytes 1105928 | tf_op jit(solution)/shard_map/ppermute | solution.py:664
  74.5 38.1 %collective-permute-start.14 = (bf16[2,160,1056]{2,1,0:T(8,128)(2,1)S(1)}, bf16[2,160,1056]{2,1,0:T(8,128)(2,1)}, u32[]{:S(2)}, u32[]{:S(2)}) collective-permute-start(bf16[2,160,1056]{2,1,0:T(8,128)(2,1)S(1)} %pad_maximum_fusion.20), channel_id=1, source_target_pairs={{0,16},{4,20},{8,24},{12,28},{16,0},{20,4},{24,8},{28,12},{1,17},{... | collective-permute-start | bytes 2027528 | tf_op jit(solution)/shard_map/ppermute | solution.py:664
  76.1 36.5 %collective-permute-start.15 = (bf16[2,160,1056]{2,1,0:T(8,128)(2,1)S(1)}, bf16[2,160,1056]{2,1,0:T(8,128)(2,1)}, u32[]{:S(2)}, u32[]{:S(2)}) collective-permute-start(bf16[2,160,1056]{2,1,0:T(8,128)(2,1)S(1)} %pad_maximum_fusion.21), channel_id=1, source_target_pairs={{0,8},{4,12},{8,0},{12,4},{16,24},{20,28},{24,16},{28,20},{1,9},{5... | collective-permute-start | bytes 2027528 | tf_op jit(solution)/shard_map/ppermute | solution.py:664
  77.6 35.0 %collective-permute-start.16 = (bf16[320,640]{1,0:T(8,128)(2,1)S(1)}, bf16[320,640]{1,0:T(8,128)(2,1)S(1)}, u32[]{:S(2)}, u32[]{:S(2)}) collective-permute-start(bf16[320,640]{1,0:T(8,128)(2,1)S(1)} %collective-permute-done.10), channel_id=1, source_target_pairs={{1,2},{2,3},{5,6},{6,7},{9,10},{10,11},{13,14},{14,15},{17,18},{18... | collective-permute-start | bytes 1228808 | tf_op jit(solution)/shard_map/ppermute | solution.py:599
  78.3 34.3 %collective-permute-start.17 = (bf16[320,640]{1,0:T(8,128)(2,1)S(1)}, bf16[320,640]{1,0:T(8,128)(2,1)S(1)}, u32[]{:S(2)}, u32[]{:S(2)}) collective-permute-start(bf16[320,640]{1,0:T(8,128)(2,1)S(1)} %collective-permute-done.11), channel_id=1, source_target_pairs={{1,0},{2,1},{5,4},{6,5},{9,8},{10,9},{13,12},{14,13},{17,16},{18,1... | collective-permute-start | bytes 1228808 | tf_op jit(solution)/shard_map/ppermute | solution.py:600
  85.4 27.1 %collective-permute-start.13 = (bf16[2,72,1280]{2,1,0:T(8,128)(2,1)S(1)}, bf16[2,72,1280]{2,1,0:T(8,128)(2,1)S(1)}, u32[]{:S(2)}, u32[]{:S(2)}) collective-permute-start(bf16[2,72,1280]{2,1,0:T(8,128)(2,1)S(1)} %pad_maximum_fusion.24), channel_id=1, source_target_pairs={{0,8},{4,12},{8,0},{12,4},{16,24},{20,28},{24,16},{28,20},{1,9},{5... | collective-permute-start | bytes 1105928 | tf_op jit(solution)/shard_map/ppermute | solution.py:664
  113.3 9.8 %collective-permute-start.35 = (bf16[320,640]{1,0:T(8,128)(2,1)S(1)}, bf16[320,640]{1,0:T(8,128)(2,1)S(1)}, u32[]{:S(2)}, u32[]{:S(2)}) collective-permute-start(bf16[320,640]{1,0:T(8,128)(2,1)S(1)} %collective-permute-done.17), channel_id=1, source_target_pairs={{1,0},{5,4},{9,8},{13,12},{17,16},{21,20},{25,24},{29,28}} | collective-permute-start | bytes 1228808 | tf_op jit(solution)/shard_map/ppermute | solution.py:600
  124.8 278.9 %reduce-scatter.6.cloned.1.call-start = ((), (), s32[]{:S(2)}) async-start(), calls=%async_computation.7 | async-start | bytes 3276800 | tf_op jit(solution)/shard_map/reduce_scatter | solution.py:874
  135.9 12.7 %collective-permute-start.21 = (bf16[4,160,1056]{2,1,0:T(8,128)(2,1)}, bf16[4,160,1056]{2,1,0:T(8,128)(2,1)}, u32[]{:S(2)}, u32[]{:S(2)}) collective-permute-start(bf16[4,160,1056]{2,1,0:T(8,128)(2,1)} %pad_maximum_fusion.17), channel_id=1, source_target_pairs={{0,4},{4,0},{8,12},{12,8},{16,20},{20,16},{24,28},{28,24},{1,5},{5... | collective-permute-start | bytes 4055048 | tf_op jit(solution)/shard_map/ppermute | solution.py:664
  192.2 16.2 %collective-permute-start.22 = (bf16[640,512]{1,0:T(8,128)(2,1)}, bf16[640,512]{1,0:T(8,128)(2,1)S(1)}, u32[]{:S(2)}, u32[]{:S(2)}) collective-permute-start(bf16[640,512]{1,0:T(8,128)(2,1)} %bitcast.246), channel_id=1, source_target_pairs={{0,1},{1,2},{2,3},{4,5},{5,6},{6,7},{8,9},{9,10},{10,11},{12,13},{... | collective-permute-start | bytes 1966088 | tf_op jit(solution)/shard_map/ppermute | solution.py:599
  193.7 18.7 %collective-permute-start.23 = (bf16[640,512]{1,0:T(8,128)(2,1)}, bf16[640,512]{1,0:T(8,128)(2,1)S(1)}, u32[]{:S(2)}, u32[]{:S(2)}) collective-permute-start(bf16[640,512]{1,0:T(8,128)(2,1)} %bitcast.247), channel_id=1, source_target_pairs={{1,0},{2,1},{3,2},{5,4},{6,5},{7,6},{9,8},{10,9},{11,10},{13,12},{... | collective-permute-start | bytes 1966088 | tf_op jit(solution)/shard_map/ppermute | solution.py:600
  212.5 15.3 %collective-permute-start.26 = (bf16[640,512]{1,0:T(8,128)(2,1)S(1)}, bf16[640,512]{1,0:T(8,128)(2,1)S(1)}, u32[]{:S(2)}, u32[]{:S(2)}) collective-permute-start(bf16[640,512]{1,0:T(8,128)(2,1)S(1)} %collective-permute-done.22), channel_id=1, source_target_pairs={{1,2},{2,3},{5,6},{6,7},{9,10},{10,11},{13,14},{14,15},{17,18},{18... | collective-permute-start | bytes 1966088 | tf_op jit(solution)/shard_map/ppermute | solution.py:599
  213.3 21.3 %collective-permute-start.27 = (bf16[640,512]{1,0:T(8,128)(2,1)S(1)}, bf16[640,512]{1,0:T(8,128)(2,1)S(1)}, u32[]{:S(2)}, u32[]{:S(2)}) collective-permute-start(bf16[640,512]{1,0:T(8,128)(2,1)S(1)} %collective-permute-done.23), channel_id=1, source_target_pairs={{1,0},{2,1},{5,4},{6,5},{9,8},{10,9},{13,12},{14,13},{17,16},{18,1... | collective-permute-start | bytes 1966088 | tf_op jit(solution)/shard_map/ppermute | solution.py:600
  214.8 19.8 %collective-permute-start.24 = (bf16[640,512]{1,0:T(8,128)(2,1)}, bf16[640,512]{1,0:T(8,128)(2,1)S(1)}, u32[]{:S(2)}, u32[]{:S(2)}) collective-permute-start(bf16[640,512]{1,0:T(8,128)(2,1)} %bitcast.249), channel_id=1, source_target_pairs={{0,1},{1,2},{2,3},{4,5},{5,6},{6,7},{8,9},{9,10},{10,11},{12,13},{... | collective-permute-start | bytes 1966088 | tf_op jit(solution)/shard_map/ppermute | solution.py:599
  220.9 25.9 %collective-permute-start.25 = (bf16[640,512]{1,0:T(8,128)(2,1)}, bf16[640,512]{1,0:T(8,128)(2,1)}, u32[]{:S(2)}, u32[]{:S(2)}) collective-permute-start(bf16[640,512]{1,0:T(8,128)(2,1)} %bitcast.250), channel_id=1, source_target_pairs={{1,0},{2,1},{3,2},{5,4},{6,5},{7,6},{9,8},{10,9},{11,10},{13,12},{... | collective-permute-start | bytes 1966088 | tf_op jit(solution)/shard_map/ppermute | solution.py:600
  247.5 19.6 %collective-permute-start.31 = (bf16[640,512]{1,0:T(8,128)(2,1)S(1)}, bf16[640,512]{1,0:T(8,128)(2,1)S(1)}, u32[]{:S(2)}, u32[]{:S(2)}) collective-permute-start(bf16[640,512]{1,0:T(8,128)(2,1)S(1)} %collective-permute-done.27), channel_id=1, source_target_pairs={{1,0},{5,4},{9,8},{13,12},{17,16},{21,20},{25,24},{29,28}} | collective-permute-start | bytes 1966088 | tf_op jit(solution)/shard_map/ppermute | solution.py:600
  252.0 32.7 %collective-permute-start.28 = (bf16[640,512]{1,0:T(8,128)(2,1)S(1)}, bf16[640,512]{1,0:T(8,128)(2,1)}, u32[]{:S(2)}, u32[]{:S(2)}) collective-permute-start(bf16[640,512]{1,0:T(8,128)(2,1)S(1)} %collective-permute-done.24), channel_id=1, source_target_pairs={{1,2},{2,3},{5,6},{6,7},{9,10},{10,11},{13,14},{14,15},{17,18},{18... | collective-permute-start | bytes 1966088 | tf_op jit(solution)/shard_map/ppermute | solution.py:599
  253.6 31.2 %collective-permute-start.29 = (bf16[640,512]{1,0:T(8,128)(2,1)}, bf16[640,512]{1,0:T(8,128)(2,1)}, u32[]{:S(2)}, u32[]{:S(2)}) collective-permute-start(bf16[640,512]{1,0:T(8,128)(2,1)} %collective-permute-done.25), channel_id=1, source_target_pairs={{1,0},{2,1},{5,4},{6,5},{9,8},{10,9},{13,12},{14,13},{17,16},{18,1... | collective-permute-start | bytes 1966088 | tf_op jit(solution)/shard_map/ppermute | solution.py:600
  298.0 13.1 %collective-permute-start.33 = (bf16[640,512]{1,0:T(8,128)(2,1)}, bf16[640,512]{1,0:T(8,128)(2,1)S(1)}, u32[]{:S(2)}, u32[]{:S(2)}) collective-permute-start(bf16[640,512]{1,0:T(8,128)(2,1)} %collective-permute-done.29), channel_id=1, source_target_pairs={{1,0},{5,4},{9,8},{13,12},{17,16},{21,20},{25,24},{29,28}} | collective-permute-start | bytes 1966088 | tf_op jit(solution)/shard_map/ppermute | solution.py:600
  346.2 132.9 %reduce-scatter.8.cloned.1.call-start = ((), (), s32[]{:S(2)}) async-start(), calls=%async_computation.8 | async-start | bytes 3276800 | tf_op jit(solution)/shard_map/reduce_scatter | solution.py:874
  402.1 337.6 %reduce-scatter.10.cloned.1.call-start = ((), (), s32[]{:S(2)}) async-start(), calls=%async_computation.9 | async-start | bytes 28753920 | tf_op jit(solution)/shard_map/reduce_scatter | solution.py:707
  407.6 26.0 %collective-permute-start.36 = (bf16[128,2560]{1,0:T(8,128)(2,1)S(1)}, bf16[128,2560]{1,0:T(8,128)(2,1)S(1)}, u32[]{:S(2)}, u32[]{:S(2)}) collective-permute-start(bf16[128,2560]{1,0:T(8,128)(2,1)S(1)} %fusion.33), channel_id=1, source_target_pairs={{0,1},{1,2},{2,3},{4,5},{5,6},{6,7},{8,9},{9,10},{10,11},{12,13},{... | collective-permute-start | bytes 1966088 | tf_op jit(solution)/shard_map/ppermute | solution.py:599
  409.4 47.4 %collective-permute-start.37 = (bf16[128,2560]{1,0:T(8,128)(2,1)S(1)}, bf16[128,2560]{1,0:T(8,128)(2,1)S(1)}, u32[]{:S(2)}, u32[]{:S(2)}) collective-permute-start(bf16[128,2560]{1,0:T(8,128)(2,1)S(1)} %fusion.33), channel_id=1, source_target_pairs={{1,0},{2,1},{3,2},{5,4},{6,5},{7,6},{9,8},{10,9},{11,10},{13,12},{... | collective-permute-start | bytes 1966088 | tf_op jit(solution)/shard_map/ppermute | solution.py:600
  456.8 16.9 %collective-permute-start.38 = (bf16[128,2560]{1,0:T(8,128)(2,1)S(1)}, bf16[128,2560]{1,0:T(8,128)(2,1)S(1)}, u32[]{:S(2)}, u32[]{:S(2)}) collective-permute-start(bf16[128,2560]{1,0:T(8,128)(2,1)S(1)} %collective-permute-done.36), channel_id=1, source_target_pairs={{1,2},{2,3},{5,6},{6,7},{9,10},{10,11},{13,14},{14,15},{17,18},{18... | collective-permute-start | bytes 1966088 | tf_op jit(solution)/shard_map/ppermute | solution.py:599
  457.5 19.5 %collective-permute-start.39 = (bf16[128,2560]{1,0:T(8,128)(2,1)S(1)}, bf16[128,2560]{1,0:T(8,128)(2,1)S(1)}, u32[]{:S(2)}, u32[]{:S(2)}) collective-permute-start(bf16[128,2560]{1,0:T(8,128)(2,1)S(1)} %collective-permute-done.37), channel_id=1, source_target_pairs={{1,0},{2,1},{5,4},{6,5},{9,8},{10,9},{13,12},{14,13},{17,16},{18,1... | collective-permute-start | bytes 1966088 | tf_op jit(solution)/shard_map/ppermute | solution.py:600
  477.0 18.0 %collective-permute-start.40 = (bf16[128,2560]{1,0:T(8,128)(2,1)S(1)}, bf16[128,2560]{1,0:T(8,128)(2,1)S(1)}, u32[]{:S(2)}, u32[]{:S(2)}) collective-permute-start(bf16[128,2560]{1,0:T(8,128)(2,1)S(1)} %collective-permute-done.38), channel_id=1, source_target_pairs={{2,3},{6,7},{10,11},{14,15},{18,19},{22,23},{26,27},{30,31}} | collective-permute-start | bytes 1966088 | tf_op jit(solution)/shard_map/ppermute | solution.py:599
  477.7 17.3 %collective-permute-start.41 = (bf16[128,2560]{1,0:T(8,128)(2,1)S(1)}, bf16[128,2560]{1,0:T(8,128)(2,1)}, u32[]{:S(2)}, u32[]{:S(2)}) collective-permute-start(bf16[128,2560]{1,0:T(8,128)(2,1)S(1)} %collective-permute-done.39), channel_id=1, source_target_pairs={{1,0},{5,4},{9,8},{13,12},{17,16},{21,20},{25,24},{29,28}} | collective-permute-start | bytes 1966088 | tf_op jit(solution)/shard_map/ppermute | solution.py:600
  495.9 402.2 %reduce-scatter.12.cloned.1.call-start = ((), (), s32[]{:S(2)}) async-start(), calls=%async_computation.10 | async-start | bytes 6635520 | tf_op jit(solution)/shard_map/reduce_scatter | solution.py:707
  511.8 35.3 %collective-permute-start.42 = (bf16[128,2560]{1,0:T(8,128)(2,1)}, bf16[128,2560]{1,0:T(8,128)(2,1)}, u32[]{:S(2)}, u32[]{:S(2)}) collective-permute-start(bf16[128,2560]{1,0:T(8,128)(2,1)} %fusion.34), channel_id=1, source_target_pairs={{0,1},{1,2},{2,3},{4,5},{5,6},{6,7},{8,9},{9,10},{10,11},{12,13},{... | collective-permute-start | bytes 1966088 | tf_op jit(solution)/shard_map/ppermute | solution.py:599
  518.2 28.9 %collective-permute-start.43 = (bf16[128,2560]{1,0:T(8,128)(2,1)}, bf16[128,2560]{1,0:T(8,128)(2,1)}, u32[]{:S(2)}, u32[]{:S(2)}) collective-permute-start(bf16[128,2560]{1,0:T(8,128)(2,1)} %fusion.34), channel_id=1, source_target_pairs={{1,0},{2,1},{3,2},{5,4},{6,5},{7,6},{9,8},{10,9},{11,10},{13,12},{... | collective-permute-start | bytes 1966088 | tf_op jit(solution)/shard_map/ppermute | solution.py:600
  547.2 41.0 %collective-permute-start.46 = (bf16[128,2560]{1,0:T(8,128)(2,1)}, bf16[128,2560]{1,0:T(8,128)(2,1)}, u32[]{:S(2)}, u32[]{:S(2)}) collective-permute-start(bf16[128,2560]{1,0:T(8,128)(2,1)} %collective-permute-done.42), channel_id=1, source_target_pairs={{1,2},{2,3},{5,6},{6,7},{9,10},{10,11},{13,14},{14,15},{17,18},{18... | collective-permute-start | bytes 1966088 | tf_op jit(solution)/shard_map/ppermute | solution.py:599
  548.8 39.4 %collective-permute-start.47 = (bf16[128,2560]{1,0:T(8,128)(2,1)}, bf16[128,2560]{1,0:T(8,128)(2,1)}, u32[]{:S(2)}, u32[]{:S(2)}) collective-permute-start(bf16[128,2560]{1,0:T(8,128)(2,1)} %collective-permute-done.43), channel_id=1, source_target_pairs={{1,0},{2,1},{5,4},{6,5},{9,8},{10,9},{13,12},{14,13},{17,16},{18,1... | collective-permute-start | bytes 1966088 | tf_op jit(solution)/shard_map/ppermute | solution.py:600
  550.2 38.0 %collective-permute-start.44 = (bf16[256,2560]{1,0:T(8,128)(2,1)S(1)}, bf16[256,2560]{1,0:T(8,128)(2,1)}, u32[]{:S(2)}, u32[]{:S(2)}) collective-permute-start(bf16[256,2560]{1,0:T(8,128)(2,1)S(1)} %get-tuple-element.213), channel_id=1, source_target_pairs={{0,1},{4,5},{8,9},{12,13},{16,17},{20,21},{24,25},{28,29}} | collective-permute-start | bytes 3932168 | tf_op jit(solution)/shard_map/ppermute | solution.py:637
  557.5 30.7 %collective-permute-start.45 = (bf16[256,2560]{1,0:T(8,128)(2,1)S(1)}, bf16[256,2560]{1,0:T(8,128)(2,1)}, u32[]{:S(2)}, u32[]{:S(2)}) collective-permute-start(bf16[256,2560]{1,0:T(8,128)(2,1)S(1)} %get-tuple-element.214), channel_id=1, source_target_pairs={{3,2},{7,6},{11,10},{15,14},{19,18},{23,22},{27,26},{31,30}} | collective-permute-start | bytes 3932168 | tf_op jit(solution)/shard_map/ppermute | solution.py:639
  588.9 15.1 %collective-permute-start.49 = (bf16[128,2560]{1,0:T(8,128)(2,1)}, bf16[128,2560]{1,0:T(8,128)(2,1)S(1)}, u32[]{:S(2)}, u32[]{:S(2)}) collective-permute-start(bf16[128,2560]{1,0:T(8,128)(2,1)} %collective-permute-done.47), channel_id=1, source_target_pairs={{1,0},{5,4},{9,8},{13,12},{17,16},{21,20},{25,24},{29,28}} | collective-permute-start | bytes 1966088 | tf_op jit(solution)/shard_map/ppermute | solution.py:600
  606.6 32.7 %collective-permute-start.50 = (bf16[256,2560]{1,0:T(8,128)(2,1)}, bf16[256,2560]{1,0:T(8,128)(2,1)}, u32[]{:S(2)}, u32[]{:S(2)}) collective-permute-start(bf16[256,2560]{1,0:T(8,128)(2,1)} %get-tuple-element.222), channel_id=1, source_target_pairs={{0,1},{1,2},{4,5},{5,6},{8,9},{9,10},{12,13},{13,14},{16,17},{17,1... | collective-permute-start | bytes 3932168 | tf_op jit(solution)/shard_map/ppermute | solution.py:637
  609.4 29.9 %collective-permute-start.51 = (bf16[256,2560]{1,0:T(8,128)(2,1)}, bf16[256,2560]{1,0:T(8,128)(2,1)}, u32[]{:S(2)}, u32[]{:S(2)}) collective-permute-start(bf16[256,2560]{1,0:T(8,128)(2,1)} %get-tuple-element.223), channel_id=1, source_target_pairs={{3,2},{2,1},{7,6},{6,5},{11,10},{10,9},{15,14},{14,13},{19,18},{18... | collective-permute-start | bytes 3932168 | tf_op jit(solution)/shard_map/ppermute | solution.py:639
  643.3 42.7 %collective-permute-start.52 = (bf16[256,2560]{1,0:T(8,128)(2,1)}, bf16[256,2560]{1,0:T(8,128)(2,1)}, u32[]{:S(2)}, u32[]{:S(2)}) collective-permute-start(bf16[256,2560]{1,0:T(8,128)(2,1)} %get-tuple-element.233), channel_id=1, source_target_pairs={{0,1},{1,2},{2,3},{4,5},{5,6},{6,7},{8,9},{9,10},{10,11},{12,13},{... | collective-permute-start | bytes 3932168 | tf_op jit(solution)/shard_map/ppermute | solution.py:637
  646.6 39.3 %collective-permute-start.53 = (bf16[256,2560]{1,0:T(8,128)(2,1)}, bf16[256,2560]{1,0:T(8,128)(2,1)}, u32[]{:S(2)}, u32[]{:S(2)}) collective-permute-start(bf16[256,2560]{1,0:T(8,128)(2,1)} %get-tuple-element.234), channel_id=1, source_target_pairs={{3,2},{2,1},{1,0},{7,6},{6,5},{5,4},{11,10},{10,9},{9,8},{15,14},{... | collective-permute-start | bytes 3932168 | tf_op jit(solution)/shard_map/ppermute | solution.py:639
  651.9 28.5 %collective-permute-start.54 = (bf16[256,1056]{0,1:T(8,128)(2,1)}, bf16[256,1056]{0,1:T(8,128)(2,1)}, u32[]{:S(2)}, u32[]{:S(2)}) collective-permute-start(bf16[256,1056]{0,1:T(8,128)(2,1)} %bitcast.259), channel_id=1, source_target_pairs={{0,1},{4,5},{8,9},{12,13},{16,17},{20,21},{24,25},{28,29}} | collective-permute-start | bytes 1622024 | tf_op jit(solution)/shard_map/ppermute | solution.py:637
  657.3 25.2 %collective-permute-start.55 = (bf16[256,1056]{0,1:T(8,128)(2,1)}, bf16[256,1056]{0,1:T(8,128)(2,1)S(1)}, u32[]{:S(2)}, u32[]{:S(2)}) collective-permute-start(bf16[256,1056]{0,1:T(8,128)(2,1)} %bitcast.258), channel_id=1, source_target_pairs={{3,2},{7,6},{11,10},{15,14},{19,18},{23,22},{27,26},{31,30}} | collective-permute-start | bytes 1622024 | tf_op jit(solution)/shard_map/ppermute | solution.py:639
  687.2 11.3 %collective-permute-start.56 = (bf16[256,1056]{0,1:T(8,128)(2,1)S(1)}, bf16[256,1056]{0,1:T(8,128)(2,1)S(1)}, u32[]{:S(2)}, u32[]{:S(2)}) collective-permute-start(bf16[256,1056]{0,1:T(8,128)(2,1)S(1)} %copy.107), channel_id=1, source_target_pairs={{0,1},{1,2},{4,5},{5,6},{8,9},{9,10},{12,13},{13,14},{16,17},{17,1... | collective-permute-start | bytes 1622024 | tf_op jit(solution)/shard_map/ppermute | solution.py:637
  705.7 26.6 %collective-permute-start.58 = (bf16[256,1056]{0,1:T(8,128)(2,1)}, bf16[256,1056]{0,1:T(8,128)(2,1)}, u32[]{:S(2)}, u32[]{:S(2)}) collective-permute-start(bf16[256,1056]{0,1:T(8,128)(2,1)} %copy.111), channel_id=1, source_target_pairs={{0,1},{1,2},{2,3},{4,5},{5,6},{6,7},{8,9},{9,10},{10,11},{12,13},{... | collective-permute-start | bytes 1622024 | tf_op jit(solution)/shard_map/ppermute | solution.py:637
  717.0 17.4 %collective-permute-start.59 = (bf16[256,1056]{0,1:T(8,128)(2,1)}, bf16[256,1056]{0,1:T(8,128)(2,1)}, u32[]{:S(2)}, u32[]{:S(2)}) collective-permute-start(bf16[256,1056]{0,1:T(8,128)(2,1)} %copy.113), channel_id=1, source_target_pairs={{3,2},{2,1},{1,0},{7,6},{6,5},{5,4},{11,10},{10,9},{9,8},{15,14},{... | collective-permute-start | bytes 1622024 | tf_op jit(solution)/shard_map/ppermute | solution.py:639
  744.7 195.7 %reduce-scatter.14.cloned.1.call-start = ((), (), s32[]{:S(2)}) async-start(), calls=%async_computation.11 | async-start | bytes 1990656 | tf_op jit(solution)/shard_map/reduce_scatter | solution.py:707
  752.9 12.5 %collective-permute-start.60 = (bf16[272,1056]{1,0:T(8,128)(2,1)S(1)}, bf16[272,1056]{1,0:T(8,128)(2,1)S(1)}, u32[]{:S(2)}, u32[]{:S(2)}) collective-permute-start(bf16[272,1056]{1,0:T(8,128)(2,1)S(1)} %pad_maximum_fusion.22), channel_id=1, source_target_pairs={{0,1},{1,2},{2,3},{4,5},{5,6},{6,7},{8,9},{9,10},{10,11},{12,13},{... | collective-permute-start | bytes 1723400 | tf_op jit(solution)/shard_map/ppermute | solution.py:599
  757.6 16.6 %collective-permute-start.61 = (bf16[272,1056]{1,0:T(8,128)(2,1)S(1)}, bf16[272,1056]{1,0:T(8,128)(2,1)S(1)}, u32[]{:S(2)}, u32[]{:S(2)}) collective-permute-start(bf16[272,1056]{1,0:T(8,128)(2,1)S(1)} %pad_maximum_fusion.22), channel_id=1, source_target_pairs={{1,0},{2,1},{3,2},{5,4},{6,5},{7,6},{9,8},{10,9},{11,10},{13,12},{... | collective-permute-start | bytes 1723400 | tf_op jit(solution)/shard_map/ppermute | solution.py:600
  774.8 15.3 %collective-permute-start.63 = (bf16[272,1056]{1,0:T(8,128)(2,1)S(1)}, bf16[272,1056]{1,0:T(8,128)(2,1)S(1)}, u32[]{:S(2)}, u32[]{:S(2)}) collective-permute-start(bf16[272,1056]{1,0:T(8,128)(2,1)S(1)} %collective-permute-done.61), channel_id=1, source_target_pairs={{1,0},{2,1},{5,4},{6,5},{9,8},{10,9},{13,12},{14,13},{17,16},{18,1... | collective-permute-start | bytes 1723400 | tf_op jit(solution)/shard_map/ppermute | solution.py:600
  790.1 44.4 %collective-permute-start.64 = (bf16[256,2560]{1,0:T(8,128)(2,1)S(1)}, bf16[256,2560]{1,0:T(8,128)(2,1)}, u32[]{:S(2)}, u32[]{:S(2)}) collective-permute-start(bf16[256,2560]{1,0:T(8,128)(2,1)S(1)} %fusion.11), channel_id=1, source_target_pairs={{0,1},{1,2},{2,3},{4,5},{5,6},{6,7},{8,9},{9,10},{10,11},{12,13},{... | collective-permute-start | bytes 3932168 | tf_op jit(solution)/shard_map/ppermute | solution.py:599
  794.2 40.3 %collective-permute-start.65 = (bf16[256,2560]{1,0:T(8,128)(2,1)S(1)}, bf16[256,2560]{1,0:T(8,128)(2,1)}, u32[]{:S(2)}, u32[]{:S(2)}) collective-permute-start(bf16[256,2560]{1,0:T(8,128)(2,1)S(1)} %fusion.11), channel_id=1, source_target_pairs={{1,0},{2,1},{3,2},{5,4},{6,5},{7,6},{9,8},{10,9},{11,10},{13,12},{... | collective-permute-start | bytes 3932168 | tf_op jit(solution)/shard_map/ppermute | solution.py:600
  798.3 36.2 %collective-permute-start.67 = (bf16[272,1056]{1,0:T(8,128)(2,1)S(1)}, bf16[272,1056]{1,0:T(8,128)(2,1)S(1)}, u32[]{:S(2)}, u32[]{:S(2)}) collective-permute-start(bf16[272,1056]{1,0:T(8,128)(2,1)S(1)} %collective-permute-done.63), channel_id=1, source_target_pairs={{1,0},{5,4},{9,8},{13,12},{17,16},{21,20},{25,24},{29,28}} | collective-permute-start | bytes 1723400 | tf_op jit(solution)/shard_map/ppermute | solution.py:600
  834.5 18.2 %collective-permute-start.68 = (bf16[256,2560]{1,0:T(8,128)(2,1)}, bf16[256,2560]{1,0:T(8,128)(2,1)}, u32[]{:S(2)}, u32[]{:S(2)}) collective-permute-start(bf16[256,2560]{1,0:T(8,128)(2,1)} %collective-permute-done.64), channel_id=1, source_target_pairs={{1,2},{2,3},{5,6},{6,7},{9,10},{10,11},{13,14},{14,15},{17,18},{18... | collective-permute-start | bytes 3932168 | tf_op jit(solution)/shard_map/ppermute | solution.py:599
  836.3 27.2 %collective-permute-start.69 = (bf16[256,2560]{1,0:T(8,128)(2,1)}, bf16[256,2560]{1,0:T(8,128)(2,1)}, u32[]{:S(2)}, u32[]{:S(2)}) collective-permute-start(bf16[256,2560]{1,0:T(8,128)(2,1)} %collective-permute-done.65), channel_id=1, source_target_pairs={{1,0},{2,1},{5,4},{6,5},{9,8},{10,9},{13,12},{14,13},{17,16},{18,1... | collective-permute-start | bytes 3932168 | tf_op jit(solution)/shard_map/ppermute | solution.py:600
  863.5 28.0 %collective-permute-start.70 = (bf16[256,2560]{1,0:T(8,128)(2,1)}, bf16[256,2560]{1,0:T(8,128)(2,1)}, u32[]{:S(2)}, u32[]{:S(2)}) collective-permute-start(bf16[256,2560]{1,0:T(8,128)(2,1)} %collective-permute-done.68), channel_id=1, source_target_pairs={{2,3},{6,7},{10,11},{14,15},{18,19},{22,23},{26,27},{30,31}} | collective-permute-start | bytes 3932168 | tf_op jit(solution)/shard_map/ppermute | solution.py:599
  865.2 26.3 %collective-permute-start.71 = (bf16[256,2560]{1,0:T(8,128)(2,1)}, bf16[256,2560]{1,0:T(8,128)(2,1)}, u32[]{:S(2)}, u32[]{:S(2)}) collective-permute-start(bf16[256,2560]{1,0:T(8,128)(2,1)} %collective-permute-done.69), channel_id=1, source_target_pairs={{1,0},{5,4},{9,8},{13,12},{17,16},{21,20},{25,24},{29,28}} | collective-permute-start | bytes 3932168 | tf_op jit(solution)/shard_map/ppermute | solution.py:600
  (107 other events, 1420.2 us)
Sparse Core Ops, SparseCore 0:
  13.6 157.5 all-gather.2
  173.6 74.4 all-gather.4
  346.3 49.6 reduce-scatter.5
  402.2 65.3 reduce-scatter.7
  495.2 160.0 reduce-scatter.9
  744.8 62.7 reduce-scatter.11
  900.7 39.6 reduce-scatter.13
where the time goes:
time: 960 us; the launch traced here: 951 us
  waiting for transfers between devices  286 us (30%)
  Pallas kernels  264 us (28%)
  other arithmetic  162 us (17%)
  starting transfers between devices  128 us (13%)
  local copies, waits for them, and re-layouts  48.5 us (5%)
  matrix products  45.2 us (5%)
  between operations  17 us (2%)
    ppermute x24, waiting for transfers between devices, advance(): self.above.append(lax.ppermute(down, 'mp', downs))  170 us
    ppermute x12, waiting for transfers between devices, advance(): came.append(lax.ppermute(part, 'dp', pairs))  52 us
    pallas_call x4, Pallas kernels, ffn_back(): pl.pallas_call(functools.partial(back_kernel, count), grid=(2, tokens //...  51.2 us
    ppermute x24, starting transfers between devices, advance(): self.below.append(lax.ppermute(up, 'mp', ups))  46.1 us
    pallas_call x3, Pallas kernels, ffn_outer(): pl.pallas_call(functools.partial(outer_kernel, count), grid=(2,), in_spec...  44.4 us
    pallas_call x2, Pallas kernels, ffn_inner(): pl.pallas_call(inner_kernel, grid=(steps, 2, 2), in_specs=[pl.BlockSpec((...  39.2 us
    dot_general x6, matrix products, contract(): return jnp.einsum(spec, left, right, preferred_element_type=jnp.float32)  39.2 us
    pallas_call x2, Pallas kernels, attend_backward(): pl.pallas_call(functools.partial(backward_kernel, half * size // BLK, hal...  36.3 us
  transfers between devices with their start and end apart: 79, of which 27 were waited for; matrix products, arithmetic and copies ran while one was open for 23% of the time, Pallas kernels for 24%

commit v1 on v0

--- a/solution.py
+++ b/solution.py
@@ -368,33 +368,41 @@
 
 
 def outer_kernel(count, *refs):
-    out_ref = refs[-1]
+    out_ref, mark_ref = refs[-2:]
     total = dot_tn(refs[0][...], refs[count][...])
     for number in range(1, count):
         total = total + dot_tn(refs[number][...], refs[count + number][...])
     out_ref[...] = total.astype(jnp.bfloat16).reshape(out_ref.shape)
+    mark_ref[...] = jnp.zeros(mark_ref.shape, jnp.float32)
 
 
 def ffn_outer(lefts, places, rights, blocks, slot, held):
     tokens, units = rights[0].shape
     model = lefts[0].shape[1]
     rows = model // blocks
-    extra = [] if held is None else [held]
     count = len(lefts)
     left_spec = lambda place: pl.BlockSpec((tokens, model // 2), lambda k: (place, k))
+    mark_spec = pl.BlockSpec((8, 128), lambda k: (0, 0))
+    held_specs = [] if held is None else [pl.BlockSpec(memory_space=pl.ANY), mark_spec]
     return pl.pallas_call(
         functools.partial(outer_kernel, count),
         grid=(2,),
         in_specs=[left_spec(place) for place in places]
         + [pl.BlockSpec((tokens, units), lambda k: (0, 0)) for unused in rights]
-        + [pl.BlockSpec(memory_space=pl.ANY) for unused in extra],
-        out_specs=pl.BlockSpec((blocks // 2, 1, rows, units), lambda k: (k, slot, 0, 0)),
-        out_shape=jax.ShapeDtypeStruct((blocks, 3, rows, units), jnp.bfloat16),
+        + held_specs,
+        out_specs=[
+            pl.BlockSpec((blocks // 2, 1, rows, units), lambda k: (k, slot, 0, 0)),
+            mark_spec,
+        ],
+        out_shape=[
+            jax.ShapeDtypeStruct((blocks, 3, rows, units), jnp.bfloat16),
+            jax.ShapeDtypeStruct((8, 128), jnp.float32),
+        ],
         input_output_aliases={} if held is None else {2 * count: 0},
         compiler_params=kernel_params(),
         cost_estimate=light(4 * count * tokens * model * units),
         name="ffn_outer",
-    )(*lefts, *rights, *extra)
+    )(*lefts, *rights, *(held or ()))
 
 
 def down_kernel(normed_ref, grad_ref, weight_ref, gain_ref, out_ref, part_ref):
@@ -471,18 +479,28 @@
         out_ref[rows, :QR] = dot_nt(grad_q[...].T, query_up[...]).astype(jnp.bfloat16)
         out_ref[rows, QR : QR + KVR] = dot_nt(grad_kv[...].T, latent_up[...]).astype(jnp.bfloat16)
         out_ref[rows, QR + KVR :] = rope[...].T.astype(jnp.bfloat16)
-
-
-def latent_back(grads_q, grads_kv, ropes, query_up, latent_up):
+    mid_part = refs[3 * count + 2][...] + refs[3 * count + 3][...]
+    lane = QR + KVR
+    lines = []
+    for start in range(0, D, lane):
+        line = mid_part[:, start : start + lane]
+        lines.append(jnp.pad(line, ((0, 0), (0, lane - line.shape[1]))))
+    extra = out_ref.shape[0] - count * size
+    lines.append(jnp.zeros((extra - len(lines), lane), jnp.float32))
+    out_ref[count * size :, :lane] = jnp.concatenate(lines, axis=0).astype(jnp.bfloat16)
+    out_ref[count * size :, lane:] = jnp.zeros((extra, RD), jnp.bfloat16)
+
+
+def latent_back(grads_q, grads_kv, ropes, query_up, latent_up, mid_parts, extra):
     count = len(grads_q)
     tokens = count * grads_q[0].shape[1]
     return pl.pallas_call(
         functools.partial(latent_kernel, count),
-        out_shape=jax.ShapeDtypeStruct((tokens, QR + KVR + RD), jnp.bfloat16),
+        out_shape=jax.ShapeDtypeStruct((tokens + extra, QR + KVR + RD), jnp.bfloat16),
         compiler_params=kernel_params(),
         cost_estimate=light(tokens * (QR + KVR) * 4000),
         name="latent_back",
-    )(*grads_q, *grads_kv, *ropes, query_up, latent_up)
+    )(*grads_q, *grads_kv, *ropes, query_up, latent_up, *mid_parts)
 
 
 def heads_kernel(count, *refs):
@@ -520,7 +538,7 @@
     )
 
 
-def heads_outer(grads_attn, mixed, grads_q, grads_kv, q_normed, kv_normed, blocks):
+def heads_outer(grads_attn, mixed, grads_q, grads_kv, q_normed, kv_normed, blocks, mark):
     count = len(mixed)
     size = grads_attn[0].shape[0]
     wide_cols = grads_kv[0].shape[0]
@@ -534,13 +552,237 @@
         + [
             pl.BlockSpec((q_normed.shape[0], QR // 2), lambda k: (0, k)),
             pl.BlockSpec((kv_normed.shape[0], KVR // 2), lambda k: (0, k)),
+            pl.BlockSpec((8, 128), lambda k: (0, 0)),
         ],
         out_specs=pl.BlockSpec((blocks // 2, rows, wide_cols), lambda k: (k, 0, 0)),
         out_shape=jax.ShapeDtypeStruct((blocks, rows, wide_cols), jnp.bfloat16),
         compiler_params=kernel_params(),
         cost_estimate=light(count * size * D * wide_cols * 2),
         name="heads_outer",
-    )(*grads_attn, *mixed, *grads_q, *grads_kv, q_normed, kv_normed)
+    )(*grads_attn, *mixed, *grads_q, *grads_kv, q_normed, kv_normed, mark)
+
+
+def scaled_rate(value):
+    return lax.rsqrt(jnp.mean(value * value, axis=1, keepdims=True) + NORM_EPS)
+
+
+def norm_pull(value, gain_vec, gradient):
+    rate = scaled_rate(value)
+    scaled = gradient * gain_vec
+    dotted = jnp.mean(scaled * value, axis=1, keepdims=True)
+    pulled = rate * (scaled - value * (rate * rate * dotted))
+    return pulled, jnp.sum(gradient * value * rate, axis=0, keepdims=True)
+
+
+def latents_kernel(
+    inputs_ref, gain_in, down_ref, gain_query, gain_latent, cos_ref, sin_ref,
+    normed_ref, latents_ref, q_ref, kv_ref, rope_ref,
+):
+    value = inputs_ref[...].astype(jnp.float32)
+    normed = (value * scaled_rate(value) * gain_in[...]).astype(jnp.bfloat16)
+    normed_ref[...] = normed
+    latents = dot_nn(normed, down_ref[...])
+    latents_ref[...] = latents
+    q_latent = latents[:, :QR]
+    kv_latent = latents[:, QR : QR + KVR]
+    q_ref[...] = (q_latent * scaled_rate(q_latent) * gain_query[...]).astype(jnp.bfloat16)
+    kv_ref[...] = (kv_latent * scaled_rate(kv_latent) * gain_latent[...]).astype(jnp.bfloat16)
+    rope = latents[:, QR + KVR :].T
+    low, high = rope[: RD // 2], rope[RD // 2 :]
+    cos_blk, sin_blk = cos_ref[...], sin_ref[...]
+    rope_ref[: RD // 2, :] = (low * cos_blk - high * sin_blk).astype(jnp.bfloat16)
+    rope_ref[RD // 2 :, :] = (high * cos_blk + low * sin_blk).astype(jnp.bfloat16)
+
+
+def latents_forward(inputs, gain_in, down_all, gain_query, gain_latent, cosines, sines):
+    tokens, model = inputs.shape
+    width = down_all.shape[1]
+    row_spec = lambda cols: pl.BlockSpec((BLK, cols), lambda i: (i, 0))
+    column_spec = lambda rows: pl.BlockSpec((rows, BLK), lambda i: (0, i))
+    whole = lambda value: pl.BlockSpec(value.shape, lambda i: (0, 0))
+    return pl.pallas_call(
+        latents_kernel,
+        grid=(tokens // BLK,),
+        in_specs=[row_spec(model), whole(gain_in), whole(down_all), whole(gain_query), whole(gain_latent)]
+        + [column_spec(RD // 2), column_spec(RD // 2)],
+        out_specs=[row_spec(model), row_spec(width), row_spec(QR), row_spec(KVR), column_spec(RD)],
+        out_shape=[
+            jax.ShapeDtypeStruct((tokens, model), jnp.bfloat16),
+            jax.ShapeDtypeStruct((tokens, width), jnp.float32),
+            jax.ShapeDtypeStruct((tokens, QR), jnp.bfloat16),
+            jax.ShapeDtypeStruct((tokens, KVR), jnp.bfloat16),
+            jax.ShapeDtypeStruct((RD, tokens), jnp.bfloat16),
+        ],
+        compiler_params=kernel_params(),
+        cost_estimate=light(tokens * model * width),
+        name="latents_forward",
+    )(inputs, gain_in, down_all, gain_query, gain_latent, cosines, sines)
+
+
+def split_kernel(q_ref, kv_ref, rope_ref, query_up, latent_up, cos_ref, sin_ref, queries, keys, values):
+    heads = queries.shape[0]
+    half = RD // 2
+    grown = dot_nt(query_up[...], q_ref[...]).reshape(heads, HD + RD, -1)
+    low, high = grown[:, HD : HD + half], grown[:, HD + half :]
+    cos_blk, sin_blk = cos_ref[...][None], sin_ref[...][None]
+    queries[:, :HD] = grown[:, :HD].astype(jnp.bfloat16)
+    queries[:, HD : HD + half] = (low * cos_blk - high * sin_blk).astype(jnp.bfloat16)
+    queries[:, HD + half :] = (high * cos_blk + low * sin_blk).astype(jnp.bfloat16)
+    grown = dot_nt(latent_up[...], kv_ref[...]).astype(jnp.bfloat16).reshape(heads, 2 * HD, -1)
+    keys[:, :HD] = grown[:, :HD]
+    keys[:, HD:] = jnp.broadcast_to(rope_ref[...][None], (heads, RD, rope_ref.shape[1]))
+    values[...] = grown[:, HD:]
+
+
+def heads_forward(q_normed, kv_normed, key_rope, query_up, latent_up, cosines, sines):
+    tokens = q_normed.shape[0]
+    heads = query_up.shape[0] // (HD + RD)
+    row_spec = lambda cols: pl.BlockSpec((BLK, cols), lambda i: (i, 0))
+    column_spec = lambda rows: pl.BlockSpec((rows, BLK), lambda i: (0, i))
+    head_spec = lambda rows: pl.BlockSpec((heads, rows, BLK), lambda i: (0, 0, i))
+    whole = lambda value: pl.BlockSpec(value.shape, lambda i: (0, 0))
+    return pl.pallas_call(
+        split_kernel,
+        grid=(tokens // BLK,),
+        in_specs=[
+            row_spec(QR),
+            row_spec(KVR),
+            column_spec(RD),
+            whole(query_up),
+            whole(latent_up),
+            column_spec(RD // 2),
+            column_spec(RD // 2),
+        ],
+        out_specs=[head_spec(HD + RD), head_spec(HD + RD), head_spec(HD)],
+        out_shape=[
+            jax.ShapeDtypeStruct((heads, HD + RD, tokens), jnp.bfloat16),
+            jax.ShapeDtypeStruct((heads, HD + RD, tokens), jnp.bfloat16),
+            jax.ShapeDtypeStruct((heads, HD, tokens), jnp.bfloat16),
+        ],
+        compiler_params=kernel_params(),
+        cost_estimate=light(tokens * QR),
+        name="heads_forward",
+    )(q_normed, kv_normed, key_rope, query_up, latent_up, cosines, sines)
+
+
+def middle_kernel(place_ref, grad_ref, resid_ref, gain_ref, out_ref, part_ref):
+    pulled, part = norm_pull(resid_ref[...], gain_ref[...], grad_ref[...].astype(jnp.float32))
+    out_ref[...] = pulled.astype(jnp.bfloat16)
+    part_ref[...] = part
+
+
+def middle_back(place, grads, resid, gain_mid):
+    rows, model = grads.shape
+    fixed = lambda size: pl.BlockSpec((size, model), lambda i, place_ref: (0, 0))
+    return pl.pallas_call(
+        middle_kernel,
+        grid_spec=pltpu.PrefetchScalarGridSpec(
+            num_scalar_prefetch=1,
+            grid=(1,),
+            in_specs=[
+                fixed(rows),
+                pl.BlockSpec((rows, model), lambda i, place_ref: (place_ref[0], 0)),
+                fixed(1),
+            ],
+            out_specs=[fixed(rows), fixed(1)],
+        ),
+        out_shape=[
+            jax.ShapeDtypeStruct((rows, model), jnp.bfloat16),
+            jax.ShapeDtypeStruct((1, model), jnp.float32),
+        ],
+        compiler_params=kernel_params(),
+        cost_estimate=light(rows * model),
+        name="middle_back",
+    )(place, grads, resid, gain_mid)
+
+
+def turned_kernel(
+    total_ref, latents_ref, cos_ref, sin_ref, gain_query, gain_latent, out_ref, query_ref, latent_ref
+):
+    half = RD // 2
+    total = total_ref[...].astype(jnp.float32)
+    latents = latents_ref[...]
+    q_pulled, q_part = norm_pull(latents[:, :QR], gain_query[...], total[:, :QR])
+    kv_pulled, kv_part = norm_pull(
+        latents[:, QR : QR + KVR], gain_latent[...], total[:, QR : QR + KVR]
+    )
+    low = total[:, QR + KVR : QR + KVR + half]
+    high = total[:, QR + KVR + half :]
+    cos_blk = cos_ref[...].T
+    sin_blk = sin_ref[...].T
+    out_ref[:, :QR] = q_pulled.astype(jnp.bfloat16)
+    out_ref[:, QR : QR + KVR] = kv_pulled.astype(jnp.bfloat16)
+    out_ref[:, QR + KVR : QR + KVR + half] = (low * cos_blk + high * sin_blk).astype(jnp.bfloat16)
+    out_ref[:, QR + KVR + half :] = (high * cos_blk - low * sin_blk).astype(jnp.bfloat16)
+
+    @pl.when(pl.program_id(0) == 0)
+    def _():
+        query_ref[...] = q_part
+        latent_ref[...] = kv_part
+
+    @pl.when(pl.program_id(0) != 0)
+    def _():
+        query_ref[...] += q_part
+        latent_ref[...] += kv_part
+
+
+def latents_turned(total, latents, cosines, sines, gain_query, gain_latent):
+    tokens, width = latents.shape
+    row_spec = lambda cols: pl.BlockSpec((BLK, cols), lambda i: (i, 0))
+    column_spec = pl.BlockSpec((RD // 2, BLK), lambda i: (0, i))
+    whole = lambda cols: pl.BlockSpec((1, cols), lambda i: (0, 0))
+    return pl.pallas_call(
+        turned_kernel,
+        grid=(tokens // BLK,),
+        in_specs=[
+            row_spec(width),
+            row_spec(width),
+            column_spec,
+            column_spec,
+            whole(QR),
+            whole(KVR),
+        ],
+        out_specs=[row_spec(width), whole(QR), whole(KVR)],
+        out_shape=[
+            jax.ShapeDtypeStruct((tokens, width), jnp.bfloat16),
+            jax.ShapeDtypeStruct((1, QR), jnp.float32),
+            jax.ShapeDtypeStruct((1, KVR), jnp.float32),
+        ],
+        compiler_params=kernel_params(),
+        cost_estimate=light(tokens * width),
+        name="latents_turned",
+    )(total, latents, cosines, sines, gain_query, gain_latent)
+
+
+def mixed_kernel(mid_ref, cot_ref, weight_ref, attn_ref, mixed_ref):
+    grad_mid = cot_ref[...].astype(jnp.float32) + mid_ref[...].astype(jnp.float32)
+    grad_attn = (RESID_SCALE * grad_mid).astype(jnp.bfloat16)
+    attn_ref[...] = grad_attn
+    mixed_ref[...] = dot_nt(weight_ref[...], grad_attn).astype(jnp.bfloat16)
+
+
+def mixed_gradient(mid_norm, cotangent, out_own, half):
+    tokens, model = mid_norm.shape
+    heads_width = out_own.shape[0]
+    steps = tokens // BLK
+    row_spec = pl.BlockSpec((BLK, model), lambda i: (i, 0))
+    return pl.pallas_call(
+        mixed_kernel,
+        grid=(steps,),
+        in_specs=[
+            row_spec,
+            pl.BlockSpec((BLK, model), lambda i: (i + half * steps, 0)),
+            pl.BlockSpec(out_own.shape, lambda i: (0, 0)),
+        ],
+        out_specs=[row_spec, pl.BlockSpec((heads_width, BLK), lambda i: (0, i))],
+        out_shape=[
+            jax.ShapeDtypeStruct((tokens, model), jnp.bfloat16),
+            jax.ShapeDtypeStruct((heads_width, tokens), jnp.bfloat16),
+        ],
+        compiler_params=kernel_params(),
+        cost_estimate=light(tokens * model),
+        name="mixed_gradient",
+    )(mid_norm, cotangent, out_own)
 
 
 def update_rates():
@@ -614,6 +856,33 @@
                     block = jnp.where(place + step == slot, self.above[step], block)
             blocks.append(block)
         return jnp.concatenate(blocks, axis=self.axis)
+
+
+class Direct:
+    def __init__(self, own, count):
+        self.own, self.count, self.came = own, count, None
+
+    def advance(self, gate):
+        if self.came is not None:
+            return []
+        (sent,) = gate(self.own)
+        count = self.count
+        self.came = [
+            lax.ppermute(sent, "mp", [(k, (k + step) % count) for k in range(count)])
+            for step in range(1, count)
+        ]
+        return self.came
+
+    def result(self):
+        self.advance(tie)
+        place = lax.axis_index("mp")
+        blocks = []
+        for slot in range(self.count):
+            block = self.own
+            for step in range(1, self.count):
+                block = jnp.where((place - step) % self.count == slot, self.came[step - 1], block)
+            blocks.append(block)
+        return jnp.concatenate(blocks, axis=0)
 
 
 class Scatter:
@@ -639,9 +908,13 @@
         self.above = lax.ppermute(down, "mp", downs)
         return [self.below, self.above]
 
-    def result(self):
+    def arrived(self):
         while self.advance(tie):
             pass
+        return self.below, self.above
+
+    def result(self):
+        self.arrived()
         own = chunk_of(self.stacked, lax.axis_index("mp"))
         return wide(own) + wide(self.below) + wide(self.above)
 
@@ -682,6 +955,32 @@
         return jnp.concatenate(blocks, axis=0)
 
 
+class PlaneScatter:
+    def __init__(self, stacked, count):
+        self.bits = count.bit_length() - 1
+        self.left = stacked.reshape((2,) * self.bits + stacked.shape[1:])
+        self.step = 0
+
+    def advance(self, gate):
+        if self.step == self.bits:
+            return []
+        bit = 1 << self.step
+        axis = self.bits - 1 - self.step
+        mine = jnp.where(jnp.bitwise_and(lax.axis_index("dp"), bit) != 0, 1, 0)
+        kept = lax.dynamic_index_in_dim(self.left, mine, axis, keepdims=False)
+        (gone,) = gate(lax.dynamic_index_in_dim(self.left, 1 - mine, axis, keepdims=False))
+        pairs = [(k, k ^ bit) for k in range(1 << self.bits)]
+        came = lax.ppermute(gone, "dp", pairs)
+        self.left = (wide(kept) + wide(came)).astype(kept.dtype)
+        self.step += 1
+        return [came]
+
+    def result(self):
+        while self.advance(tie):
+            pass
+        return self.left
+
+
 class Clock:
     def __init__(self):
         self.past, self.present = (), []
@@ -700,15 +999,6 @@
         if self.present or values:
             self.past = (*self.present, *values)
             self.present = []
-
-
-def sum_rows(stacked):
-    flat = stacked.reshape(-1, stacked.shape[-1])
-    return wide(lax.psum_scatter(flat, "dp", scatter_dimension=0, tiled=True))
-
-
-def turn(low, high, cosines, sines, direction):
-    return (low * cosines - direction * high * sines, high * cosines + direction * low * sines)
 
 
 def local(
@@ -750,6 +1040,7 @@
     heads_dev = query_up.shape[1] // (HD + RD)
     half_tokens = tokens_dev // 2
     own_tokens = half_tokens // n_model
+    spread = tokens_dev // n_model
     hidden_dev = ffn_gate.shape[1]
     out_width = heads_dev * HD
     down_rows = query_down.shape[0]
@@ -780,12 +1071,11 @@
     )
     down_own = jnp.concatenate([query_down, latent_down], axis=1).astype(low_type)
     up_flow = Plane(up_pack, n_data)
-    down_flow = Gather(down_own, n_model, 0)
+    down_flow = Direct(down_own, n_model)
     out_flow = Gather(out_proj.T.astype(low_type), n_model, 1)
     clock = Clock()
-    for unused in range(3):
-        clock.move(down_flow)
-        clock.tick()
+    clock.move(down_flow)
+    clock.tick()
     down_flow = Plane(down_flow.result(), n_data)
     for unused in range(3):
         clock.move(down_flow, up_flow, out_flow)
@@ -793,7 +1083,7 @@
     up_all = up_flow.result().reshape(n_data, -1, up_width)
     down_all = down_flow.result()
     out_all = lax.all_gather(out_flow.result(), "dp", axis=0, tiled=True)
-    out_own = lax.dynamic_slice_in_dim(out_all, place * out_width, out_width, 1)
+    out_own = lax.dynamic_slice_in_dim(out_all, place * out_width, out_width, 1).T
     ffn_pack = jnp.stack([ffn_gate, ffn_up, ffn_down.T]).astype(low_type)
     ffn_all = lax.all_gather(ffn_pack, "dp", axis=0, tiled=False)
     query_up_all = up_all[:, :up_rows, : query_up.shape[1]].reshape(QR, query_up.shape[1])
@@ -805,36 +1095,20 @@
     gain_latent = gains_all[D + QR : D + QR + KVR]
     gain_mid = gains_all[D + QR + KVR :]
     cosines, sines = tables(LEN)
-    cos_tok = cosines
-    sin_tok = sines
     cosines = cosines.T
     sines = sines.T
 
-    inputs_wide = wide(inputs)
-    cot_wide = wide(cotangent)
-    normed_in = normalize(inputs_wide, gain_in).astype(low_type)
-    latents = product(normed_in, down_all)
-    q_latent = latents[:, :QR]
-    kv_latent = latents[:, QR : QR + KVR]
-    q_normed = normalize(q_latent, gain_query).astype(low_type)
-    kv_normed = normalize(kv_latent, gain_latent).astype(low_type)
-    q_heads = contract("rc,tr->ct", query_up_all, q_normed).reshape(heads_dev, HD + RD, tokens_dev)
-    turned = turn(q_heads[:, HD : HD + RD // 2], q_heads[:, HD + RD // 2 :], cosines, sines, 1.0)
-    queries = jnp.concatenate([q_heads[:, :HD], turned[0], turned[1]], axis=1).astype(low_type)
-    kv_heads = contract("rc,tr->ct", latent_up_all, kv_normed).astype(low_type)
-    kv_heads = kv_heads.reshape(heads_dev, 2 * HD, tokens_dev)
-    rope_in = latents[:, QR + KVR :].T
-    turned = turn(rope_in[: RD // 2], rope_in[RD // 2 :], cosines, sines, 1.0)
-    key_rope = jnp.concatenate(turned, axis=0).astype(low_type)
-    keys = jnp.concatenate(
-        [kv_heads[:, :HD], jnp.broadcast_to(key_rope[None], (heads_dev, RD, tokens_dev))], axis=1
-    )
-    values = kv_heads[:, HD:]
+    normed_in, latents, q_normed, kv_normed, key_rope = latents_forward(
+        inputs, gain_in[None], down_all, gain_query[None], gain_latent[None], cosines, sines
+    )
+    queries, keys, values = heads_forward(
+        q_normed, kv_normed, key_rope, query_up_all.T, latent_up_all.T, cosines, sines
+    )
     mixed = {}
     log_sums = {}
     resid_mid = {}
     normed_mid = {}
-    grad_ffn = (RESID_SCALE * cot_wide).astype(low_type)
+    grad_ffn = (RESID_SCALE * wide(cotangent)).astype(low_type)
     mixed_flow = {}
     for half in order:
         asked = queries if half == 1 else clock.wait(queries)
@@ -843,17 +1117,16 @@
         mixed_flow[half] = Gather(mixed[half], n_model, 0)
         clock.tick(mixed[half])
         clock.move(mixed_flow[1])
-    clock.move(mixed_flow[0])
-    clock.tick()
-    clock.move(mixed_flow[1], mixed_flow[0])
     grad_hidden = hidden_back(clock.wait(grad_ffn), ffn_all)
     clock.tick(grad_hidden)
+    clock.move(mixed_flow[1])
+    clock.tick()
     clock.move(mixed_flow[0])
 
     def middle(half):
         mixed_all = clock.wait(mixed_flow[half].result())
         attn_out = contract("ht,dh->td", mixed_all, out_all)
-        resid_mid[half] = half_of(inputs_wide, half) + RESID_SCALE * attn_out
+        resid_mid[half] = wide(half_of(inputs, half)) + RESID_SCALE * attn_out
         normed_mid[half] = normalize(resid_mid[half], gain_mid).astype(low_type)
         clock.tick(normed_mid[half])
 
@@ -864,14 +1137,16 @@
     mid_own = {}
     for half in order:
         middle(half)
+        clock.move(mixed_flow[0])
         hidden[half], grad_gate[half], grad_up[half] = ffn_inner(
             clock.wait(normed_mid[half]), grad_hidden, ffn_all, half
         )
         clock.tick(grad_up[half])
+        clock.move(mixed_flow[0])
         part_mid[half] = ffn_back([clock.wait(grad_gate[half]), grad_up[half]], ffn_all, 0)
         clock.tick(part_mid[half])
         sent_mid = part_mid[half] if half == 1 else after(part_mid[half], mid_own[1])
-        mid_own[half] = wide(lax.psum_scatter(sent_mid, "mp", scatter_dimension=0, tiled=True))
+        mid_own[half] = lax.psum_scatter(sent_mid, "mp", scatter_dimension=0, tiled=True)
     pairs = lambda values: [values[half] for half in order]
     both = lambda values: [values[half] for half in (0, 1)]
     mid_norm = {}
@@ -881,36 +1156,35 @@
     grad_mixed = {}
 
     def mid_back(half):
-        own, gain_mid_part[half] = norm_back(own_rows(resid_mid[half]), gain_mid, mid_own[half])
-        mid_flow[half] = Gather(own.astype(low_type), n_model, 0)
+        own, gain_mid_part[half] = middle_back(
+            place[None], mid_own[half], resid_mid[half], gain_mid[None]
+        )
+        mid_flow[half] = Gather(own, n_model, 0)
 
     def mixed_back(half):
-        mid_norm[half] = clock.wait(mid_flow[half].result())
-        grad_mid = half_of(cot_wide, half) + wide(mid_norm[half])
-        grad_attn[half] = (RESID_SCALE * grad_mid).astype(low_type)
-        grad_mixed[half] = contract("td,dh->ht", grad_attn[half], out_own).astype(low_type)
+        mid_norm[half] = mid_flow[half].result()
+        grad_attn[half], grad_mixed[half] = mixed_gradient(
+            clock.wait(mid_norm[half]), cotangent, out_own, half
+        )
 
     mid_back(1)
     clock.move(mid_flow[1])
     grad_gate[1] = clock.wait(grad_gate[1])
-    ffn_grads = ffn_outer(pairs(normed_mid), (0, 0), pairs(grad_gate), n_data, 0, None)
-    clock.tick(ffn_grads[0, 0, :16, :128])
+    held = ffn_outer(pairs(normed_mid), (0, 0), pairs(grad_gate), n_data, 0, None)
+    held = ffn_outer(pairs(normed_mid), (0, 0), pairs(grad_up), n_data, 1, held)
+    ffn_grads, mark = ffn_outer([grad_ffn, grad_ffn], order, pairs(hidden), n_data, 2, held)
+    clock.tick(mark)
     clock.move(mid_flow[1])
-    grad_up[1] = clock.wait(grad_up[1])
-    ffn_grads = ffn_outer(pairs(normed_mid), (0, 0), pairs(grad_up), n_data, 1, ffn_grads)
-    clock.tick(ffn_grads[0, 1, :16, :128])
+    ffn_term = {}
+    ffn_term[1] = ffn_back([clock.wait(hidden[1])], ffn_all, 2)
+    clock.tick(ffn_term[1])
     clock.move(mid_flow[1])
-    hidden_late = clock.wait(hidden[1])
-    ffn_grads = ffn_outer([grad_ffn, grad_ffn], order, [hidden_late, hidden[0]], n_data, 2, ffn_grads)
-    clock.tick(ffn_grads[0, 2, :16, :128])
+    ffn_term[0] = ffn_back([clock.wait(hidden[0])], ffn_all, 2)
     mid_own[0] = clock.wait(mid_own[0])
+    mid_back(0)
+    clock.tick(ffn_term[0], mid_flow[0].own)
     ffn_grads = after(ffn_grads, mid_own[0])
-    ffn_sum = sum_rows(ffn_grads).reshape(3, -1, hidden_dev)
-    mid_back(0)
-    clock.move(mid_flow[0])
-    ffn_term = [ffn_back([clock.wait(hidden[half])], ffn_all, 2) for half in (0, 1)]
-    ffn_term = jnp.concatenate(ffn_term, axis=0)
-    clock.tick(ffn_term)
+    ffn_sum = lax.psum_scatter(ffn_grads.reshape(-1, hidden_dev), "dp", scatter_dimension=0, tiled=True)
     resid_all = jnp.concatenate([resid_mid[0], resid_mid[1]], axis=0)
 
     seeds = ()
@@ -935,22 +1209,38 @@
         grad_rope[half] = back[2]
         return back[3:]
 
-    out_flow = Scatter(ffn_term, n_model)
-    clock.move(mid_flow[0], out_flow)
+    clock.move(mid_flow[0])
     mixed_back(1)
     seeds = heads_back(1)
     clock.tick(grad_rope[1])
-    clock.move(mid_flow[0])
+    out_flow = Scatter(jnp.concatenate(both(ffn_term), axis=0), n_model)
+    clock.move(mid_flow[0], out_flow)
+    clock.tick()
+    clock.move(mid_flow[0], out_flow)
     clock.tick()
     clock.move(out_flow)
     mixed_back(0)
     seeds = heads_back(0)
     part_latents = latent_back(
-        both(grad_q_heads), both(grad_kv_heads), both(grad_rope), query_up_all, latent_up_all
+        both(grad_q_heads),
+        both(grad_kv_heads),
+        both(grad_rope),
+        query_up_all,
+        latent_up_all,
+        both(gain_mid_part),
+        gain_rows,
     )
     clock.tick(part_latents)
-    lat_flow = Scatter(part_latents, n_model)
-    clock.move(lat_flow, out_flow)
+    latents_sum = lax.psum(after(part_latents, ffn_sum), "mp")
+    ffn_own = out_flow.result()
+
+    def wide_rows(value):
+        return lax.dynamic_slice_in_dim(value, place * spread, spread, 0)
+
+    output_own = (wide_rows(resid_all) + RESID_SCALE * ffn_own).astype(low_type)
+    output_flow = Gather(output_own, n_model, 0)
+    output_flow.advance(clock.gate)
+    output_flow.advance(tie)
     head_grads = heads_outer(
         both(grad_attn),
         both(mixed),
@@ -959,72 +1249,40 @@
         clock.wait(q_normed),
         kv_normed,
         n_data,
-    )
-    clock.tick(head_grads[0, :16, :128])
-    clock.move(lat_flow)
-    clock.tick()
-    clock.move(lat_flow)
-    rows = lat_flow.result()
-    ffn_own = out_flow.result()
-    clock.tick()
-
-    spread = 2 * own_tokens
-
-    def wide_rows(value):
-        return lax.dynamic_slice_in_dim(value, place * spread, spread, 0)
-
-    grad_q_own, gain_query_part = norm_back(wide_rows(q_latent), gain_query, rows[:, :QR])
-    grad_kv_own, gain_latent_part = norm_back(
-        wide_rows(kv_latent), gain_latent, rows[:, QR : QR + KVR]
-    )
-    turned = turn(
-        rows[:, QR + KVR : QR + KVR + RD // 2],
-        rows[:, QR + KVR + RD // 2 :],
-        wide_rows(cos_tok),
-        wide_rows(sin_tok),
-        -1.0,
-    )
-    gain_parts = jnp.concatenate(
-        [gain_query_part, gain_latent_part, gain_mid_part[0] + gain_mid_part[1]]
-    )
-    gain_parts = jnp.pad(gain_parts, (0, gain_rows * width - gain_parts.shape[0]))
-    sent_own = jnp.concatenate(
-        [
-            jnp.concatenate([grad_q_own, grad_kv_own, turned[0], turned[1]], axis=1),
-            gain_parts.reshape(gain_rows, width),
-        ],
-        axis=0,
-    ).astype(low_type)
-    sent_flow = Gather(sent_own, n_model, 0)
-    clock.move(sent_flow)
-    clock.tick()
-    clock.move(sent_flow)
-    clock.tick()
-    output_own = (wide_rows(resid_all) + RESID_SCALE * ffn_own).astype(low_type)
-    output_flow = Gather(output_own, n_model, 0)
-    clock.move(sent_flow, output_flow)
-    sent = sent_flow.result().reshape(n_model, spread + gain_rows, width)
-    head_grads, ffn_sum = tie(head_grads, ffn_sum)
-    head_sum = sum_rows(head_grads)
+        mark,
+    )
+    head_sum = lax.psum_scatter(
+        after(head_grads, latents_sum).reshape(-1, up_width), "dp", scatter_dimension=0, tiled=True
+    )
     out_rows = D // n_data // 2
-    clock.tick()
-    clock.move(output_flow)
-    grad_latents = sent[:, :spread].reshape(tokens_dev, width)
-    gain_rest = jnp.sum(wide(sent[:, spread:]), axis=0).reshape(-1)[: QR + KVR + D]
-
-    grad_down, gain_in_part = down_outer(clock.wait(normed_in), grad_latents, down_all, gain_in[:, None])
+    grad_latents, gain_query_sum, gain_latent_sum = latents_turned(
+        latents_sum, latents, cosines, sines, gain_query[None], gain_latent[None]
+    )
+
+    def later(*values):
+        return lax.optimization_barrier((*values, grad_latents))[: len(values)]
+
+    while output_flow.advance(later):
+        pass
+    output = output_flow.result()
+    gain_rest = jnp.concatenate(
+        [gain_query_sum[0], gain_latent_sum[0], wide(latents_sum[tokens_dev:, : QR + KVR]).reshape(-1)[:D]]
+    )
+
+    grad_down, gain_in_part = down_outer(normed_in, grad_latents, down_all, gain_in[:, None])
     gain_grad = jnp.concatenate([gain_in_part[:, 0], gain_rest]).reshape(n_data, 1, -1)
     gain_count = gain_grad.shape[2]
     gain_grad = jnp.pad(gain_grad, ((0, 0), (0, gain_rows - 1), (0, width - gain_count)))
     down_mine = lax.dynamic_index_in_dim(
         grad_down.reshape(n_data, n_model, down_rows, width), place, axis=1, keepdims=False
     )
-    down_sent = jnp.concatenate([down_mine, gain_grad.astype(low_type)], axis=1)
-    down_sent, head_sum = tie(down_sent, head_sum)
-    down_sum = sum_rows(down_sent)
+    down_flow = PlaneScatter(
+        jnp.concatenate([down_mine, gain_grad.astype(low_type)], axis=1), n_data
+    )
     clock.tick(grad_down)
-    clock.move(output_flow)
-    output = output_flow.result()
+    clock.move(down_flow)
+    clock.tick()
+    clock.move(down_flow)
     input_grad = input_back(
         clock.wait(grad_latents),
         down_all,
@@ -1033,16 +1291,22 @@
         jnp.concatenate([mid_norm[0], mid_norm[1]], axis=0),
         gain_in[None],
     )
+    clock.tick(input_grad)
+    clock.move(down_flow)
+    down_sum = wide(down_flow.result())
+    ffn_parts = ffn_sum.reshape(3, -1, hidden_dev)
     reduced = (
         down_sum[down_rows, :gain_count],
         down_sum[:down_rows, :QR],
         down_sum[:down_rows, QR:],
-        head_sum[out_rows : out_rows + up_rows, : query_up.shape[1]],
-        head_sum[out_rows + up_rows :],
-        jnp.concatenate([head_sum[:out_rows, :out_width], head_sum[:out_rows, out_width:]], axis=0).T,
-        ffn_sum[0],
-        ffn_sum[1],
-        ffn_sum[2].T,
+        wide(head_sum[out_rows : out_rows + up_rows, : query_up.shape[1]]),
+        wide(head_sum[out_rows + up_rows :]),
+        wide(
+            jnp.concatenate([head_sum[:out_rows, :out_width], head_sum[:out_rows, out_width:]], axis=0).T
+        ),
+        wide(ffn_parts[0]),
+        wide(ffn_parts[1]),
+        wide(ffn_parts[2].T),
     )
     weights = (
         norm_gains,

time: 960 us -> 849 us (0.88)
  other arithmetic: 162 us -> 84.3 us
  Pallas kernels: 264 us -> 311 us
  starting transfers between devices: 128 us -> 97.8 us
  matrix products: 45.2 us -> 21.7 us
  waiting for transfers between devices: 286 us -> 272 us
  local copies, waits for them, and re-layouts: 48.5 us -> 38.9 us
    psum x0 -> x1, waiting for transfers between devices: none -> 98.3 us  [local(): latents_sum = lax.psum(after(part_latents, ffn_sum), 'mp')]
    ppermute x24 -> x18, waiting for transfers between devices: 170 us -> 72.3 us  [advance(): self.above.append(lax.ppermute(down, 'mp', downs))]
    pallas_call x0 -> x7, Pallas kernels: none -> 46.2 us  [the longest x1 13.8 us: latents_forward(): pl.pallas_call(latents_kernel, grid=(tokens // BLK,), in_specs=[row_spec(...]
    convert_element_type x6 -> x2, other arithmetic: 19.4 us -> 0.07 us  [wide(): return value.astype(jnp.float32)]
    dot_general x6 -> x2, matrix products: 39.2 us -> 21.7 us  [contract(): return jnp.einsum(spec, left, right, preferred_element_type=jnp.float32)]
    reduce_scatter x3 -> x2, waiting for transfers between devices: 17.2 us -> 0.01 us  [the longest x1 0.01 us: local(): lax.psum_scatter(ffn_grads.reshape(-1, hidden_dev), 'dp', scatter_dimensi...]
    ppermute x24 -> x18, waiting for transfers between devices: 20.2 us -> 3.21 us  [advance(): self.below.append(lax.ppermute(up, 'mp', ups))]
    reduce_sum x12 -> x0, other arithmetic: 14.5 us -> none  [the longest x7 8.83 us: normalize(): jnp.mean(vector * vector, axis=-1, keepdims=True) + NORM_EPS]
  transfers between devices with their start and end apart: 79 -> 67, of which waited for: 27 -> 20; matrix products, arithmetic and copies ran while one was open for 23% -> 14% of each run, Pallas kernels for 24% -> 37%
where the time goes in v1:
time: 849 us; the launch traced here: 842 us
  Pallas kernels  311 us (37%)
  waiting for transfers between devices  272 us (32%)
  starting transfers between devices  97.8 us (12%)
  other arithmetic  84.3 us (10%)
  local copies, waits for them, and re-layouts  38.9 us (5%)
  matrix products  21.7 us (3%)
  between operations  16.5 us (2%)
    psum x1, waiting for transfers between devices, local(): latents_sum = lax.psum(after(part_latents, ffn_sum), 'mp')  98.3 us
    ppermute x18, waiting for transfers between devices, advance(): self.above.append(lax.ppermute(down, 'mp', downs))  72.3 us
    ppermute x12, waiting for transfers between devices, advance(): came.append(lax.ppermute(part, 'dp', pairs))  50.7 us
    pallas_call x4, Pallas kernels, ffn_back(): pl.pallas_call(functools.partial(back_kernel, count), grid=(2, tokens //...  50.5 us
    pallas_call x3, Pallas kernels, ffn_outer(): pl.pallas_call(functools.partial(outer_kernel, count), grid=(2,), in_spec...  44.8 us
    pallas_call x2, Pallas kernels, ffn_inner(): pl.pallas_call(inner_kernel, grid=(steps, 2, 2), in_specs=[pl.BlockSpec((...  39.1 us
    pallas_call x2, Pallas kernels, attend_backward(): pl.pallas_call(functools.partial(backward_kernel, half * size // BLK, hal...  36 us
    ppermute x18, starting transfers between devices, advance(): self.below.append(lax.ppermute(up, 'mp', ups))  31.9 us
  transfers between devices with their start and end apart: 67, of which 20 were waited for; matrix products, arithmetic and copies ran while one was open for 14% of the time, Pallas kernels for 37%

profile of v1, /device:TPU:0, one launch (start us, length us, event | category | flops | bytes accessed | tf_op | source)
XLA Modules:
  0.0 842.5 jit_solution(4493905679865091876)
XLA Ops:
  14.4 5.1 collective-permute-start.2
  20.8 3.8 collective-permute-done.2
  24.6 10.6 %collective-permute-done.1 = bf16[80,1056]{1,0:T(8,128)(2,1)S(1)} collective-permute-done((bf16[80,1056]{1,0:T(8,128)(2,1)S(1)}, bf16[80,1056]{1,0:T(8,128)(2,1)S(1)}, u32[]{:S(2)}, u32[]{:S(2)}) %collective-permute-start.1) | collective-permute-done | bytes 168992 | tf_op jit(solution)/shard_map/ppermute | solution.py:871
  39.7 2.8 collective-permute-start.7
  42.5 5.6 collective-permute-done.4
  49.5 13.8 %collective-permute-done.6 = bf16[1,160,1056]{2,1,0:T(8,128)(2,1)S(1)} collective-permute-done((bf16[1,160,1056]{2,1,0:T(8,128)(2,1)S(1)}, bf16[1,160,1056]{2,1,0:T(8,128)(2,1)S(1)}, u32[]{:S(2)}, u32[]{:S(2)}) %collective-permute-start.6) | collective-permute-done | bytes 337952 | tf_op jit(solution)/shard_map/ppermute | solution.py:937
  68.9 14.0 %collective-permute-done.9 = bf16[2,72,1280]{2,1,0:T(8,128)(2,1)} collective-permute-done((bf16[2,72,1280]{2,1,0:T(8,128)(2,1)S(1)}, bf16[2,72,1280]{2,1,0:T(8,128)(2,1)}, u32[]{:S(2)}, u32[]{:S(2)}) %collective-permute-start.9) | collective-permute-done | bytes 368672 | tf_op jit(solution)/shard_map/ppermute | solution.py:937
  83.5 15.8 %collective-permute-done.10 = bf16[2,72,1280]{2,1,0:T(8,128)(2,1)} collective-permute-done((bf16[2,72,1280]{2,1,0:T(8,128)(2,1)S(1)}, bf16[2,72,1280]{2,1,0:T(8,128)(2,1)}, u32[]{:S(2)}, u32[]{:S(2)}) %collective-permute-start.10) | collective-permute-done | bytes 368672 | tf_op jit(solution)/shard_map/ppermute | solution.py:937
  103.5 10.4 %collective-permute-done.28 = bf16[320,640]{1,0:T(8,128)(2,1)} collective-permute-done((bf16[320,640]{1,0:T(8,128)(2,1)}, bf16[320,640]{1,0:T(8,128)(2,1)}, u32[]{:S(2)}, u32[]{:S(2)}) %collective-permute-start.28) | collective-permute-done | bytes 409632 | tf_op jit(solution)/shard_map/ppermute | solution.py:842
  139.4 2.5 copy-done
  141.9 13.8 %latents_forward.1 = (bf16[1024,2560]{1,0:T(8,128)(2,1)}, f32[1024,1056]{1,0:T(8,128)}, bf16[1024,768]{1,0:T(8,128)(2,1)}, bf16[1024,256]{1,0:T(8,128)(2,1)}, bf16[32,1024]{1,0:T(8,128)(2,1)}) custom-call(bf16[1024,2560]{1,0:T(8,128)(2,1)} %inputs_ref.3, f32[1,2560]{1,0:T(1,128)} %broadcast_in_dim.45.gain_in.gain_ref, bf16[2560,1056]{1,0:T(8,128)(2,1)} %copy-done, ...), custom_call_target="tpu_custom_call" | custom-call | flops 27682 | bytes 1024 | tf_op jit(solution)/shard_map/latents_forward/pallas_call | solution.py:603
  155.7 6.9 heads_forward.1
  162.6 14.6 %attend_forward.2 = (bf16[10,64,512]{2,1,0:T(8,128)(2,1)}, f32[10,1,512]{2,1,0:T(1,128)}) custom-call(bf16[10,96,1024]{2,1,0:T(8,128)(2,1)} %get-tuple-element.174.q_ref.refs_0_, bf16[10,96,1024]{2,1,0:T(8,128)(2,1)} %get-tuple-element.171.k_ref.refs_1_, bf16[10,64,1024]{2,1,0:T(8,128)(2,1)} %get-tuple-element.172.v_ref.refs_2_), custom_call_target="tpu_custom_call" | custom-call | flops 73400 | bytes 1024 | tf_op jit(solution)/shard_map/attend_forward/pallas_call | solution.py:120
  179.9 10.2 %attend_forward.3 = (bf16[10,64,512]{2,1,0:T(8,128)(2,1)}, f32[10,1,512]{2,1,0:T(1,128)}) custom-call(bf16[10,96,1024]{2,1,0:T(8,128)(2,1)} %get-tuple-element.174.q_ref.refs_0_, bf16[10,96,1024]{2,1,0:T(8,128)(2,1)} %get-tuple-element.171.k_ref.refs_1_, bf16[10,64,1024]{2,1,0:T(8,128)(2,1)} %get-tuple-element.172.v_ref.refs_2_), custom_call_target="tpu_custom_call" | custom-call | flops 36700 | bytes 1024 | tf_op jit(solution)/shard_map/attend_forward/pallas_call | solution.py:120
  190.2 3.2 collective-permute-done.19
  193.3 4.0 collective-permute-done.20
  199.7 3.3 multiply_convert_fusion.grad_ref.refs_0_.refs_1_
  202.9 17.6 %hidden_back.1.grad_ref = f32[1024,1600]{1,0:T(8,128)} custom-call(bf16[1024,2560]{1,0:T(8,128)(2,1)} %multiply_convert_fusion.grad_ref.refs_0_.refs_1_, bf16[8,3,320,1600]{3,2,1,0:T(8,128)(2,1)} %all-gather.3.cloned.1.call-done.weight_ref.refs_2_.refs_1_), custom_call_target="tpu_custom_call" | custom-call | flops 83886 | bytes 1024 | tf_op jit(solution)/shard_map/hidden_back/pallas_call | solution.py:275
  222.5 17.5 %collective-permute-done.24 = bf16[640,512]{1,0:T(8,128)(2,1)S(1)} collective-permute-done((bf16[640,512]{1,0:T(8,128)(2,1)S(1)}, bf16[640,512]{1,0:T(8,128)(2,1)S(1)}, u32[]{:S(2)}, u32[]{:S(2)}) %collective-permute-start.24) | collective-permute-done | bytes 655392 | tf_op jit(solution)/shard_map/ppermute | solution.py:842
  245.1 2.9 all-gather.5.cloned.1.call-done
  248.1 10.8 %multiply_reduce_fusion.1 = (f32[512]{0:T(512)S(1)}, f32[512,2560]{1,0:T(8,128)S(1)}) fusion(bf16[2560,512]{1,0:T(8,128)(2,1)S(1)} %pad_maximum_fusion.5, bf16[2560,2560]{1,0:T(8,128)(2,1)} %all-gather.5.cloned.1.call-done, bf16[1024,2560]{1,0:T(8,128)(2,1)} %inputs_ref.3), kind=kOutput, calls=%fused_computation.9 | convolution fusion | flops 6717439488 | bytes 23595008 | tf_op jit(solution)/shard_map/ht,dh->td/dot_general | solution.py:52
  264.5 19.5 %ffn_inner.2 = (bf16[512,1600]{1,0:T(8,128)(2,1)}, bf16[512,1600]{1,0:T(8,128)(2,1)}, bf16[512,1600]{1,0:T(8,128)(2,1)}) custom-call(bf16[512,2560]{1,0:T(8,128)(2,1)} %multiply_convert_fusion.2.normed_ref.refs_0_, f32[1024,1600]{1,0:T(8,128)} %hidden_back.1.grad_ref, bf16[8,3,320,1600]{3,2,1,0:T(8,128)(2,1)} %all-gather.3.cloned.1.call-done.weight_ref.refs_2_.refs_1_), custom_call_target="tpu_custom_call" | custom-call | flops 83886 | bytes 1024 | tf_op jit(solution)/shard_map/ffn_inner/pallas_call | solution.py:323
  286.0 15.4 %ffn_back.4 = bf16[512,2560]{1,0:T(8,128)(2,1)} custom-call(bf16[512,1600]{1,0:T(8,128)(2,1)} %get-tuple-element.206.refs_0_.refs_2_, bf16[512,1600]{1,0:T(8,128)(2,1)} %get-tuple-element.191.refs_1_.refs_2_, bf16[8,3,320,1600]{3,2,1,0:T(8,128)(2,1)} %all-gather.3.cloned.1.call-done.weight_ref.refs_2_.refs_1_), custom_call_target="tpu_custom_call" | custom-call | flops 167772 | bytes 1024 | tf_op jit(solution)/shard_map/ffn_back/pallas_call | solution.py:357
  301.6 4.1 collective-permute-done.32
  307.5 10.9 %multiply_reduce_fusion = (f32[512]{0:T(512)S(1)}, f32[512,2560]{1,0:T(8,128)S(1)}) fusion(bf16[2560,512]{1,0:T(8,128)(2,1)S(1)} %pad_maximum_fusion.6, bf16[2560,2560]{1,0:T(8,128)(2,1)} %all-gather.5.cloned.1.call-done, bf16[1024,2560]{1,0:T(8,128)(2,1)} %inputs_ref.3), kind=kOutput, calls=%fused_computation.6 | convolution fusion | flops 6717439488 | bytes 23595008 | tf_op jit(solution)/shard_map/ht,dh->td/dot_general | solution.py:52
  322.8 19.6 %ffn_inner.3 = (bf16[512,1600]{1,0:T(8,128)(2,1)}, bf16[512,1600]{1,0:T(8,128)(2,1)}, bf16[512,1600]{1,0:T(8,128)(2,1)}) custom-call(bf16[512,2560]{1,0:T(8,128)(2,1)} %multiply_convert_fusion.1.normed_ref.refs_1_, f32[1024,1600]{1,0:T(8,128)} %hidden_back.1.grad_ref, bf16[8,3,320,1600]{3,2,1,0:T(8,128)(2,1)} %all-gather.3.cloned.1.call-done.weight_ref.refs_2_.refs_1_), custom_call_target="tpu_custom_call" | custom-call | flops 83886 | bytes 1024 | tf_op jit(solution)/shard_map/ffn_inner/pallas_call | solution.py:323
  342.4 15.4 %ffn_back.5 = bf16[512,2560]{1,0:T(8,128)(2,1)} custom-call(bf16[512,1600]{1,0:T(8,128)(2,1)} %get-tuple-element.202.refs_0_.refs_3_, bf16[512,1600]{1,0:T(8,128)(2,1)} %get-tuple-element.201.refs_1_.refs_3_, bf16[8,3,320,1600]{3,2,1,0:T(8,128)(2,1)} %all-gather.3.cloned.1.call-done.weight_ref.refs_2_.refs_1_), custom_call_target="tpu_custom_call" | custom-call | flops 167772 | bytes 1024 | tf_op jit(solution)/shard_map/ffn_back/pallas_call | solution.py:357
  358.5 3.2 middle_back.2
  361.6 2.6 collective-permute-start.33
  365.6 15.2 %ffn_outer.3 = (bf16[8,3,320,1600]{3,2,1,0:T(8,128)(2,1)}, f32[8,128]{1,0:T(8,128)}) custom-call(bf16[512,2560]{1,0:T(8,128)(2,1)} %multiply_convert_fusion.2.normed_ref.refs_0_, bf16[512,2560]{1,0:T(8,128)(2,1)} %multiply_convert_fusion.1.normed_ref.refs_1_, bf16[512,1600]{1,0:T(8,128)(2,1)} %get-tuple-element.206.refs_0_.refs_2_, ...), custom_call_target="tpu_custom_call" | custom-call | flops 167772 | bytes 1024 | tf_op jit(solution)/shard_map/ffn_outer/pallas_call | solution.py:387
  380.8 14.7 %ffn_outer.4 = (bf16[8,3,320,1600]{3,2,1,0:T(8,128)(2,1)}, f32[8,128]{1,0:T(8,128)}) custom-call(bf16[512,2560]{1,0:T(8,128)(2,1)} %multiply_convert_fusion.2.normed_ref.refs_0_, bf16[512,2560]{1,0:T(8,128)(2,1)} %multiply_convert_fusion.1.normed_ref.refs_1_, bf16[512,1600]{1,0:T(8,128)(2,1)} %get-tuple-element.191.refs_1_.refs_2_, ...), custom_call_target="tpu_custom_call", output_to_operand_aliasing={{0}: (4, {})} | custom-call | flops 167772 | bytes 1024 | tf_op jit(solution)/shard_map/ffn_outer/pallas_call | solution.py:387
  395.5 14.9 %ffn_outer.5 = (bf16[8,3,320,1600]{3,2,1,0:T(8,128)(2,1)}, f32[8,128]{1,0:T(8,128)}) custom-call(bf16[1024,2560]{1,0:T(8,128)(2,1)} %multiply_convert_fusion.grad_ref.refs_0_.refs_1_, bf16[1024,2560]{1,0:T(8,128)(2,1)} %multiply_convert_fusion.grad_ref.refs_0_.refs_1_, ...), custom_call_target="tpu_custom_call", output_to_operand_aliasing={{0}: (4, {})} | custom-call | flops 167772 | bytes 1024 | tf_op jit(solution)/shard_map/ffn_outer/pallas_call | solution.py:387
  412.9 9.2 %ffn_back.6 = bf16[512,2560]{1,0:T(8,128)(2,1)} custom-call(bf16[512,1600]{1,0:T(8,128)(2,1)} %get-tuple-element.214.refs_2_.refs_0_, bf16[8,3,320,1600]{3,2,1,0:T(8,128)(2,1)} %all-gather.3.cloned.1.call-done.weight_ref.refs_2_.refs_1_), custom_call_target="tpu_custom_call" | custom-call | flops 83886 | bytes 1024 | tf_op jit(solution)/shard_map/ffn_back/pallas_call | solution.py:357
  423.0 13.9 %collective-permute-done.36 = bf16[128,2560]{1,0:T(8,128)(2,1)} collective-permute-done((bf16[128,2560]{1,0:T(8,128)(2,1)S(1)}, bf16[128,2560]{1,0:T(8,128)(2,1)}, u32[]{:S(2)}, u32[]{:S(2)}) %collective-permute-start.36) | collective-permute-done | bytes 655392 | tf_op jit(solution)/shard_map/ppermute | solution.py:842
  439.2 3.6 copy.75
  445.1 10.6 %ffn_back.7 = bf16[512,2560]{1,0:T(8,128)(2,1)} custom-call(bf16[512,1600]{1,0:T(8,128)(2,1)} %get-tuple-element.215.refs_3_.refs_0_, bf16[8,3,320,1600]{3,2,1,0:T(8,128)(2,1)} %all-gather.3.cloned.1.call-done.weight_ref.refs_2_.refs_1_), custom_call_target="tpu_custom_call" | custom-call | flops 83886 | bytes 1024 | tf_op jit(solution)/shard_map/ffn_back/pallas_call | solution.py:357
  455.6 2.7 pad_maximum_fusion
  458.4 3.1 copy-done.3
  463.1 3.9 middle_back.3
  467.0 5.4 collective-permute-start.39
  476.7 6.3 mixed_gradient.2
  483.0 22.4 %attend_backward.2 = (bf16[10,96,512]{2,1,0:T(8,128)(2,1)}, bf16[10,128,512]{2,1,0:T(8,128)(2,1)}, f32[32,512]{1,0:T(8,128)}, f32[10,96,512]{2,1,0:T(8,128)}, f32[10,64,512]{2,1,0:T(8,128)}) custom-call(bf16[10,96,1024]{2,1,0:T(8,128)(2,1)} %get-tuple-element.174.q_ref.refs_0_, bf16[10,96,1024]{2,1,0:T(8,128)(2,1)} %get-tuple-element.171.k_ref.refs_1_, ...), custom_call_target="tpu_custom_call" | custom-call | flops 157286 | bytes 1024 | tf_op jit(solution)/shard_map/attend_backward/pallas_call | solution.py:242
  505.4 6.1 collective-permute-start.41
  516.1 16.1 %collective-permute-done.44 = bf16[128,2560]{1,0:T(8,128)(2,1)} collective-permute-done((bf16[128,2560]{1,0:T(8,128)(2,1)S(1)}, bf16[128,2560]{1,0:T(8,128)(2,1)}, u32[]{:S(2)}, u32[]{:S(2)}) %collective-permute-start.44) | collective-permute-done | bytes 655392 | tf_op jit(solution)/shard_map/ppermute | solution.py:842
  532.2 5.8 collective-permute-done.41
  540.0 3.3 fusion.4
  543.3 4.9 collective-permute-start.45
  549.7 24.5 %collective-permute-done.45 = bf16[256,2560]{1,0:T(8,128)(2,1)S(1)} collective-permute-done((bf16[256,2560]{1,0:T(8,128)(2,1)S(1)}, bf16[256,2560]{1,0:T(8,128)(2,1)S(1)}, u32[]{:S(2)}, u32[]{:S(2)}) %collective-permute-start.45) | collective-permute-done | bytes 1310752 | tf_op jit(solution)/shard_map/ppermute | solution.py:906
  576.3 7.6 collective-permute-start.49
  591.1 5.7 mixed_gradient.3
  596.8 13.6 %attend_backward.3 = (bf16[10,96,512]{2,1,0:T(8,128)(2,1)}, bf16[10,128,512]{2,1,0:T(8,128)(2,1)}, f32[32,512]{1,0:T(8,128)}) custom-call(bf16[10,96,1024]{2,1,0:T(8,128)(2,1)} %get-tuple-element.174.q_ref.refs_0_, bf16[10,96,1024]{2,1,0:T(8,128)(2,1)} %get-tuple-element.171.k_ref.refs_1_, bf16[10,64,1024]{2,1,0:T(8,128)(2,1)} %get-tuple-element.172.v_ref.refs_2_, ...), custom_call_target="tpu_custom_call" | custom-call | flops 78643 | bytes 1024 | tf_op jit(solution)/shard_map/attend_backward/pallas_call | solution.py:242
  610.5 7.0 latent_back.1
  617.5 5.2 fusion.2
  624.3 5.5 collective-permute-start.51
  632.9 13.5 %heads_outer.1 = bf16[8,288,1280]{2,1,0:T(8,128)(2,1)} custom-call(bf16[512,2560]{1,0:T(8,128)(2,1)} %get-tuple-element.269.refs_0_, bf16[512,2560]{1,0:T(8,128)(2,1)} %get-tuple-element.270.refs_1_, bf16[640,512]{1,0:T(8,128)(2,1)} %bitcast.207, bf16[640,512]{1,0:T(8,128)(2,1)} %bitcast.206, bf16[960,512]{1,0:T(8,128)(2,1)} %bitcast.201, ...), custom_call_target="tpu_custom_call" | custom-call | flops 67108 | bytes 1024 | tf_op jit(solution)/shard_map/heads_outer/pallas_call | solution.py:547
  646.4 98.3 %all-reduce.5.cloned.1.call-done.total_ref = bf16[1040,1056]{1,0:T(8,128)(2,1)} async-done(((bf16[1040,1056]{1,0:T(8,128)(2,1)}), bf16[1040,1056]{1,0:T(8,128)(2,1)}) %all-reduce.5.cloned.1.call-update) | async-done | bytes 2196496 | tf_op jit(solution)/shard_map/psum | solution.py:1234
  749.8 6.5 latents_turned.1
  756.3 13.8 %down_outer.1 = (bf16[2560,1056]{1,0:T(8,128)(2,1)}, f32[2560,1]{1,0:T(8,128)}) custom-call(bf16[1024,2560]{1,0:T(8,128)(2,1)} %get-tuple-element.260.normed_ref, bf16[1024,1056]{1,0:T(8,128)(2,1)} %get-tuple-element.266.grad_ref, bf16[2560,1056]{1,0:T(8,128)(2,1)} %copy-done, f32[2560,1]{1,0:T(8,128)} %broadcast_in_dim.51.gain_ref), custom_call_target="tpu_custom_call" | custom-call | flops 110729 | bytes 1024 | tf_op jit(solution)/shard_map/down_outer/pallas_call | solution.py:420
  775.5 8.1 multiply_subtract_fusion.1
  788.8 3.9 multiply_subtract_fusion
  792.6 17.7 %input_back.1 = f32[1024,2560]{1,0:T(8,128)} custom-call(bf16[1024,1056]{1,0:T(8,128)(2,1)} %get-tuple-element.266.grad_ref, bf16[2560,1056]{1,0:T(8,128)(2,1)} %copy-done, bf16[1024,2560]{1,0:T(8,128)(2,1)} %inputs_ref.3, bf16[1024,2560]{1,0:T(8,128)(2,1)} %cot_ref.5, bf16[1024,2560]{1,0:T(8,128)(2,1)} %constant_dynamic-update-slice_fusion.mid_ref, ...), custom_call_target="tpu_custom_call" | custom-call | flops 110729 | bytes 1024 | tf_op jit(solution)/shard_map/input_back/pallas_call | solution.py:453
  813.2 5.8 collective-permute-done.56
  819.0 3.2 select_select_fusion.3
  822.3 3.4 pad_maximum_fusion.1
  (363 shorter events, 140.7 us)
Async XLA Ops:
  7.2 195.7 %all-gather.3.cloned.1.call-start = ((), (), s32[]{:S(2)}) async-start(), calls=%async_computation.4 | async-start | bytes 28753920 | tf_op jit(solution)/shard_map/all_gather | solution.py:1088
  13.4 234.6 %all-gather.5.cloned.1.call-start = ((), (), s32[]{:S(2)}) async-start(), calls=%async_computation.5 | async-start | bytes 14745600 | tf_op jit(solution)/shard_map/all_gather | solution.py:1085
  14.4 10.2 %collective-permute-start.2 = (bf16[80,1056]{1,0:T(8,128)(2,1)S(1)}, bf16[80,1056]{1,0:T(8,128)(2,1)S(1)}, u32[]{:S(2)}, u32[]{:S(2)}) collective-permute-start(bf16[80,1056]{1,0:T(8,128)(2,1)S(1)} %pad_maximum_fusion.23), channel_id=1, source_target_pairs={{0,3},{1,0},{2,1},{3,2},{4,7},{5,4},{6,5},{7,6},{8,11},{9,8},{10,9... | collective-permute-start | bytes 506888 | tf_op jit(solution)/shard_map/ppermute | solution.py:871
  19.5 15.6 %collective-permute-start.1 = (bf16[80,1056]{1,0:T(8,128)(2,1)S(1)}, bf16[80,1056]{1,0:T(8,128)(2,1)S(1)}, u32[]{:S(2)}, u32[]{:S(2)}) collective-permute-start(bf16[80,1056]{1,0:T(8,128)(2,1)S(1)} %pad_maximum_fusion.23), channel_id=1, source_target_pairs={{0,2},{1,3},{2,0},{3,1},{4,6},{5,7},{6,4},{7,5},{8,10},{9,11},{10,... | collective-permute-start | bytes 506888 | tf_op jit(solution)/shard_map/ppermute | solution.py:871
  19.5 15.6 %collective-permute-start = (bf16[80,1056]{1,0:T(8,128)(2,1)S(1)}, bf16[80,1056]{1,0:T(8,128)(2,1)S(1)}, u32[]{:S(2)}, u32[]{:S(2)}) collective-permute-start(bf16[80,1056]{1,0:T(8,128)(2,1)S(1)} %pad_maximum_fusion.23), channel_id=1, source_target_pairs={{0,1},{1,2},{2,3},{3,0},{4,5},{5,6},{6,7},{7,4},{8,9},{9,10},{10,1... | collective-permute-start | bytes 506888 | tf_op jit(solution)/shard_map/ppermute | solution.py:871
  35.2 14.2 %collective-permute-start.3 = (bf16[1,72,1280]{2,1,0:T(8,128)(2,1)S(1)}, bf16[1,72,1280]{2,1,0:T(8,128)(2,1)S(1)}, u32[]{:S(2)}, u32[]{:S(2)}) collective-permute-start(bf16[1,72,1280]{2,1,0:T(8,128)(2,1)S(1)} %get-tuple-element.151), channel_id=1, source_target_pairs={{0,8},{4,12},{8,0},{12,4},{16,24},{20,28},{24,16},{28,20},{1,9},{5... | collective-permute-start | bytes 552968 | tf_op jit(solution)/shard_map/ppermute | solution.py:937
  36.7 11.4 %collective-permute-start.4 = (bf16[1,72,1280]{2,1,0:T(8,128)(2,1)S(1)}, bf16[1,72,1280]{2,1,0:T(8,128)(2,1)S(1)}, u32[]{:S(2)}, u32[]{:S(2)}) collective-permute-start(bf16[1,72,1280]{2,1,0:T(8,128)(2,1)S(1)} %get-tuple-element.152), channel_id=1, source_target_pairs={{0,16},{4,20},{8,24},{12,28},{16,0},{20,4},{24,8},{28,12},{1,17},{... | collective-permute-start | bytes 552968 | tf_op jit(solution)/shard_map/ppermute | solution.py:937
  38.6 24.8 %collective-permute-start.5 = (bf16[1,160,1056]{2,1,0:T(8,128)(2,1)S(1)}, bf16[1,160,1056]{2,1,0:T(8,128)(2,1)S(1)}, u32[]{:S(2)}, u32[]{:S(2)}) collective-permute-start(bf16[1,160,1056]{2,1,0:T(8,128)(2,1)S(1)} %get-tuple-element.153), channel_id=1, source_target_pairs={{0,8},{4,12},{8,0},{12,4},{16,24},{20,28},{24,16},{28,20},{1,9},{5... | collective-permute-start | bytes 1013768 | tf_op jit(solution)/shard_map/ppermute | solution.py:937
  39.2 24.1 %collective-permute-start.6 = (bf16[1,160,1056]{2,1,0:T(8,128)(2,1)S(1)}, bf16[1,160,1056]{2,1,0:T(8,128)(2,1)S(1)}, u32[]{:S(2)}, u32[]{:S(2)}) collective-permute-start(bf16[1,160,1056]{2,1,0:T(8,128)(2,1)S(1)} %get-tuple-element.154), channel_id=1, source_target_pairs={{0,16},{4,20},{8,24},{12,28},{16,0},{20,4},{24,8},{28,12},{1,17},{... | collective-permute-start | bytes 1013768 | tf_op jit(solution)/shard_map/ppermute | solution.py:937
  39.7 23.7 %collective-permute-start.7 = (bf16[320,640]{1,0:T(8,128)(2,1)S(1)}, bf16[320,640]{1,0:T(8,128)(2,1)S(1)}, u32[]{:S(2)}, u32[]{:S(2)}) collective-permute-start(bf16[320,640]{1,0:T(8,128)(2,1)S(1)} %convert_bitcast_fusion.3), channel_id=1, source_target_pairs={{0,1},{1,2},{2,3},{4,5},{5,6},{6,7},{8,9},{9,10},{10,11},{12,13},{... | collective-permute-start | bytes 1228808 | tf_op jit(solution)/shard_map/ppermute | solution.py:841
  48.1 15.3 %collective-permute-start.8 = (bf16[320,640]{1,0:T(8,128)(2,1)S(1)}, bf16[320,640]{1,0:T(8,128)(2,1)S(1)}, u32[]{:S(2)}, u32[]{:S(2)}) collective-permute-start(bf16[320,640]{1,0:T(8,128)(2,1)S(1)} %convert_bitcast_fusion.3), channel_id=1, source_target_pairs={{1,0},{2,1},{3,2},{5,4},{6,5},{7,6},{9,8},{10,9},{11,10},{13,12},{... | collective-permute-start | bytes 1228808 | tf_op jit(solution)/shard_map/ppermute | solution.py:842
  63.5 19.5 %collective-permute-start.9 = (bf16[2,72,1280]{2,1,0:T(8,128)(2,1)S(1)}, bf16[2,72,1280]{2,1,0:T(8,128)(2,1)}, u32[]{:S(2)}, u32[]{:S(2)}) collective-permute-start(bf16[2,72,1280]{2,1,0:T(8,128)(2,1)S(1)} %pad_maximum_fusion.19), channel_id=1, source_target_pairs={{0,16},{4,20},{8,24},{12,28},{16,0},{20,4},{24,8},{28,12},{1,17},{... | collective-permute-start | bytes 1105928 | tf_op jit(solution)/shard_map/ppermute | solution.py:937
  65.1 35.6 %collective-permute-start.11 = (bf16[2,160,1056]{2,1,0:T(8,128)(2,1)S(1)}, bf16[2,160,1056]{2,1,0:T(8,128)(2,1)}, u32[]{:S(2)}, u32[]{:S(2)}) collective-permute-start(bf16[2,160,1056]{2,1,0:T(8,128)(2,1)S(1)} %pad_maximum_fusion.16), channel_id=1, source_target_pairs={{0,16},{4,20},{8,24},{12,28},{16,0},{20,4},{24,8},{28,12},{1,17},{... | collective-permute-start | bytes 2027528 | tf_op jit(solution)/shard_map/ppermute | solution.py:937
  65.7 35.1 %collective-permute-start.12 = (bf16[2,160,1056]{2,1,0:T(8,128)(2,1)S(1)}, bf16[2,160,1056]{2,1,0:T(8,128)(2,1)}, u32[]{:S(2)}, u32[]{:S(2)}) collective-permute-start(bf16[2,160,1056]{2,1,0:T(8,128)(2,1)S(1)} %pad_maximum_fusion.17), channel_id=1, source_target_pairs={{0,8},{4,12},{8,0},{12,4},{16,24},{20,28},{24,16},{28,20},{1,9},{5... | collective-permute-start | bytes 2027528 | tf_op jit(solution)/shard_map/ppermute | solution.py:937
  66.2 33.0 %collective-permute-start.13 = (bf16[320,640]{1,0:T(8,128)(2,1)S(1)}, bf16[320,640]{1,0:T(8,128)(2,1)}, u32[]{:S(2)}, u32[]{:S(2)}) collective-permute-start(bf16[320,640]{1,0:T(8,128)(2,1)S(1)} %collective-permute-done.7), channel_id=1, source_target_pairs={{1,2},{2,3},{5,6},{6,7},{9,10},{10,11},{13,14},{14,15},{17,18},{18... | collective-permute-start | bytes 1228808 | tf_op jit(solution)/shard_map/ppermute | solution.py:841
  67.6 31.6 %collective-permute-start.14 = (bf16[320,640]{1,0:T(8,128)(2,1)S(1)}, bf16[320,640]{1,0:T(8,128)(2,1)}, u32[]{:S(2)}, u32[]{:S(2)}) collective-permute-start(bf16[320,640]{1,0:T(8,128)(2,1)S(1)} %collective-permute-done.8), channel_id=1, source_target_pairs={{1,0},{2,1},{5,4},{6,5},{9,8},{10,9},{13,12},{14,13},{17,16},{18,1... | collective-permute-start | bytes 1228808 | tf_op jit(solution)/shard_map/ppermute | solution.py:842
  82.9 16.3 %collective-permute-start.10 = (bf16[2,72,1280]{2,1,0:T(8,128)(2,1)S(1)}, bf16[2,72,1280]{2,1,0:T(8,128)(2,1)}, u32[]{:S(2)}, u32[]{:S(2)}) collective-permute-start(bf16[2,72,1280]{2,1,0:T(8,128)(2,1)S(1)} %pad_maximum_fusion.20), channel_id=1, source_target_pairs={{0,8},{4,12},{8,0},{12,4},{16,24},{20,28},{24,16},{28,20},{1,9},{5... | collective-permute-start | bytes 1105928 | tf_op jit(solution)/shard_map/ppermute | solution.py:937
  102.2 11.7 %collective-permute-start.28 = (bf16[320,640]{1,0:T(8,128)(2,1)}, bf16[320,640]{1,0:T(8,128)(2,1)}, u32[]{:S(2)}, u32[]{:S(2)}) collective-permute-start(bf16[320,640]{1,0:T(8,128)(2,1)} %collective-permute-done.14), channel_id=1, source_target_pairs={{1,0},{5,4},{9,8},{13,12},{17,16},{21,20},{25,24},{29,28}} | collective-permute-start | bytes 1228808 | tf_op jit(solution)/shard_map/ppermute | solution.py:842
  117.1 240.7 %reduce-scatter.5.cloned.1.call-start = ((), (), s32[]{:S(2)}) async-start(), calls=%async_computation.6 | async-start | bytes 3276800 | tf_op jit(solution)/shard_map/reduce_scatter | solution.py:1149
  119.7 6.9 collective-permute-start.15
  120.8 7.0 collective-permute-start.16
  126.1 8.7 %collective-permute-start.17 = (bf16[4,160,1056]{2,1,0:T(8,128)(2,1)}, bf16[4,160,1056]{2,1,0:T(8,128)(2,1)}, u32[]{:S(2)}, u32[]{:S(2)}) collective-permute-start(bf16[4,160,1056]{2,1,0:T(8,128)(2,1)} %pad_maximum_fusion.12), channel_id=1, source_target_pairs={{0,4},{4,0},{8,12},{12,8},{16,20},{20,16},{24,28},{28,24},{1,5},{5... | collective-permute-start | bytes 4055048 | tf_op jit(solution)/shard_map/ppermute | solution.py:937
  126.1 10.6 %collective-permute-start.18 = (bf16[4,160,1056]{2,1,0:T(8,128)(2,1)}, bf16[4,160,1056]{2,1,0:T(8,128)(2,1)}, u32[]{:S(2)}, u32[]{:S(2)}) collective-permute-start(bf16[4,160,1056]{2,1,0:T(8,128)(2,1)} %pad_maximum_fusion.13), channel_id=1, source_target_pairs={{0,4},{4,0},{8,12},{12,8},{16,20},{20,16},{24,28},{28,24},{1,5},{5... | collective-permute-start | bytes 4055048 | tf_op jit(solution)/shard_map/ppermute | solution.py:937
  177.3 16.0 %collective-permute-start.19 = (bf16[640,512]{1,0:T(8,128)(2,1)}, bf16[640,512]{1,0:T(8,128)(2,1)S(1)}, u32[]{:S(2)}, u32[]{:S(2)}) collective-permute-start(bf16[640,512]{1,0:T(8,128)(2,1)} %bitcast.204), channel_id=1, source_target_pairs={{0,1},{1,2},{2,3},{4,5},{5,6},{6,7},{8,9},{9,10},{10,11},{12,13},{... | collective-permute-start | bytes 1966088 | tf_op jit(solution)/shard_map/ppermute | solution.py:841
  178.6 18.8 %collective-permute-start.20 = (bf16[640,512]{1,0:T(8,128)(2,1)}, bf16[640,512]{1,0:T(8,128)(2,1)S(1)}, u32[]{:S(2)}, u32[]{:S(2)}) collective-permute-start(bf16[640,512]{1,0:T(8,128)(2,1)} %bitcast.205), channel_id=1, source_target_pairs={{1,0},{2,1},{3,2},{5,4},{6,5},{7,6},{9,8},{10,9},{11,10},{13,12},{... | collective-permute-start | bytes 1966088 | tf_op jit(solution)/shard_map/ppermute | solution.py:842
  197.4 23.1 %collective-permute-start.21 = (bf16[640,512]{1,0:T(8,128)(2,1)S(1)}, bf16[640,512]{1,0:T(8,128)(2,1)S(1)}, u32[]{:S(2)}, u32[]{:S(2)}) collective-permute-start(bf16[640,512]{1,0:T(8,128)(2,1)S(1)} %collective-permute-done.19), channel_id=1, source_target_pairs={{1,2},{2,3},{5,6},{6,7},{9,10},{10,11},{13,14},{14,15},{17,18},{18... | collective-permute-start | bytes 1966088 | tf_op jit(solution)/shard_map/ppermute | solution.py:841
  198.1 22.4 %collective-permute-start.22 = (bf16[640,512]{1,0:T(8,128)(2,1)S(1)}, bf16[640,512]{1,0:T(8,128)(2,1)S(1)}, u32[]{:S(2)}, u32[]{:S(2)}) collective-permute-start(bf16[640,512]{1,0:T(8,128)(2,1)S(1)} %collective-permute-done.20), channel_id=1, source_target_pairs={{1,0},{2,1},{5,4},{6,5},{9,8},{10,9},{13,12},{14,13},{17,16},{18,1... | collective-permute-start | bytes 1966088 | tf_op jit(solution)/shard_map/ppermute | solution.py:842
  221.2 18.8 %collective-permute-start.24 = (bf16[640,512]{1,0:T(8,128)(2,1)S(1)}, bf16[640,512]{1,0:T(8,128)(2,1)S(1)}, u32[]{:S(2)}, u32[]{:S(2)}) collective-permute-start(bf16[640,512]{1,0:T(8,128)(2,1)S(1)} %collective-permute-done.22), channel_id=1, source_target_pairs={{1,0},{5,4},{9,8},{13,12},{17,16},{21,20},{25,24},{29,28}} | collective-permute-start | bytes 1966088 | tf_op jit(solution)/shard_map/ppermute | solution.py:842
  241.5 20.5 %collective-permute-start.25 = (bf16[640,512]{1,0:T(8,128)(2,1)S(1)}, bf16[640,512]{1,0:T(8,128)(2,1)}, u32[]{:S(2)}, u32[]{:S(2)}) collective-permute-start(bf16[640,512]{1,0:T(8,128)(2,1)S(1)} %bitcast.208), channel_id=1, source_target_pairs={{0,1},{1,2},{2,3},{4,5},{5,6},{6,7},{8,9},{9,10},{10,11},{12,13},{... | collective-permute-start | bytes 1966088 | tf_op jit(solution)/shard_map/ppermute | solution.py:841
  243.8 18.2 %collective-permute-start.26 = (bf16[640,512]{1,0:T(8,128)(2,1)S(1)}, bf16[640,512]{1,0:T(8,128)(2,1)}, u32[]{:S(2)}, u32[]{:S(2)}) collective-permute-start(bf16[640,512]{1,0:T(8,128)(2,1)S(1)} %bitcast.209), channel_id=1, source_target_pairs={{1,0},{2,1},{3,2},{5,4},{6,5},{7,6},{9,8},{10,9},{11,10},{13,12},{... | collective-permute-start | bytes 1966088 | tf_op jit(solution)/shard_map/ppermute | solution.py:842
  262.0 22.0 %collective-permute-start.29 = (bf16[640,512]{1,0:T(8,128)(2,1)}, bf16[640,512]{1,0:T(8,128)(2,1)S(1)}, u32[]{:S(2)}, u32[]{:S(2)}) collective-permute-start(bf16[640,512]{1,0:T(8,128)(2,1)} %collective-permute-done.25), channel_id=1, source_target_pairs={{1,2},{2,3},{5,6},{6,7},{9,10},{10,11},{13,14},{14,15},{17,18},{18... | collective-permute-start | bytes 1966088 | tf_op jit(solution)/shard_map/ppermute | solution.py:841
  262.7 21.3 %collective-permute-start.30 = (bf16[640,512]{1,0:T(8,128)(2,1)}, bf16[640,512]{1,0:T(8,128)(2,1)S(1)}, u32[]{:S(2)}, u32[]{:S(2)}) collective-permute-start(bf16[640,512]{1,0:T(8,128)(2,1)} %collective-permute-done.26), channel_id=1, source_target_pairs={{1,0},{2,1},{5,4},{6,5},{9,8},{10,9},{13,12},{14,13},{17,16},{18,1... | collective-permute-start | bytes 1966088 | tf_op jit(solution)/shard_map/ppermute | solution.py:842
  284.0 17.6 %collective-permute-start.31 = (bf16[640,512]{1,0:T(8,128)(2,1)S(1)}, bf16[640,512]{1,0:T(8,128)(2,1)S(1)}, u32[]{:S(2)}, u32[]{:S(2)}) collective-permute-start(bf16[640,512]{1,0:T(8,128)(2,1)S(1)} %collective-permute-done.29), channel_id=1, source_target_pairs={{2,3},{6,7},{10,11},{14,15},{18,19},{22,23},{26,27},{30,31}} | collective-permute-start | bytes 1966088 | tf_op jit(solution)/shard_map/ppermute | solution.py:841
  284.7 21.0 %collective-permute-start.32 = (bf16[640,512]{1,0:T(8,128)(2,1)S(1)}, bf16[640,512]{1,0:T(8,128)(2,1)S(1)}, u32[]{:S(2)}, u32[]{:S(2)}) collective-permute-start(bf16[640,512]{1,0:T(8,128)(2,1)S(1)} %collective-permute-done.30), channel_id=1, source_target_pairs={{1,0},{5,4},{9,8},{13,12},{17,16},{21,20},{25,24},{29,28}} | collective-permute-start | bytes 1966088 | tf_op jit(solution)/shard_map/ppermute | solution.py:842
  301.4 135.5 %reduce-scatter.7.cloned.1.call-start = ((), (), s32[]{:S(2)}) async-start(), calls=%async_computation.7 | async-start | bytes 3276800 | tf_op jit(solution)/shard_map/reduce_scatter | solution.py:1149
  357.8 264.9 %reduce-scatter.9.cloned.1.call-start = ((), (), s32[]{:S(2)}) async-start(), calls=%async_computation.8 | async-start | bytes 28753920 | tf_op jit(solution)/shard_map/reduce_scatter | solution.py:1187
  361.6 48.8 %collective-permute-start.33 = (bf16[128,2560]{1,0:T(8,128)(2,1)}, bf16[128,2560]{1,0:T(8,128)(2,1)S(1)}, u32[]{:S(2)}, u32[]{:S(2)}) collective-permute-start(bf16[128,2560]{1,0:T(8,128)(2,1)} %get-tuple-element.204), channel_id=1, source_target_pairs={{0,1},{1,2},{2,3},{4,5},{5,6},{6,7},{8,9},{9,10},{10,11},{12,13},{... | collective-permute-start | bytes 1966088 | tf_op jit(solution)/shard_map/ppermute | solution.py:841
  364.3 46.6 %collective-permute-start.34 = (bf16[128,2560]{1,0:T(8,128)(2,1)}, bf16[128,2560]{1,0:T(8,128)(2,1)S(1)}, u32[]{:S(2)}, u32[]{:S(2)}) collective-permute-start(bf16[128,2560]{1,0:T(8,128)(2,1)} %get-tuple-element.204), channel_id=1, source_target_pairs={{1,0},{2,1},{3,2},{5,4},{6,5},{7,6},{9,8},{10,9},{11,10},{13,12},{... | collective-permute-start | bytes 1966088 | tf_op jit(solution)/shard_map/ppermute | solution.py:842
  410.9 11.2 %collective-permute-start.35 = (bf16[128,2560]{1,0:T(8,128)(2,1)S(1)}, bf16[128,2560]{1,0:T(8,128)(2,1)S(1)}, u32[]{:S(2)}, u32[]{:S(2)}) collective-permute-start(bf16[128,2560]{1,0:T(8,128)(2,1)S(1)} %collective-permute-done.33), channel_id=1, source_target_pairs={{1,2},{2,3},{5,6},{6,7},{9,10},{10,11},{13,14},{14,15},{17,18},{18... | collective-permute-start | bytes 1966088 | tf_op jit(solution)/shard_map/ppermute | solution.py:841
  411.6 25.3 %collective-permute-start.36 = (bf16[128,2560]{1,0:T(8,128)(2,1)S(1)}, bf16[128,2560]{1,0:T(8,128)(2,1)}, u32[]{:S(2)}, u32[]{:S(2)}) collective-permute-start(bf16[128,2560]{1,0:T(8,128)(2,1)S(1)} %collective-permute-done.34), channel_id=1, source_target_pairs={{1,0},{2,1},{5,4},{6,5},{9,8},{10,9},{13,12},{14,13},{17,16},{18,1... | collective-permute-start | bytes 1966088 | tf_op jit(solution)/shard_map/ppermute | solution.py:842
  436.9 307.7 %all-reduce.5.cloned.1.call-start = ((), (), s32[]{:S(2)}) async-start(), calls=%async_computation.9 | async-start | bytes 4792320 | tf_op jit(solution)/shard_map/psum | solution.py:1234
  442.8 24.1 %collective-permute-start.37 = (bf16[128,2560]{1,0:T(8,128)(2,1)}, bf16[128,2560]{1,0:T(8,128)(2,1)S(1)}, u32[]{:S(2)}, u32[]{:S(2)}) collective-permute-start(bf16[128,2560]{1,0:T(8,128)(2,1)} %copy-done.35), channel_id=1, source_target_pairs={{2,3},{6,7},{10,11},{14,15},{18,19},{22,23},{26,27},{30,31}} | collective-permute-start | bytes 1966088 | tf_op jit(solution)/shard_map/ppermute | solution.py:841
  443.7 23.3 %collective-permute-start.38 = (bf16[128,2560]{1,0:T(8,128)(2,1)}, bf16[128,2560]{1,0:T(8,128)(2,1)S(1)}, u32[]{:S(2)}, u32[]{:S(2)}) collective-permute-start(bf16[128,2560]{1,0:T(8,128)(2,1)} %collective-permute-done.36), channel_id=1, source_target_pairs={{1,0},{5,4},{9,8},{13,12},{17,16},{21,20},{25,24},{29,28}} | collective-permute-start | bytes 1966088 | tf_op jit(solution)/shard_map/ppermute | solution.py:842
  467.0 38.4 %collective-permute-start.39 = (bf16[128,2560]{1,0:T(8,128)(2,1)}, bf16[128,2560]{1,0:T(8,128)(2,1)}, u32[]{:S(2)}, u32[]{:S(2)}) collective-permute-start(bf16[128,2560]{1,0:T(8,128)(2,1)} %get-tuple-element.222), channel_id=1, source_target_pairs={{0,1},{1,2},{2,3},{4,5},{5,6},{6,7},{8,9},{9,10},{10,11},{12,13},{... | collective-permute-start | bytes 1966088 | tf_op jit(solution)/shard_map/ppermute | solution.py:841
  472.4 33.0 %collective-permute-start.40 = (bf16[128,2560]{1,0:T(8,128)(2,1)}, bf16[128,2560]{1,0:T(8,128)(2,1)S(1)}, u32[]{:S(2)}, u32[]{:S(2)}) collective-permute-start(bf16[128,2560]{1,0:T(8,128)(2,1)} %get-tuple-element.222), channel_id=1, source_target_pairs={{1,0},{2,1},{3,2},{5,4},{6,5},{7,6},{9,8},{10,9},{11,10},{13,12},{... | collective-permute-start | bytes 1966088 | tf_op jit(solution)/shard_map/ppermute | solution.py:842
  505.4 32.6 %collective-permute-start.41 = (bf16[256,2560]{1,0:T(8,128)(2,1)}, bf16[256,2560]{1,0:T(8,128)(2,1)}, u32[]{:S(2)}, u32[]{:S(2)}) collective-permute-start(bf16[256,2560]{1,0:T(8,128)(2,1)} %get-tuple-element.227), channel_id=1, source_target_pairs={{0,1},{4,5},{8,9},{12,13},{16,17},{20,21},{24,25},{28,29}} | collective-permute-start | bytes 3932168 | tf_op jit(solution)/shard_map/ppermute | solution.py:906
  511.5 26.4 %collective-permute-start.42 = (bf16[256,2560]{1,0:T(8,128)(2,1)}, bf16[256,2560]{1,0:T(8,128)(2,1)}, u32[]{:S(2)}, u32[]{:S(2)}) collective-permute-start(bf16[256,2560]{1,0:T(8,128)(2,1)} %get-tuple-element.228), channel_id=1, source_target_pairs={{3,2},{7,6},{11,10},{15,14},{19,18},{23,22},{27,26},{31,30}} | collective-permute-start | bytes 3932168 | tf_op jit(solution)/shard_map/ppermute | solution.py:908
  514.7 17.4 %collective-permute-start.44 = (bf16[128,2560]{1,0:T(8,128)(2,1)S(1)}, bf16[128,2560]{1,0:T(8,128)(2,1)}, u32[]{:S(2)}, u32[]{:S(2)}) collective-permute-start(bf16[128,2560]{1,0:T(8,128)(2,1)S(1)} %collective-permute-done.40), channel_id=1, source_target_pairs={{1,0},{2,1},{5,4},{6,5},{9,8},{10,9},{13,12},{14,13},{17,16},{18,1... | collective-permute-start | bytes 1966088 | tf_op jit(solution)/shard_map/ppermute | solution.py:842
  537.9 11.0 %collective-permute-start.47 = (bf16[128,2560]{1,0:T(8,128)(2,1)}, bf16[128,2560]{1,0:T(8,128)(2,1)S(1)}, u32[]{:S(2)}, u32[]{:S(2)}) collective-permute-start(bf16[128,2560]{1,0:T(8,128)(2,1)} %collective-permute-done.43), channel_id=1, source_target_pairs={{2,3},{6,7},{10,11},{14,15},{18,19},{22,23},{26,27},{30,31}} | collective-permute-start | bytes 1966088 | tf_op jit(solution)/shard_map/ppermute | solution.py:841
  538.6 37.7 %collective-permute-start.48 = (bf16[128,2560]{1,0:T(8,128)(2,1)}, bf16[128,2560]{1,0:T(8,128)(2,1)S(1)}, u32[]{:S(2)}, u32[]{:S(2)}) collective-permute-start(bf16[128,2560]{1,0:T(8,128)(2,1)} %collective-permute-done.44), channel_id=1, source_target_pairs={{1,0},{5,4},{9,8},{13,12},{17,16},{21,20},{25,24},{29,28}} | collective-permute-start | bytes 1966088 | tf_op jit(solution)/shard_map/ppermute | solution.py:842
  543.3 30.9 %collective-permute-start.45 = (bf16[256,2560]{1,0:T(8,128)(2,1)S(1)}, bf16[256,2560]{1,0:T(8,128)(2,1)S(1)}, u32[]{:S(2)}, u32[]{:S(2)}) collective-permute-start(bf16[256,2560]{1,0:T(8,128)(2,1)S(1)} %get-tuple-element.231), channel_id=1, source_target_pairs={{0,1},{1,2},{4,5},{5,6},{8,9},{9,10},{12,13},{13,14},{16,17},{17,1... | collective-permute-start | bytes 3932168 | tf_op jit(solution)/shard_map/ppermute | solution.py:906
  548.2 26.0 %collective-permute-start.46 = (bf16[256,2560]{1,0:T(8,128)(2,1)S(1)}, bf16[256,2560]{1,0:T(8,128)(2,1)S(1)}, u32[]{:S(2)}, u32[]{:S(2)}) collective-permute-start(bf16[256,2560]{1,0:T(8,128)(2,1)S(1)} %get-tuple-element.232), channel_id=1, source_target_pairs={{3,2},{2,1},{7,6},{6,5},{11,10},{10,9},{15,14},{14,13},{19,18},{18... | collective-permute-start | bytes 3932168 | tf_op jit(solution)/shard_map/ppermute | solution.py:908
  576.3 41.2 %collective-permute-start.49 = (bf16[256,2560]{1,0:T(8,128)(2,1)}, bf16[256,2560]{1,0:T(8,128)(2,1)}, u32[]{:S(2)}, u32[]{:S(2)}) collective-permute-start(bf16[256,2560]{1,0:T(8,128)(2,1)} %get-tuple-element.235), channel_id=1, source_target_pairs={{0,1},{1,2},{2,3},{4,5},{5,6},{6,7},{8,9},{9,10},{10,11},{12,13},{... | collective-permute-start | bytes 3932168 | tf_op jit(solution)/shard_map/ppermute | solution.py:906
  583.9 33.6 %collective-permute-start.50 = (bf16[256,2560]{1,0:T(8,128)(2,1)}, bf16[256,2560]{1,0:T(8,128)(2,1)}, u32[]{:S(2)}, u32[]{:S(2)}) collective-permute-start(bf16[256,2560]{1,0:T(8,128)(2,1)} %get-tuple-element.236), channel_id=1, source_target_pairs={{3,2},{2,1},{1,0},{7,6},{6,5},{5,4},{11,10},{10,9},{9,8},{15,14},{... | collective-permute-start | bytes 3932168 | tf_op jit(solution)/shard_map/ppermute | solution.py:908
  622.8 205.5 %reduce-scatter.11.cloned.1.call-start = ((), (), s32[]{:S(2)}) async-start(), calls=%async_computation.10 | async-start | bytes 6635520 | tf_op jit(solution)/shard_map/reduce_scatter | solution.py:1254
  624.3 122.2 %collective-permute-start.51 = (bf16[256,2560]{1,0:T(8,128)(2,1)}, bf16[256,2560]{1,0:T(8,128)(2,1)}, u32[]{:S(2)}, u32[]{:S(2)}) collective-permute-start(bf16[256,2560]{1,0:T(8,128)(2,1)} %fusion.2), channel_id=1, source_target_pairs={{0,1},{1,2},{2,3},{4,5},{5,6},{6,7},{8,9},{9,10},{10,11},{12,13},{... | collective-permute-start | bytes 3932168 | tf_op jit(solution)/shard_map/ppermute | solution.py:841
  629.8 116.7 %collective-permute-start.52 = (bf16[256,2560]{1,0:T(8,128)(2,1)}, bf16[256,2560]{1,0:T(8,128)(2,1)}, u32[]{:S(2)}, u32[]{:S(2)}) collective-permute-start(bf16[256,2560]{1,0:T(8,128)(2,1)} %fusion.2), channel_id=1, source_target_pairs={{1,0},{2,1},{3,2},{5,4},{6,5},{7,6},{9,8},{10,9},{11,10},{13,12},{... | collective-permute-start | bytes 3932168 | tf_op jit(solution)/shard_map/ppermute | solution.py:842
  746.5 37.1 %collective-permute-start.53 = (bf16[256,2560]{1,0:T(8,128)(2,1)}, bf16[256,2560]{1,0:T(8,128)(2,1)}, u32[]{:S(2)}, u32[]{:S(2)}) collective-permute-start(bf16[256,2560]{1,0:T(8,128)(2,1)} %collective-permute-done.51), channel_id=1, source_target_pairs={{1,2},{2,3},{5,6},{6,7},{9,10},{10,11},{13,14},{14,15},{17,18},{18... | collective-permute-start | bytes 3932168 | tf_op jit(solution)/shard_map/ppermute | solution.py:841
  748.2 35.4 %collective-permute-start.54 = (bf16[256,2560]{1,0:T(8,128)(2,1)}, bf16[256,2560]{1,0:T(8,128)(2,1)}, u32[]{:S(2)}, u32[]{:S(2)}) collective-permute-start(bf16[256,2560]{1,0:T(8,128)(2,1)} %collective-permute-done.52), channel_id=1, source_target_pairs={{1,0},{2,1},{5,4},{6,5},{9,8},{10,9},{13,12},{14,13},{17,16},{18,1... | collective-permute-start | bytes 3932168 | tf_op jit(solution)/shard_map/ppermute | solution.py:842
  774.6 11.4 %collective-permute-start.57 = (bf16[2,2,96,1056]{3,2,1,0:T(8,128)(2,1)S(1)}, bf16[2,2,96,1056]{3,2,1,0:T(8,128)(2,1)S(1)}, u32[]{:S(2)}, u32[]{:S(2)}) collective-permute-start(bf16[2,2,96,1056]{3,2,1,0:T(8,128)(2,1)S(1)} %fusion.19), channel_id=1, source_target_pairs={{0,4},{4,0},{8,12},{12,8},{16,20},{20,16},{24,28},{28,24},{1,5},{5... | collective-permute-start | bytes 2433032 | tf_op jit(solution)/shard_map/ppermute | solution.py:973
  783.7 29.6 %collective-permute-start.55 = (bf16[256,2560]{1,0:T(8,128)(2,1)}, bf16[256,2560]{1,0:T(8,128)(2,1)S(1)}, u32[]{:S(2)}, u32[]{:S(2)}) collective-permute-start(bf16[256,2560]{1,0:T(8,128)(2,1)} %collective-permute-done.53), channel_id=1, source_target_pairs={{2,3},{6,7},{10,11},{14,15},{18,19},{22,23},{26,27},{30,31}} | collective-permute-start | bytes 3932168 | tf_op jit(solution)/shard_map/ppermute | solution.py:841
  784.5 34.5 %collective-permute-start.56 = (bf16[256,2560]{1,0:T(8,128)(2,1)}, bf16[256,2560]{1,0:T(8,128)(2,1)}, u32[]{:S(2)}, u32[]{:S(2)}) collective-permute-start(bf16[256,2560]{1,0:T(8,128)(2,1)} %collective-permute-done.54), channel_id=1, source_target_pairs={{1,0},{5,4},{9,8},{13,12},{17,16},{21,20},{25,24},{29,28}} | collective-permute-start | bytes 3932168 | tf_op jit(solution)/shard_map/ppermute | solution.py:842
  787.0 23.3 %collective-permute-start.58 = (bf16[2,96,1056]{2,1,0:T(8,128)(2,1)}, bf16[2,96,1056]{2,1,0:T(8,128)(2,1)}, u32[]{:S(2)}, u32[]{:S(2)}) collective-permute-start(bf16[2,96,1056]{2,1,0:T(8,128)(2,1)} %dynamic-slice_bitcast_fusion.2), channel_id=1, source_target_pairs={{0,8},{4,12},{8,0},{12,4},{16,24},{20,28},{24,16},{28,20},{1,9},{5... | collective-permute-start | bytes 1216520 | tf_op jit(solution)/shard_map/ppermute | solution.py:973
  811.6 14.2 %collective-permute-start.59 = (bf16[96,1056]{1,0:T(8,128)(2,1)S(1)}, bf16[96,1056]{1,0:T(8,128)(2,1)S(1)}, u32[]{:S(2)}, u32[]{:S(2)}) collective-permute-start(bf16[96,1056]{1,0:T(8,128)(2,1)S(1)} %dynamic-slice_bitcast_fusion.3), channel_id=1, source_target_pairs={{0,16},{4,20},{8,24},{12,28},{16,0},{20,4},{24,8},{28,12},{1,17},{... | collective-permute-start | bytes 608264 | tf_op jit(solution)/shard_map/ppermute | solution.py:973
  (64 other events, 652.5 us)
Sparse Core Ops, SparseCore 0:
  13.6 157.5 all-gather.2
  173.7 74.3 all-gather.4
  301.5 55.1 reduce-scatter.4
  358.9 66.0 reduce-scatter.6
  437.0 158.0 reduce-scatter.8
  622.9 121.7 all-reduce.4
  748.1 60.5 reduce-scatter.10

commit v2 on v1

--- a/solution.py
+++ b/solution.py
@@ -257,6 +257,31 @@
     )(queries, keys, values, grad_mixed, lse, cosines, sines, *seeds)
 
 
+def update_rates():
+    return [
+        (0.25, 0.0),
+        (2.5 / math.sqrt(D), DECAY_RATE),
+        (2.5 / math.sqrt(D), DECAY_RATE),
+        (2.5 / math.sqrt(QR), DECAY_RATE),
+        (2.5 / math.sqrt(KVR), DECAY_RATE),
+        (1.75, DECAY_RATE),
+        (2.5 / math.sqrt(D), DECAY_RATE),
+        (2.5 / math.sqrt(D), DECAY_RATE),
+        (0.375, DECAY_RATE),
+    ]
+
+
+def adam_step(weight, gradient, first, second, rate_pair):
+    first_new = BETA_ONE * first + (1.0 - BETA_ONE) * gradient
+    second_new = BETA_TWO * second + (1.0 - BETA_TWO) * gradient * gradient
+    first_hat = first_new / (1.0 - BETA_ONE**STEP)
+    second_hat = second_new / (1.0 - BETA_TWO**STEP)
+    weight_new = weight - rate_pair[0] * (
+        first_hat / (jnp.sqrt(second_hat) + ADAM_EPS) + rate_pair[1] * weight
+    )
+    return (first_new, second_new, weight_new)
+
+
 def hidden_kernel(grad_ref, weight_ref, out_ref):
     weight = weight_ref[...].reshape(-1, weight_ref.shape[3])
 
@@ -785,29 +810,31 @@
     )(mid_norm, cotangent, out_own)
 
 
-def update_rates():
-    return [
-        (0.25, 0.0),
-        (2.5 / math.sqrt(D), DECAY_RATE),
-        (2.5 / math.sqrt(D), DECAY_RATE),
-        (2.5 / math.sqrt(QR), DECAY_RATE),
-        (2.5 / math.sqrt(KVR), DECAY_RATE),
-        (1.75, DECAY_RATE),
-        (2.5 / math.sqrt(D), DECAY_RATE),
-        (2.5 / math.sqrt(D), DECAY_RATE),
-        (0.375, DECAY_RATE),
-    ]
-
-
-def adam_step(weight, gradient, first, second, rate_pair):
-    first_new = BETA_ONE * first + (1.0 - BETA_ONE) * gradient
-    second_new = BETA_TWO * second + (1.0 - BETA_TWO) * gradient * gradient
-    first_hat = first_new / (1.0 - BETA_ONE**STEP)
-    second_hat = second_new / (1.0 - BETA_TWO**STEP)
-    weight_new = weight - rate_pair[0] * (
-        first_hat / (jnp.sqrt(second_hat) + ADAM_EPS) + rate_pair[1] * weight
-    )
-    return (first_new, second_new, weight_new)
+def adam_kernel(rate_pair, weight_ref, grad_ref, first_ref, second_ref, first_out, second_out, weight_out):
+    gradient = grad_ref[...].astype(jnp.float32)
+    updates = adam_step(weight_ref[...], gradient, first_ref[...], second_ref[...], rate_pair)
+    first_out[...], second_out[...], weight_out[...] = updates
+
+
+def adam_rows(weight, grads, slot, first, second, rate_pair):
+    rows, cols = weight.shape
+    block = pl.BlockSpec((rows // 5, cols), lambda i: (i, 0))
+    shape = jax.ShapeDtypeStruct((rows, cols), jnp.float32)
+    return pl.pallas_call(
+        functools.partial(adam_kernel, rate_pair),
+        grid=(5,),
+        in_specs=[
+            block,
+            pl.BlockSpec((rows // 5, cols), lambda i: (5 * slot + i, 0)),
+            block,
+            block,
+        ],
+        out_specs=[block, block, block],
+        out_shape=[shape, shape, shape],
+        compiler_params=kernel_params(),
+        cost_estimate=light(rows * cols),
+        name="adam_rows",
+    )(weight, grads, first, second)
 
 
 def wide(value):
@@ -1171,18 +1198,20 @@
     clock.move(mid_flow[1])
     grad_gate[1] = clock.wait(grad_gate[1])
     held = ffn_outer(pairs(normed_mid), (0, 0), pairs(grad_gate), n_data, 0, None)
+    grad_up[1] = after(grad_up[1], out_own)
     held = ffn_outer(pairs(normed_mid), (0, 0), pairs(grad_up), n_data, 1, held)
     ffn_grads, mark = ffn_outer([grad_ffn, grad_ffn], order, pairs(hidden), n_data, 2, held)
     clock.tick(mark)
     clock.move(mid_flow[1])
     ffn_term = {}
-    ffn_term[1] = ffn_back([clock.wait(hidden[1])], ffn_all, 2)
-    clock.tick(ffn_term[1])
+    for half in order:
+        ffn_term[half] = ffn_back([clock.wait(hidden[half])], ffn_all, 2)
+    clock.tick(ffn_term[1], ffn_term[0])
     clock.move(mid_flow[1])
-    ffn_term[0] = ffn_back([clock.wait(hidden[0])], ffn_all, 2)
+    ffn_term = jnp.concatenate([clock.wait(ffn_term[0]), ffn_term[1]], axis=0)
     mid_own[0] = clock.wait(mid_own[0])
     mid_back(0)
-    clock.tick(ffn_term[0], mid_flow[0].own)
+    clock.tick(ffn_term, mid_flow[0].own)
     ffn_grads = after(ffn_grads, mid_own[0])
     ffn_sum = lax.psum_scatter(ffn_grads.reshape(-1, hidden_dev), "dp", scatter_dimension=0, tiled=True)
     resid_all = jnp.concatenate([resid_mid[0], resid_mid[1]], axis=0)
@@ -1213,7 +1242,7 @@
     mixed_back(1)
     seeds = heads_back(1)
     clock.tick(grad_rope[1])
-    out_flow = Scatter(jnp.concatenate(both(ffn_term), axis=0), n_model)
+    out_flow = Scatter(ffn_term, n_model)
     clock.move(mid_flow[0], out_flow)
     clock.tick()
     clock.move(mid_flow[0], out_flow)
@@ -1239,18 +1268,23 @@
 
     output_own = (wide_rows(resid_all) + RESID_SCALE * ffn_own).astype(low_type)
     output_flow = Gather(output_own, n_model, 0)
-    output_flow.advance(clock.gate)
+    arrived = output_flow.advance(clock.gate)
     output_flow.advance(tie)
     head_grads = heads_outer(
         both(grad_attn),
         both(mixed),
         both(grad_q_heads),
         both(grad_kv_heads),
-        clock.wait(q_normed),
+        after(q_normed, *arrived),
         kv_normed,
         n_data,
         mark,
     )
+    ffn_rates = update_rates()[6:]
+    ffn_late = after(ffn_sum, *arrived)
+    gate_updates = adam_rows(ffn_gate, ffn_late, 0, ffn_gate_first, ffn_gate_second, ffn_rates[0])
+    up_updates = adam_rows(ffn_up, ffn_late, 1, ffn_up_first, ffn_up_second, ffn_rates[1])
+    latents_sum = after(latents_sum, head_grads, gate_updates[2], up_updates[2])
     head_sum = lax.psum_scatter(
         after(head_grads, latents_sum).reshape(-1, up_width), "dp", scatter_dimension=0, tiled=True
     )
@@ -1294,7 +1328,13 @@
     clock.tick(input_grad)
     clock.move(down_flow)
     down_sum = wide(down_flow.result())
-    ffn_parts = ffn_sum.reshape(3, -1, hidden_dev)
+    down_rate = ffn_rates[2]
+    down_part = ffn_sum.reshape(3, -1, hidden_dev)[2].T
+    ffn_updated = [
+        gate_updates,
+        up_updates,
+        adam_step(ffn_down, wide(down_part), ffn_down_first, ffn_down_second, down_rate),
+    ]
     reduced = (
         down_sum[down_rows, :gain_count],
         down_sum[:down_rows, :QR],
@@ -1304,9 +1344,6 @@
         wide(
             jnp.concatenate([head_sum[:out_rows, :out_width], head_sum[:out_rows, out_width:]], axis=0).T
         ),
-        wide(ffn_parts[0]),
-        wide(ffn_parts[1]),
-        wide(ffn_parts[2].T),
     )
     weights = (
         norm_gains,
@@ -1344,8 +1381,8 @@
     rates = update_rates()
     updated = [
         adam_step(weights[number], reduced[number], firsts[number], seconds[number], rates[number])
-        for number in range(9)
-    ]
+        for number in range(6)
+    ] + ffn_updated
     return (
         output,
         input_grad,

time: 849 us -> 834 us (0.982)
  waiting for transfers between devices: 272 us -> 256 us
  Pallas kernels: 311 us -> 325 us
    psum x1, waiting for transfers between devices: 98.3 us -> 18.3 us  [local(): latents_sum = lax.psum(after(part_latents, ffn_sum), 'mp')]
    ppermute x18, waiting for transfers between devices: 3.21 us -> 52.9 us  [advance(): self.below.append(lax.ppermute(up, 'mp', ups))]
    pallas_call x0 -> x2, Pallas kernels: none -> 15.5 us  [adam_rows(): pl.pallas_call(functools.partial(adam_kernel, rate_pair), grid=(5,), in_s...]
    ppermute x18, waiting for transfers between devices: 72.3 us -> 87.1 us  [advance(): self.above.append(lax.ppermute(down, 'mp', downs))]
    sub x8 -> x7, other arithmetic: 20.1 us -> 13.2 us  [adam_step(): weight - rate_pair[0] * (first_hat / (jnp.sqrt(second_hat) + ADAM_EPS) +...]
    unnamed x158 -> x144, local copies, waits for them, and re-layouts: 23.7 us -> 22.4 us
  transfers between devices with their start and end apart: 67 -> 67, of which waited for: 20 -> 23; matrix products, arithmetic and copies ran while one was open for 14% -> 13% of each run, Pallas kernels for 37% -> 39%
where the time goes in v2:
time: 834 us; the launch traced here: 828 us
  Pallas kernels  325 us (39%)
  waiting for transfers between devices  256 us (31%)
  starting transfers between devices  95 us (11%)
  other arithmetic  76.1 us (9%)
  local copies, waits for them, and re-layouts  37.5 us (4%)
  matrix products  21.7 us (3%)
  between operations  16.4 us (2%)
    ppermute x18, waiting for transfers between devices, advance(): self.above.append(lax.ppermute(down, 'mp', downs))  87.1 us
    ppermute x18, waiting for transfers between devices, advance(): self.below.append(lax.ppermute(up, 'mp', ups))  52.9 us
    ppermute x12, waiting for transfers between devices, advance(): came.append(lax.ppermute(part, 'dp', pairs))  50.7 us
    pallas_call x4, Pallas kernels, ffn_back(): pl.pallas_call(functools.partial(back_kernel, count), grid=(2, tokens //...  48.7 us
    pallas_call x3, Pallas kernels, ffn_outer(): pl.pallas_call(functools.partial(outer_kernel, count), grid=(2,), in_spec...  44.4 us
    pallas_call x2, Pallas kernels, ffn_inner(): pl.pallas_call(inner_kernel, grid=(steps, 2, 2), in_specs=[pl.BlockSpec((...  39.1 us
    pallas_call x2, Pallas kernels, attend_backward(): pl.pallas_call(functools.partial(backward_kernel, half * size // BLK, hal...  36.2 us
    ppermute x3, waiting for transfers between devices, advance(): self.below = lax.ppermute(up, 'mp', [(k, k + 1) for k in range(step)])  29.4 us
  transfers between devices with their start and end apart: 67, of which 23 were waited for; matrix products, arithmetic and copies ran while one was open for 13% of the time, Pallas kernels for 39%

profile of v2, /device:TPU:0, one launch (start us, length us, event | category | flops | bytes accessed | tf_op | source)
XLA Modules:
  0.0 827.7 jit_solution(13946801233308420447)
XLA Ops:
  14.4 5.1 collective-permute-start.2
  20.8 3.8 collective-permute-done.2
  24.6 10.6 %collective-permute-done.1 = bf16[80,1056]{1,0:T(8,128)(2,1)S(1)} collective-permute-done((bf16[80,1056]{1,0:T(8,128)(2,1)S(1)}, bf16[80,1056]{1,0:T(8,128)(2,1)S(1)}, u32[]{:S(2)}, u32[]{:S(2)}) %collective-permute-start.1) | collective-permute-done | bytes 168992 | tf_op jit(solution)/shard_map/ppermute | solution.py:898
  39.7 2.8 collective-permute-start.7
  42.5 5.6 collective-permute-done.4
  49.5 13.8 %collective-permute-done.6 = bf16[1,160,1056]{2,1,0:T(8,128)(2,1)S(1)} collective-permute-done((bf16[1,160,1056]{2,1,0:T(8,128)(2,1)S(1)}, bf16[1,160,1056]{2,1,0:T(8,128)(2,1)S(1)}, u32[]{:S(2)}, u32[]{:S(2)}) %collective-permute-start.6) | collective-permute-done | bytes 337952 | tf_op jit(solution)/shard_map/ppermute | solution.py:964
  68.9 14.0 %collective-permute-done.9 = bf16[2,72,1280]{2,1,0:T(8,128)(2,1)} collective-permute-done((bf16[2,72,1280]{2,1,0:T(8,128)(2,1)S(1)}, bf16[2,72,1280]{2,1,0:T(8,128)(2,1)}, u32[]{:S(2)}, u32[]{:S(2)}) %collective-permute-start.9) | collective-permute-done | bytes 368672 | tf_op jit(solution)/shard_map/ppermute | solution.py:964
  83.5 15.8 %collective-permute-done.10 = bf16[2,72,1280]{2,1,0:T(8,128)(2,1)} collective-permute-done((bf16[2,72,1280]{2,1,0:T(8,128)(2,1)S(1)}, bf16[2,72,1280]{2,1,0:T(8,128)(2,1)}, u32[]{:S(2)}, u32[]{:S(2)}) %collective-permute-start.10) | collective-permute-done | bytes 368672 | tf_op jit(solution)/shard_map/ppermute | solution.py:964
  103.5 10.4 %collective-permute-done.28 = bf16[320,640]{1,0:T(8,128)(2,1)} collective-permute-done((bf16[320,640]{1,0:T(8,128)(2,1)}, bf16[320,640]{1,0:T(8,128)(2,1)}, u32[]{:S(2)}, u32[]{:S(2)}) %collective-permute-start.28) | collective-permute-done | bytes 409632 | tf_op jit(solution)/shard_map/ppermute | solution.py:869
  139.4 2.5 copy-done
  141.9 13.8 %latents_forward.1 = (bf16[1024,2560]{1,0:T(8,128)(2,1)}, f32[1024,1056]{1,0:T(8,128)}, bf16[1024,768]{1,0:T(8,128)(2,1)}, bf16[1024,256]{1,0:T(8,128)(2,1)}, bf16[32,1024]{1,0:T(8,128)(2,1)}) custom-call(bf16[1024,2560]{1,0:T(8,128)(2,1)} %inputs_ref.3, f32[1,2560]{1,0:T(1,128)} %broadcast_in_dim.45.gain_in.gain_ref, bf16[2560,1056]{1,0:T(8,128)(2,1)} %copy-done, ...), custom_call_target="tpu_custom_call" | custom-call | flops 27682 | bytes 1024 | tf_op jit(solution)/shard_map/latents_forward/pallas_call | solution.py:628
  155.7 6.9 heads_forward.1
  162.6 14.6 %attend_forward.2 = (bf16[10,64,512]{2,1,0:T(8,128)(2,1)}, f32[10,1,512]{2,1,0:T(1,128)}) custom-call(bf16[10,96,1024]{2,1,0:T(8,128)(2,1)} %get-tuple-element.184.q_ref.refs_0_, bf16[10,96,1024]{2,1,0:T(8,128)(2,1)} %get-tuple-element.181.k_ref.refs_1_, bf16[10,64,1024]{2,1,0:T(8,128)(2,1)} %get-tuple-element.182.v_ref.refs_2_), custom_call_target="tpu_custom_call" | custom-call | flops 73400 | bytes 1024 | tf_op jit(solution)/shard_map/attend_forward/pallas_call | solution.py:120
  179.8 10.3 %attend_forward.3 = (bf16[10,64,512]{2,1,0:T(8,128)(2,1)}, f32[10,1,512]{2,1,0:T(1,128)}) custom-call(bf16[10,96,1024]{2,1,0:T(8,128)(2,1)} %get-tuple-element.184.q_ref.refs_0_, bf16[10,96,1024]{2,1,0:T(8,128)(2,1)} %get-tuple-element.181.k_ref.refs_1_, bf16[10,64,1024]{2,1,0:T(8,128)(2,1)} %get-tuple-element.182.v_ref.refs_2_), custom_call_target="tpu_custom_call" | custom-call | flops 36700 | bytes 1024 | tf_op jit(solution)/shard_map/attend_forward/pallas_call | solution.py:120
  190.1 3.2 collective-permute-done.19
  193.3 4.0 collective-permute-done.20
  199.6 3.3 multiply_convert_fusion.grad_ref.refs_0_.refs_1_
  202.9 17.6 %hidden_back.1.grad_ref = f32[1024,1600]{1,0:T(8,128)} custom-call(bf16[1024,2560]{1,0:T(8,128)(2,1)} %multiply_convert_fusion.grad_ref.refs_0_.refs_1_, bf16[8,3,320,1600]{3,2,1,0:T(8,128)(2,1)} %all-gather.3.cloned.1.call-done.weight_ref.refs_2_.refs_1_), custom_call_target="tpu_custom_call" | custom-call | flops 83886 | bytes 1024 | tf_op jit(solution)/shard_map/hidden_back/pallas_call | solution.py:300
  222.4 17.5 %collective-permute-done.24 = bf16[640,512]{1,0:T(8,128)(2,1)S(1)} collective-permute-done((bf16[640,512]{1,0:T(8,128)(2,1)S(1)}, bf16[640,512]{1,0:T(8,128)(2,1)S(1)}, u32[]{:S(2)}, u32[]{:S(2)}) %collective-permute-start.24) | collective-permute-done | bytes 655392 | tf_op jit(solution)/shard_map/ppermute | solution.py:869
  245.1 3.0 all-gather.5.cloned.1.call-done
  248.1 10.8 %multiply_reduce_fusion.1 = (f32[512]{0:T(512)S(1)}, f32[512,2560]{1,0:T(8,128)S(1)}) fusion(bf16[2560,512]{1,0:T(8,128)(2,1)S(1)} %pad_maximum_fusion.5, bf16[2560,2560]{1,0:T(8,128)(2,1)} %all-gather.5.cloned.1.call-done, bf16[1024,2560]{1,0:T(8,128)(2,1)} %inputs_ref.3), kind=kOutput, calls=%fused_computation.9 | convolution fusion | flops 6717439488 | bytes 23595008 | tf_op jit(solution)/shard_map/ht,dh->td/dot_general | solution.py:52
  264.5 19.5 %ffn_inner.2 = (bf16[512,1600]{1,0:T(8,128)(2,1)}, bf16[512,1600]{1,0:T(8,128)(2,1)}, bf16[512,1600]{1,0:T(8,128)(2,1)}) custom-call(bf16[512,2560]{1,0:T(8,128)(2,1)} %multiply_convert_fusion.2.normed_ref.refs_0_, f32[1024,1600]{1,0:T(8,128)} %hidden_back.1.grad_ref, bf16[8,3,320,1600]{3,2,1,0:T(8,128)(2,1)} %all-gather.3.cloned.1.call-done.weight_ref.refs_2_.refs_1_), custom_call_target="tpu_custom_call" | custom-call | flops 83886 | bytes 1024 | tf_op jit(solution)/shard_map/ffn_inner/pallas_call | solution.py:348
  286.1 15.3 %ffn_back.4 = bf16[512,2560]{1,0:T(8,128)(2,1)} custom-call(bf16[512,1600]{1,0:T(8,128)(2,1)} %get-tuple-element.217.refs_0_.refs_2_, bf16[512,1600]{1,0:T(8,128)(2,1)} %get-tuple-element.216.refs_1_.refs_2_, bf16[8,3,320,1600]{3,2,1,0:T(8,128)(2,1)} %all-gather.3.cloned.1.call-done.weight_ref.refs_2_.refs_1_), custom_call_target="tpu_custom_call" | custom-call | flops 167772 | bytes 1024 | tf_op jit(solution)/shard_map/ffn_back/pallas_call | solution.py:382
  301.7 4.1 collective-permute-done.32
  307.6 10.9 %multiply_reduce_fusion = (f32[512]{0:T(512)S(1)}, f32[512,2560]{1,0:T(8,128)S(1)}) fusion(bf16[2560,512]{1,0:T(8,128)(2,1)S(1)} %pad_maximum_fusion.6, bf16[2560,2560]{1,0:T(8,128)(2,1)} %all-gather.5.cloned.1.call-done, bf16[1024,2560]{1,0:T(8,128)(2,1)} %inputs_ref.3), kind=kOutput, calls=%fused_computation.6 | convolution fusion | flops 6717439488 | bytes 23595008 | tf_op jit(solution)/shard_map/ht,dh->td/dot_general | solution.py:52
  322.8 19.6 %ffn_inner.3 = (bf16[512,1600]{1,0:T(8,128)(2,1)}, bf16[512,1600]{1,0:T(8,128)(2,1)}, bf16[512,1600]{1,0:T(8,128)(2,1)}) custom-call(bf16[512,2560]{1,0:T(8,128)(2,1)} %multiply_convert_fusion.1.normed_ref.refs_1_, f32[1024,1600]{1,0:T(8,128)} %hidden_back.1.grad_ref, bf16[8,3,320,1600]{3,2,1,0:T(8,128)(2,1)} %all-gather.3.cloned.1.call-done.weight_ref.refs_2_.refs_1_), custom_call_target="tpu_custom_call" | custom-call | flops 83886 | bytes 1024 | tf_op jit(solution)/shard_map/ffn_inner/pallas_call | solution.py:348
  342.4 15.4 %ffn_back.5 = bf16[512,2560]{1,0:T(8,128)(2,1)} custom-call(bf16[512,1600]{1,0:T(8,128)(2,1)} %get-tuple-element.212.refs_0_.refs_3_, bf16[512,1600]{1,0:T(8,128)(2,1)} %get-tuple-element.211.refs_1_.refs_3_, bf16[8,3,320,1600]{3,2,1,0:T(8,128)(2,1)} %all-gather.3.cloned.1.call-done.weight_ref.refs_2_.refs_1_), custom_call_target="tpu_custom_call" | custom-call | flops 167772 | bytes 1024 | tf_op jit(solution)/shard_map/ffn_back/pallas_call | solution.py:382
  358.4 3.2 middle_back.2
  361.6 3.4 collective-permute-start.33
  368.5 4.1 copy.75
  372.5 14.8 %ffn_outer.3 = (bf16[8,3,320,1600]{3,2,1,0:T(8,128)(2,1)}, f32[8,128]{1,0:T(8,128)}) custom-call(bf16[512,2560]{1,0:T(8,128)(2,1)} %multiply_convert_fusion.2.normed_ref.refs_0_, bf16[512,2560]{1,0:T(8,128)(2,1)} %multiply_convert_fusion.1.normed_ref.refs_1_, bf16[512,1600]{1,0:T(8,128)(2,1)} %get-tuple-element.217.refs_0_.refs_2_, ...), custom_call_target="tpu_custom_call" | custom-call | flops 167772 | bytes 1024 | tf_op jit(solution)/shard_map/ffn_outer/pallas_call | solution.py:412
  387.3 14.7 %ffn_outer.4 = (bf16[8,3,320,1600]{3,2,1,0:T(8,128)(2,1)}, f32[8,128]{1,0:T(8,128)}) custom-call(bf16[512,2560]{1,0:T(8,128)(2,1)} %multiply_convert_fusion.2.normed_ref.refs_0_, bf16[512,2560]{1,0:T(8,128)(2,1)} %multiply_convert_fusion.1.normed_ref.refs_1_, bf16[512,1600]{1,0:T(8,128)(2,1)} %get-tuple-element.216.refs_1_.refs_2_, ...), custom_call_target="tpu_custom_call", output_to_operand_aliasing={{0}: (4, {})} | custom-call | flops 167772 | bytes 1024 | tf_op jit(solution)/shard_map/ffn_outer/pallas_call | solution.py:412
  402.0 14.9 %ffn_outer.5 = (bf16[8,3,320,1600]{3,2,1,0:T(8,128)(2,1)}, f32[8,128]{1,0:T(8,128)}) custom-call(bf16[1024,2560]{1,0:T(8,128)(2,1)} %multiply_convert_fusion.grad_ref.refs_0_.refs_1_, bf16[1024,2560]{1,0:T(8,128)(2,1)} %multiply_convert_fusion.grad_ref.refs_0_.refs_1_, ...), custom_call_target="tpu_custom_call", output_to_operand_aliasing={{0}: (4, {})} | custom-call | flops 167772 | bytes 1024 | tf_op jit(solution)/shard_map/ffn_outer/pallas_call | solution.py:412
  419.2 9.0 %ffn_back.7 = bf16[512,2560]{1,0:T(8,128)(2,1)} custom-call(bf16[512,1600]{1,0:T(8,128)(2,1)} %get-tuple-element.226.refs_2_.refs_0_, bf16[8,3,320,1600]{3,2,1,0:T(8,128)(2,1)} %all-gather.3.cloned.1.call-done.weight_ref.refs_2_.refs_1_), custom_call_target="tpu_custom_call" | custom-call | flops 83886 | bytes 1024 | tf_op jit(solution)/shard_map/ffn_back/pallas_call | solution.py:382
  428.2 9.0 %ffn_back.6 = bf16[512,2560]{1,0:T(8,128)(2,1)} custom-call(bf16[512,1600]{1,0:T(8,128)(2,1)} %get-tuple-element.223.refs_3_.refs_0_, bf16[8,3,320,1600]{3,2,1,0:T(8,128)(2,1)} %all-gather.3.cloned.1.call-done.weight_ref.refs_2_.refs_1_), custom_call_target="tpu_custom_call" | custom-call | flops 83886 | bytes 1024 | tf_op jit(solution)/shard_map/ffn_back/pallas_call | solution.py:382
  447.3 3.7 middle_back.3
  451.0 8.9 %collective-permute-done.38 = bf16[128,2560]{1,0:T(8,128)(2,1)S(1)} collective-permute-done((bf16[128,2560]{1,0:T(8,128)(2,1)}, bf16[128,2560]{1,0:T(8,128)(2,1)S(1)}, u32[]{:S(2)}, u32[]{:S(2)}) %collective-permute-start.38) | collective-permute-done | bytes 655392 | tf_op jit(solution)/shard_map/ppermute | solution.py:869
  467.5 7.4 mixed_gradient.2
  474.9 22.4 %attend_backward.2 = (bf16[10,96,512]{2,1,0:T(8,128)(2,1)}, bf16[10,128,512]{2,1,0:T(8,128)(2,1)}, f32[32,512]{1,0:T(8,128)}, f32[10,96,512]{2,1,0:T(8,128)}, f32[10,64,512]{2,1,0:T(8,128)}) custom-call(bf16[10,96,1024]{2,1,0:T(8,128)(2,1)} %get-tuple-element.184.q_ref.refs_0_, bf16[10,96,1024]{2,1,0:T(8,128)(2,1)} %get-tuple-element.181.k_ref.refs_1_, ...), custom_call_target="tpu_custom_call" | custom-call | flops 157286 | bytes 1024 | tf_op jit(solution)/shard_map/attend_backward/pallas_call | solution.py:242
  497.3 5.6 collective-permute-start.41
  507.5 15.1 %collective-permute-done.44 = bf16[128,2560]{1,0:T(8,128)(2,1)} collective-permute-done((bf16[128,2560]{1,0:T(8,128)(2,1)S(1)}, bf16[128,2560]{1,0:T(8,128)(2,1)}, u32[]{:S(2)}, u32[]{:S(2)}) %collective-permute-start.44) | collective-permute-done | bytes 655392 | tf_op jit(solution)/shard_map/ppermute | solution.py:869
  522.7 5.8 collective-permute-done.41
  530.5 3.7 fusion.4
  534.2 4.5 collective-permute-start.45
  540.2 23.6 %collective-permute-done.45 = bf16[256,2560]{1,0:T(8,128)(2,1)S(1)} collective-permute-done((bf16[256,2560]{1,0:T(8,128)(2,1)S(1)}, bf16[256,2560]{1,0:T(8,128)(2,1)S(1)}, u32[]{:S(2)}, u32[]{:S(2)}) %collective-permute-start.45) | collective-permute-done | bytes 1310752 | tf_op jit(solution)/shard_map/ppermute | solution.py:933
  565.9 9.8 %collective-permute-start.49 = (bf16[256,2560]{1,0:T(8,128)(2,1)}, bf16[256,2560]{1,0:T(8,128)(2,1)}, u32[]{:S(2)}, u32[]{:S(2)}) collective-permute-start(bf16[256,2560]{1,0:T(8,128)(2,1)} %get-tuple-element.247), channel_id=1, source_target_pairs={{0,1},{1,2},{2,3},{4,5},{5,6},{6,7},{8,9},{9,10},{10,11},{12,13},{... | collective-permute-start | bytes 3932168 | tf_op jit(solution)/shard_map/ppermute | solution.py:933
  582.9 6.1 mixed_gradient.3
  589.0 13.7 %attend_backward.3 = (bf16[10,96,512]{2,1,0:T(8,128)(2,1)}, bf16[10,128,512]{2,1,0:T(8,128)(2,1)}, f32[32,512]{1,0:T(8,128)}) custom-call(bf16[10,96,1024]{2,1,0:T(8,128)(2,1)} %get-tuple-element.184.q_ref.refs_0_, bf16[10,96,1024]{2,1,0:T(8,128)(2,1)} %get-tuple-element.181.k_ref.refs_1_, bf16[10,64,1024]{2,1,0:T(8,128)(2,1)} %get-tuple-element.182.v_ref.refs_2_, ...), custom_call_target="tpu_custom_call" | custom-call | flops 78643 | bytes 1024 | tf_op jit(solution)/shard_map/attend_backward/pallas_call | solution.py:242
  602.7 7.0 latent_back.1
  609.7 5.1 fusion.2
  614.9 5.3 collective-permute-start.51
  621.5 49.8 %collective-permute-done.51 = bf16[256,2560]{1,0:T(8,128)(2,1)} collective-permute-done((bf16[256,2560]{1,0:T(8,128)(2,1)}, bf16[256,2560]{1,0:T(8,128)(2,1)}, u32[]{:S(2)}, u32[]{:S(2)}) %collective-permute-start.51) | collective-permute-done | bytes 1310752 | tf_op jit(solution)/shard_map/ppermute | solution.py:868
  671.2 16.1 %collective-permute-done.52 = bf16[256,2560]{1,0:T(8,128)(2,1)} collective-permute-done((bf16[256,2560]{1,0:T(8,128)(2,1)}, bf16[256,2560]{1,0:T(8,128)(2,1)}, u32[]{:S(2)}, u32[]{:S(2)}) %collective-permute-start.52) | collective-permute-done | bytes 1310752 | tf_op jit(solution)/shard_map/ppermute | solution.py:869
  687.3 13.6 %heads_outer.1 = bf16[8,288,1280]{2,1,0:T(8,128)(2,1)} custom-call(bf16[512,2560]{1,0:T(8,128)(2,1)} %get-tuple-element.268.refs_0_, bf16[512,2560]{1,0:T(8,128)(2,1)} %get-tuple-element.269.refs_1_, bf16[640,512]{1,0:T(8,128)(2,1)} %bitcast.207, bf16[640,512]{1,0:T(8,128)(2,1)} %bitcast.206, bf16[960,512]{1,0:T(8,128)(2,1)} %bitcast.201, ...), custom_call_target="tpu_custom_call" | custom-call | flops 67108 | bytes 1024 | tf_op jit(solution)/shard_map/heads_outer/pallas_call | solution.py:572
  700.9 7.8 adam_rows.3
  708.6 7.7 adam_rows.2
  716.4 18.3 %all-reduce.5.cloned.1.call-done.total_ref = bf16[1040,1056]{1,0:T(8,128)(2,1)} async-done(((bf16[1040,1056]{1,0:T(8,128)(2,1)}), bf16[1040,1056]{1,0:T(8,128)(2,1)}) %all-reduce.5.cloned.1.call-update) | async-done | bytes 2196496 | tf_op jit(solution)/shard_map/psum | solution.py:1263
  740.0 6.4 latents_turned.1
  746.4 13.6 %down_outer.1 = (bf16[2560,1056]{1,0:T(8,128)(2,1)}, f32[2560,1]{1,0:T(8,128)}) custom-call(bf16[1024,2560]{1,0:T(8,128)(2,1)} %get-tuple-element.279.normed_ref, bf16[1024,1056]{1,0:T(8,128)(2,1)} %get-tuple-element.285.grad_ref, bf16[2560,1056]{1,0:T(8,128)(2,1)} %copy-done, f32[2560,1]{1,0:T(8,128)} %broadcast_in_dim.51.gain_ref), custom_call_target="tpu_custom_call" | custom-call | flops 110729 | bytes 1024 | tf_op jit(solution)/shard_map/down_outer/pallas_call | solution.py:445
  767.4 5.1 collective-permute-done.54
  777.1 5.1 multiply_subtract_fusion
  782.2 17.1 %input_back.1 = f32[1024,2560]{1,0:T(8,128)} custom-call(bf16[1024,1056]{1,0:T(8,128)(2,1)} %get-tuple-element.285.grad_ref, bf16[2560,1056]{1,0:T(8,128)(2,1)} %copy-done, bf16[1024,2560]{1,0:T(8,128)(2,1)} %inputs_ref.3, bf16[1024,2560]{1,0:T(8,128)(2,1)} %cot_ref.5, bf16[1024,2560]{1,0:T(8,128)(2,1)} %constant_dynamic-update-slice_fusion.mid_ref, ...), custom_call_target="tpu_custom_call" | custom-call | flops 110729 | bytes 1024 | tf_op jit(solution)/shard_map/input_back/pallas_call | solution.py:478
  801.1 4.0 collective-permute-done.56
  807.5 3.4 pad_maximum_fusion.1
  (350 shorter events, 148.4 us)
Async XLA Ops:
  7.2 195.6 %all-gather.3.cloned.1.call-start = ((), (), s32[]{:S(2)}) async-start(), calls=%async_computation.4 | async-start | bytes 28753920 | tf_op jit(solution)/shard_map/all_gather | solution.py:1115
  13.4 234.6 %all-gather.5.cloned.1.call-start = ((), (), s32[]{:S(2)}) async-start(), calls=%async_computation.5 | async-start | bytes 14745600 | tf_op jit(solution)/shard_map/all_gather | solution.py:1112
  14.4 10.2 %collective-permute-start.2 = (bf16[80,1056]{1,0:T(8,128)(2,1)S(1)}, bf16[80,1056]{1,0:T(8,128)(2,1)S(1)}, u32[]{:S(2)}, u32[]{:S(2)}) collective-permute-start(bf16[80,1056]{1,0:T(8,128)(2,1)S(1)} %pad_maximum_fusion.23), channel_id=1, source_target_pairs={{0,3},{1,0},{2,1},{3,2},{4,7},{5,4},{6,5},{7,6},{8,11},{9,8},{10,9... | collective-permute-start | bytes 506888 | tf_op jit(solution)/shard_map/ppermute | solution.py:898
  19.5 15.6 %collective-permute-start.1 = (bf16[80,1056]{1,0:T(8,128)(2,1)S(1)}, bf16[80,1056]{1,0:T(8,128)(2,1)S(1)}, u32[]{:S(2)}, u32[]{:S(2)}) collective-permute-start(bf16[80,1056]{1,0:T(8,128)(2,1)S(1)} %pad_maximum_fusion.23), channel_id=1, source_target_pairs={{0,2},{1,3},{2,0},{3,1},{4,6},{5,7},{6,4},{7,5},{8,10},{9,11},{10,... | collective-permute-start | bytes 506888 | tf_op jit(solution)/shard_map/ppermute | solution.py:898
  19.5 15.6 %collective-permute-start = (bf16[80,1056]{1,0:T(8,128)(2,1)S(1)}, bf16[80,1056]{1,0:T(8,128)(2,1)S(1)}, u32[]{:S(2)}, u32[]{:S(2)}) collective-permute-start(bf16[80,1056]{1,0:T(8,128)(2,1)S(1)} %pad_maximum_fusion.23), channel_id=1, source_target_pairs={{0,1},{1,2},{2,3},{3,0},{4,5},{5,6},{6,7},{7,4},{8,9},{9,10},{10,1... | collective-permute-start | bytes 506888 | tf_op jit(solution)/shard_map/ppermute | solution.py:898
  35.2 14.2 %collective-permute-start.3 = (bf16[1,72,1280]{2,1,0:T(8,128)(2,1)S(1)}, bf16[1,72,1280]{2,1,0:T(8,128)(2,1)S(1)}, u32[]{:S(2)}, u32[]{:S(2)}) collective-permute-start(bf16[1,72,1280]{2,1,0:T(8,128)(2,1)S(1)} %get-tuple-element.161), channel_id=1, source_target_pairs={{0,8},{4,12},{8,0},{12,4},{16,24},{20,28},{24,16},{28,20},{1,9},{5... | collective-permute-start | bytes 552968 | tf_op jit(solution)/shard_map/ppermute | solution.py:964
  36.7 11.4 %collective-permute-start.4 = (bf16[1,72,1280]{2,1,0:T(8,128)(2,1)S(1)}, bf16[1,72,1280]{2,1,0:T(8,128)(2,1)S(1)}, u32[]{:S(2)}, u32[]{:S(2)}) collective-permute-start(bf16[1,72,1280]{2,1,0:T(8,128)(2,1)S(1)} %get-tuple-element.162), channel_id=1, source_target_pairs={{0,16},{4,20},{8,24},{12,28},{16,0},{20,4},{24,8},{28,12},{1,17},{... | collective-permute-start | bytes 552968 | tf_op jit(solution)/shard_map/ppermute | solution.py:964
  38.6 24.8 %collective-permute-start.5 = (bf16[1,160,1056]{2,1,0:T(8,128)(2,1)S(1)}, bf16[1,160,1056]{2,1,0:T(8,128)(2,1)S(1)}, u32[]{:S(2)}, u32[]{:S(2)}) collective-permute-start(bf16[1,160,1056]{2,1,0:T(8,128)(2,1)S(1)} %get-tuple-element.163), channel_id=1, source_target_pairs={{0,8},{4,12},{8,0},{12,4},{16,24},{20,28},{24,16},{28,20},{1,9},{5... | collective-permute-start | bytes 1013768 | tf_op jit(solution)/shard_map/ppermute | solution.py:964
  39.2 24.1 %collective-permute-start.6 = (bf16[1,160,1056]{2,1,0:T(8,128)(2,1)S(1)}, bf16[1,160,1056]{2,1,0:T(8,128)(2,1)S(1)}, u32[]{:S(2)}, u32[]{:S(2)}) collective-permute-start(bf16[1,160,1056]{2,1,0:T(8,128)(2,1)S(1)} %get-tuple-element.164), channel_id=1, source_target_pairs={{0,16},{4,20},{8,24},{12,28},{16,0},{20,4},{24,8},{28,12},{1,17},{... | collective-permute-start | bytes 1013768 | tf_op jit(solution)/shard_map/ppermute | solution.py:964
  39.7 23.7 %collective-permute-start.7 = (bf16[320,640]{1,0:T(8,128)(2,1)S(1)}, bf16[320,640]{1,0:T(8,128)(2,1)S(1)}, u32[]{:S(2)}, u32[]{:S(2)}) collective-permute-start(bf16[320,640]{1,0:T(8,128)(2,1)S(1)} %convert_bitcast_fusion.3), channel_id=1, source_target_pairs={{0,1},{1,2},{2,3},{4,5},{5,6},{6,7},{8,9},{9,10},{10,11},{12,13},{... | collective-permute-start | bytes 1228808 | tf_op jit(solution)/shard_map/ppermute | solution.py:868
  48.1 15.3 %collective-permute-start.8 = (bf16[320,640]{1,0:T(8,128)(2,1)S(1)}, bf16[320,640]{1,0:T(8,128)(2,1)S(1)}, u32[]{:S(2)}, u32[]{:S(2)}) collective-permute-start(bf16[320,640]{1,0:T(8,128)(2,1)S(1)} %convert_bitcast_fusion.3), channel_id=1, source_target_pairs={{1,0},{2,1},{3,2},{5,4},{6,5},{7,6},{9,8},{10,9},{11,10},{13,12},{... | collective-permute-start | bytes 1228808 | tf_op jit(solution)/shard_map/ppermute | solution.py:869
  63.5 19.5 %collective-permute-start.9 = (bf16[2,72,1280]{2,1,0:T(8,128)(2,1)S(1)}, bf16[2,72,1280]{2,1,0:T(8,128)(2,1)}, u32[]{:S(2)}, u32[]{:S(2)}) collective-permute-start(bf16[2,72,1280]{2,1,0:T(8,128)(2,1)S(1)} %pad_maximum_fusion.19), channel_id=1, source_target_pairs={{0,16},{4,20},{8,24},{12,28},{16,0},{20,4},{24,8},{28,12},{1,17},{... | collective-permute-start | bytes 1105928 | tf_op jit(solution)/shard_map/ppermute | solution.py:964
  65.1 35.6 %collective-permute-start.11 = (bf16[2,160,1056]{2,1,0:T(8,128)(2,1)S(1)}, bf16[2,160,1056]{2,1,0:T(8,128)(2,1)}, u32[]{:S(2)}, u32[]{:S(2)}) collective-permute-start(bf16[2,160,1056]{2,1,0:T(8,128)(2,1)S(1)} %pad_maximum_fusion.16), channel_id=1, source_target_pairs={{0,16},{4,20},{8,24},{12,28},{16,0},{20,4},{24,8},{28,12},{1,17},{... | collective-permute-start | bytes 2027528 | tf_op jit(solution)/shard_map/ppermute | solution.py:964
  65.7 35.1 %collective-permute-start.12 = (bf16[2,160,1056]{2,1,0:T(8,128)(2,1)S(1)}, bf16[2,160,1056]{2,1,0:T(8,128)(2,1)}, u32[]{:S(2)}, u32[]{:S(2)}) collective-permute-start(bf16[2,160,1056]{2,1,0:T(8,128)(2,1)S(1)} %pad_maximum_fusion.17), channel_id=1, source_target_pairs={{0,8},{4,12},{8,0},{12,4},{16,24},{20,28},{24,16},{28,20},{1,9},{5... | collective-permute-start | bytes 2027528 | tf_op jit(solution)/shard_map/ppermute | solution.py:964
  66.2 33.0 %collective-permute-start.13 = (bf16[320,640]{1,0:T(8,128)(2,1)S(1)}, bf16[320,640]{1,0:T(8,128)(2,1)}, u32[]{:S(2)}, u32[]{:S(2)}) collective-permute-start(bf16[320,640]{1,0:T(8,128)(2,1)S(1)} %collective-permute-done.7), channel_id=1, source_target_pairs={{1,2},{2,3},{5,6},{6,7},{9,10},{10,11},{13,14},{14,15},{17,18},{18... | collective-permute-start | bytes 1228808 | tf_op jit(solution)/shard_map/ppermute | solution.py:868
  67.6 31.6 %collective-permute-start.14 = (bf16[320,640]{1,0:T(8,128)(2,1)S(1)}, bf16[320,640]{1,0:T(8,128)(2,1)}, u32[]{:S(2)}, u32[]{:S(2)}) collective-permute-start(bf16[320,640]{1,0:T(8,128)(2,1)S(1)} %collective-permute-done.8), channel_id=1, source_target_pairs={{1,0},{2,1},{5,4},{6,5},{9,8},{10,9},{13,12},{14,13},{17,16},{18,1... | collective-permute-start | bytes 1228808 | tf_op jit(solution)/shard_map/ppermute | solution.py:869
  82.9 16.3 %collective-permute-start.10 = (bf16[2,72,1280]{2,1,0:T(8,128)(2,1)S(1)}, bf16[2,72,1280]{2,1,0:T(8,128)(2,1)}, u32[]{:S(2)}, u32[]{:S(2)}) collective-permute-start(bf16[2,72,1280]{2,1,0:T(8,128)(2,1)S(1)} %pad_maximum_fusion.20), channel_id=1, source_target_pairs={{0,8},{4,12},{8,0},{12,4},{16,24},{20,28},{24,16},{28,20},{1,9},{5... | collective-permute-start | bytes 1105928 | tf_op jit(solution)/shard_map/ppermute | solution.py:964
  102.2 11.7 %collective-permute-start.28 = (bf16[320,640]{1,0:T(8,128)(2,1)}, bf16[320,640]{1,0:T(8,128)(2,1)}, u32[]{:S(2)}, u32[]{:S(2)}) collective-permute-start(bf16[320,640]{1,0:T(8,128)(2,1)} %collective-permute-done.14), channel_id=1, source_target_pairs={{1,0},{5,4},{9,8},{13,12},{17,16},{21,20},{25,24},{29,28}} | collective-permute-start | bytes 1228808 | tf_op jit(solution)/shard_map/ppermute | solution.py:869
  117.1 240.7 %reduce-scatter.5.cloned.1.call-start = ((), (), s32[]{:S(2)}) async-start(), calls=%async_computation.6 | async-start | bytes 3276800 | tf_op jit(solution)/shard_map/reduce_scatter | solution.py:1176
  119.7 6.9 collective-permute-start.15
  120.8 7.0 collective-permute-start.16
  126.1 8.7 %collective-permute-start.17 = (bf16[4,160,1056]{2,1,0:T(8,128)(2,1)}, bf16[4,160,1056]{2,1,0:T(8,128)(2,1)}, u32[]{:S(2)}, u32[]{:S(2)}) collective-permute-start(bf16[4,160,1056]{2,1,0:T(8,128)(2,1)} %pad_maximum_fusion.12), channel_id=1, source_target_pairs={{0,4},{4,0},{8,12},{12,8},{16,20},{20,16},{24,28},{28,24},{1,5},{5... | collective-permute-start | bytes 4055048 | tf_op jit(solution)/shard_map/ppermute | solution.py:964
  126.1 10.6 %collective-permute-start.18 = (bf16[4,160,1056]{2,1,0:T(8,128)(2,1)}, bf16[4,160,1056]{2,1,0:T(8,128)(2,1)}, u32[]{:S(2)}, u32[]{:S(2)}) collective-permute-start(bf16[4,160,1056]{2,1,0:T(8,128)(2,1)} %pad_maximum_fusion.13), channel_id=1, source_target_pairs={{0,4},{4,0},{8,12},{12,8},{16,20},{20,16},{24,28},{28,24},{1,5},{5... | collective-permute-start | bytes 4055048 | tf_op jit(solution)/shard_map/ppermute | solution.py:964
  177.2 16.0 %collective-permute-start.19 = (bf16[640,512]{1,0:T(8,128)(2,1)}, bf16[640,512]{1,0:T(8,128)(2,1)S(1)}, u32[]{:S(2)}, u32[]{:S(2)}) collective-permute-start(bf16[640,512]{1,0:T(8,128)(2,1)} %bitcast.204), channel_id=1, source_target_pairs={{0,1},{1,2},{2,3},{4,5},{5,6},{6,7},{8,9},{9,10},{10,11},{12,13},{... | collective-permute-start | bytes 1966088 | tf_op jit(solution)/shard_map/ppermute | solution.py:868
  178.5 18.8 %collective-permute-start.20 = (bf16[640,512]{1,0:T(8,128)(2,1)}, bf16[640,512]{1,0:T(8,128)(2,1)S(1)}, u32[]{:S(2)}, u32[]{:S(2)}) collective-permute-start(bf16[640,512]{1,0:T(8,128)(2,1)} %bitcast.205), channel_id=1, source_target_pairs={{1,0},{2,1},{3,2},{5,4},{6,5},{7,6},{9,8},{10,9},{11,10},{13,12},{... | collective-permute-start | bytes 1966088 | tf_op jit(solution)/shard_map/ppermute | solution.py:869
  197.3 23.1 %collective-permute-start.21 = (bf16[640,512]{1,0:T(8,128)(2,1)S(1)}, bf16[640,512]{1,0:T(8,128)(2,1)S(1)}, u32[]{:S(2)}, u32[]{:S(2)}) collective-permute-start(bf16[640,512]{1,0:T(8,128)(2,1)S(1)} %collective-permute-done.19), channel_id=1, source_target_pairs={{1,2},{2,3},{5,6},{6,7},{9,10},{10,11},{13,14},{14,15},{17,18},{18... | collective-permute-start | bytes 1966088 | tf_op jit(solution)/shard_map/ppermute | solution.py:868
  198.0 22.4 %collective-permute-start.22 = (bf16[640,512]{1,0:T(8,128)(2,1)S(1)}, bf16[640,512]{1,0:T(8,128)(2,1)S(1)}, u32[]{:S(2)}, u32[]{:S(2)}) collective-permute-start(bf16[640,512]{1,0:T(8,128)(2,1)S(1)} %collective-permute-done.20), channel_id=1, source_target_pairs={{1,0},{2,1},{5,4},{6,5},{9,8},{10,9},{13,12},{14,13},{17,16},{18,1... | collective-permute-start | bytes 1966088 | tf_op jit(solution)/shard_map/ppermute | solution.py:869
  221.1 18.8 %collective-permute-start.24 = (bf16[640,512]{1,0:T(8,128)(2,1)S(1)}, bf16[640,512]{1,0:T(8,128)(2,1)S(1)}, u32[]{:S(2)}, u32[]{:S(2)}) collective-permute-start(bf16[640,512]{1,0:T(8,128)(2,1)S(1)} %collective-permute-done.22), channel_id=1, source_target_pairs={{1,0},{5,4},{9,8},{13,12},{17,16},{21,20},{25,24},{29,28}} | collective-permute-start | bytes 1966088 | tf_op jit(solution)/shard_map/ppermute | solution.py:869
  241.5 20.6 %collective-permute-start.25 = (bf16[640,512]{1,0:T(8,128)(2,1)S(1)}, bf16[640,512]{1,0:T(8,128)(2,1)}, u32[]{:S(2)}, u32[]{:S(2)}) collective-permute-start(bf16[640,512]{1,0:T(8,128)(2,1)S(1)} %bitcast.208), channel_id=1, source_target_pairs={{0,1},{1,2},{2,3},{4,5},{5,6},{6,7},{8,9},{9,10},{10,11},{12,13},{... | collective-permute-start | bytes 1966088 | tf_op jit(solution)/shard_map/ppermute | solution.py:868
  243.8 18.2 %collective-permute-start.26 = (bf16[640,512]{1,0:T(8,128)(2,1)S(1)}, bf16[640,512]{1,0:T(8,128)(2,1)}, u32[]{:S(2)}, u32[]{:S(2)}) collective-permute-start(bf16[640,512]{1,0:T(8,128)(2,1)S(1)} %bitcast.209), channel_id=1, source_target_pairs={{1,0},{2,1},{3,2},{5,4},{6,5},{7,6},{9,8},{10,9},{11,10},{13,12},{... | collective-permute-start | bytes 1966088 | tf_op jit(solution)/shard_map/ppermute | solution.py:869
  262.1 22.0 %collective-permute-start.29 = (bf16[640,512]{1,0:T(8,128)(2,1)}, bf16[640,512]{1,0:T(8,128)(2,1)S(1)}, u32[]{:S(2)}, u32[]{:S(2)}) collective-permute-start(bf16[640,512]{1,0:T(8,128)(2,1)} %collective-permute-done.25), channel_id=1, source_target_pairs={{1,2},{2,3},{5,6},{6,7},{9,10},{10,11},{13,14},{14,15},{17,18},{18... | collective-permute-start | bytes 1966088 | tf_op jit(solution)/shard_map/ppermute | solution.py:868
  262.8 21.3 %collective-permute-start.30 = (bf16[640,512]{1,0:T(8,128)(2,1)}, bf16[640,512]{1,0:T(8,128)(2,1)S(1)}, u32[]{:S(2)}, u32[]{:S(2)}) collective-permute-start(bf16[640,512]{1,0:T(8,128)(2,1)} %collective-permute-done.26), channel_id=1, source_target_pairs={{1,0},{2,1},{5,4},{6,5},{9,8},{10,9},{13,12},{14,13},{17,16},{18,1... | collective-permute-start | bytes 1966088 | tf_op jit(solution)/shard_map/ppermute | solution.py:869
  284.1 17.6 %collective-permute-start.31 = (bf16[640,512]{1,0:T(8,128)(2,1)S(1)}, bf16[640,512]{1,0:T(8,128)(2,1)S(1)}, u32[]{:S(2)}, u32[]{:S(2)}) collective-permute-start(bf16[640,512]{1,0:T(8,128)(2,1)S(1)} %collective-permute-done.29), channel_id=1, source_target_pairs={{2,3},{6,7},{10,11},{14,15},{18,19},{22,23},{26,27},{30,31}} | collective-permute-start | bytes 1966088 | tf_op jit(solution)/shard_map/ppermute | solution.py:868
  284.8 21.0 %collective-permute-start.32 = (bf16[640,512]{1,0:T(8,128)(2,1)S(1)}, bf16[640,512]{1,0:T(8,128)(2,1)S(1)}, u32[]{:S(2)}, u32[]{:S(2)}) collective-permute-start(bf16[640,512]{1,0:T(8,128)(2,1)S(1)} %collective-permute-done.30), channel_id=1, source_target_pairs={{1,0},{5,4},{9,8},{13,12},{17,16},{21,20},{25,24},{29,28}} | collective-permute-start | bytes 1966088 | tf_op jit(solution)/shard_map/ppermute | solution.py:869
  301.4 137.5 %reduce-scatter.7.cloned.1.call-start = ((), (), s32[]{:S(2)}) async-start(), calls=%async_computation.7 | async-start | bytes 3276800 | tf_op jit(solution)/shard_map/reduce_scatter | solution.py:1176
  357.7 257.1 %reduce-scatter.9.cloned.1.call-start = ((), (), s32[]{:S(2)}) async-start(), calls=%async_computation.8 | async-start | bytes 28753920 | tf_op jit(solution)/shard_map/reduce_scatter | solution.py:1216
  361.6 55.4 %collective-permute-start.33 = (bf16[128,2560]{1,0:T(8,128)(2,1)}, bf16[128,2560]{1,0:T(8,128)(2,1)}, u32[]{:S(2)}, u32[]{:S(2)}) collective-permute-start(bf16[128,2560]{1,0:T(8,128)(2,1)} %get-tuple-element.214), channel_id=1, source_target_pairs={{0,1},{1,2},{2,3},{4,5},{5,6},{6,7},{8,9},{9,10},{10,11},{12,13},{... | collective-permute-start | bytes 1966088 | tf_op jit(solution)/shard_map/ppermute | solution.py:868
  365.0 52.0 %collective-permute-start.34 = (bf16[128,2560]{1,0:T(8,128)(2,1)}, bf16[128,2560]{1,0:T(8,128)(2,1)}, u32[]{:S(2)}, u32[]{:S(2)}) collective-permute-start(bf16[128,2560]{1,0:T(8,128)(2,1)} %get-tuple-element.214), channel_id=1, source_target_pairs={{1,0},{2,1},{3,2},{5,4},{6,5},{7,6},{9,8},{10,9},{11,10},{13,12},{... | collective-permute-start | bytes 1966088 | tf_op jit(solution)/shard_map/ppermute | solution.py:869
  417.0 20.2 %collective-permute-start.35 = (bf16[128,2560]{1,0:T(8,128)(2,1)}, bf16[128,2560]{1,0:T(8,128)(2,1)S(1)}, u32[]{:S(2)}, u32[]{:S(2)}) collective-permute-start(bf16[128,2560]{1,0:T(8,128)(2,1)} %collective-permute-done.33), channel_id=1, source_target_pairs={{1,2},{2,3},{5,6},{6,7},{9,10},{10,11},{13,14},{14,15},{17,18},{18... | collective-permute-start | bytes 1966088 | tf_op jit(solution)/shard_map/ppermute | solution.py:868
  417.9 21.1 %collective-permute-start.36 = (bf16[128,2560]{1,0:T(8,128)(2,1)}, bf16[128,2560]{1,0:T(8,128)(2,1)}, u32[]{:S(2)}, u32[]{:S(2)}) collective-permute-start(bf16[128,2560]{1,0:T(8,128)(2,1)} %collective-permute-done.34), channel_id=1, source_target_pairs={{1,0},{2,1},{5,4},{6,5},{9,8},{10,9},{13,12},{14,13},{17,16},{18,1... | collective-permute-start | bytes 1966088 | tf_op jit(solution)/shard_map/ppermute | solution.py:869
  439.0 295.7 %all-reduce.5.cloned.1.call-start = ((), (), s32[]{:S(2)}) async-start(), calls=%async_computation.9 | async-start | bytes 4792320 | tf_op jit(solution)/shard_map/psum | solution.py:1263
  439.1 11.9 %collective-permute-start.37 = (bf16[128,2560]{1,0:T(8,128)(2,1)S(1)}, bf16[128,2560]{1,0:T(8,128)(2,1)S(1)}, u32[]{:S(2)}, u32[]{:S(2)}) collective-permute-start(bf16[128,2560]{1,0:T(8,128)(2,1)S(1)} %collective-permute-done.35), channel_id=1, source_target_pairs={{2,3},{6,7},{10,11},{14,15},{18,19},{22,23},{26,27},{30,31}} | collective-permute-start | bytes 1966088 | tf_op jit(solution)/shard_map/ppermute | solution.py:868
  439.9 20.0 %collective-permute-start.38 = (bf16[128,2560]{1,0:T(8,128)(2,1)}, bf16[128,2560]{1,0:T(8,128)(2,1)S(1)}, u32[]{:S(2)}, u32[]{:S(2)}) collective-permute-start(bf16[128,2560]{1,0:T(8,128)(2,1)} %collective-permute-done.36), channel_id=1, source_target_pairs={{1,0},{5,4},{9,8},{13,12},{17,16},{21,20},{25,24},{29,28}} | collective-permute-start | bytes 1966088 | tf_op jit(solution)/shard_map/ppermute | solution.py:869
  459.9 37.4 %collective-permute-start.39 = (bf16[128,2560]{1,0:T(8,128)(2,1)}, bf16[128,2560]{1,0:T(8,128)(2,1)}, u32[]{:S(2)}, u32[]{:S(2)}) collective-permute-start(bf16[128,2560]{1,0:T(8,128)(2,1)} %get-tuple-element.234), channel_id=1, source_target_pairs={{0,1},{1,2},{2,3},{4,5},{5,6},{6,7},{8,9},{9,10},{10,11},{12,13},{... | collective-permute-start | bytes 1966088 | tf_op jit(solution)/shard_map/ppermute | solution.py:868
  462.3 35.1 %collective-permute-start.40 = (bf16[128,2560]{1,0:T(8,128)(2,1)}, bf16[128,2560]{1,0:T(8,128)(2,1)S(1)}, u32[]{:S(2)}, u32[]{:S(2)}) collective-permute-start(bf16[128,2560]{1,0:T(8,128)(2,1)} %get-tuple-element.234), channel_id=1, source_target_pairs={{1,0},{2,1},{3,2},{5,4},{6,5},{7,6},{9,8},{10,9},{11,10},{13,12},{... | collective-permute-start | bytes 1966088 | tf_op jit(solution)/shard_map/ppermute | solution.py:869
  497.3 31.2 %collective-permute-start.41 = (bf16[256,2560]{1,0:T(8,128)(2,1)}, bf16[256,2560]{1,0:T(8,128)(2,1)}, u32[]{:S(2)}, u32[]{:S(2)}) collective-permute-start(bf16[256,2560]{1,0:T(8,128)(2,1)} %get-tuple-element.239), channel_id=1, source_target_pairs={{0,1},{4,5},{8,9},{12,13},{16,17},{20,21},{24,25},{28,29}} | collective-permute-start | bytes 3932168 | tf_op jit(solution)/shard_map/ppermute | solution.py:933
  503.0 25.5 %collective-permute-start.42 = (bf16[256,2560]{1,0:T(8,128)(2,1)}, bf16[256,2560]{1,0:T(8,128)(2,1)}, u32[]{:S(2)}, u32[]{:S(2)}) collective-permute-start(bf16[256,2560]{1,0:T(8,128)(2,1)} %get-tuple-element.240), channel_id=1, source_target_pairs={{3,2},{7,6},{11,10},{15,14},{19,18},{23,22},{27,26},{31,30}} | collective-permute-start | bytes 3932168 | tf_op jit(solution)/shard_map/ppermute | solution.py:935
  506.2 16.5 %collective-permute-start.44 = (bf16[128,2560]{1,0:T(8,128)(2,1)S(1)}, bf16[128,2560]{1,0:T(8,128)(2,1)}, u32[]{:S(2)}, u32[]{:S(2)}) collective-permute-start(bf16[128,2560]{1,0:T(8,128)(2,1)S(1)} %collective-permute-done.40), channel_id=1, source_target_pairs={{1,0},{2,1},{5,4},{6,5},{9,8},{10,9},{13,12},{14,13},{17,16},{18,1... | collective-permute-start | bytes 1966088 | tf_op jit(solution)/shard_map/ppermute | solution.py:869
  528.5 11.0 %collective-permute-start.47 = (bf16[128,2560]{1,0:T(8,128)(2,1)}, bf16[128,2560]{1,0:T(8,128)(2,1)S(1)}, u32[]{:S(2)}, u32[]{:S(2)}) collective-permute-start(bf16[128,2560]{1,0:T(8,128)(2,1)} %collective-permute-done.43), channel_id=1, source_target_pairs={{2,3},{6,7},{10,11},{14,15},{18,19},{22,23},{26,27},{30,31}} | collective-permute-start | bytes 1966088 | tf_op jit(solution)/shard_map/ppermute | solution.py:868
  529.2 36.7 %collective-permute-start.48 = (bf16[128,2560]{1,0:T(8,128)(2,1)}, bf16[128,2560]{1,0:T(8,128)(2,1)S(1)}, u32[]{:S(2)}, u32[]{:S(2)}) collective-permute-start(bf16[128,2560]{1,0:T(8,128)(2,1)} %collective-permute-done.44), channel_id=1, source_target_pairs={{1,0},{5,4},{9,8},{13,12},{17,16},{21,20},{25,24},{29,28}} | collective-permute-start | bytes 1966088 | tf_op jit(solution)/shard_map/ppermute | solution.py:869
  534.2 29.5 %collective-permute-start.45 = (bf16[256,2560]{1,0:T(8,128)(2,1)S(1)}, bf16[256,2560]{1,0:T(8,128)(2,1)S(1)}, u32[]{:S(2)}, u32[]{:S(2)}) collective-permute-start(bf16[256,2560]{1,0:T(8,128)(2,1)S(1)} %get-tuple-element.243), channel_id=1, source_target_pairs={{0,1},{1,2},{4,5},{5,6},{8,9},{9,10},{12,13},{13,14},{16,17},{17,1... | collective-permute-start | bytes 3932168 | tf_op jit(solution)/shard_map/ppermute | solution.py:933
  538.7 25.0 %collective-permute-start.46 = (bf16[256,2560]{1,0:T(8,128)(2,1)S(1)}, bf16[256,2560]{1,0:T(8,128)(2,1)S(1)}, u32[]{:S(2)}, u32[]{:S(2)}) collective-permute-start(bf16[256,2560]{1,0:T(8,128)(2,1)S(1)} %get-tuple-element.244), channel_id=1, source_target_pairs={{3,2},{2,1},{7,6},{6,5},{11,10},{10,9},{15,14},{14,13},{19,18},{18... | collective-permute-start | bytes 3932168 | tf_op jit(solution)/shard_map/ppermute | solution.py:935
  565.9 43.8 %collective-permute-start.49 = (bf16[256,2560]{1,0:T(8,128)(2,1)}, bf16[256,2560]{1,0:T(8,128)(2,1)}, u32[]{:S(2)}, u32[]{:S(2)}) collective-permute-start(bf16[256,2560]{1,0:T(8,128)(2,1)} %get-tuple-element.247), channel_id=1, source_target_pairs={{0,1},{1,2},{2,3},{4,5},{5,6},{6,7},{8,9},{9,10},{10,11},{12,13},{... | collective-permute-start | bytes 3932168 | tf_op jit(solution)/shard_map/ppermute | solution.py:933
  575.7 34.1 %collective-permute-start.50 = (bf16[256,2560]{1,0:T(8,128)(2,1)}, bf16[256,2560]{1,0:T(8,128)(2,1)}, u32[]{:S(2)}, u32[]{:S(2)}) collective-permute-start(bf16[256,2560]{1,0:T(8,128)(2,1)} %get-tuple-element.248), channel_id=1, source_target_pairs={{3,2},{2,1},{1,0},{7,6},{6,5},{5,4},{11,10},{10,9},{9,8},{15,14},{... | collective-permute-start | bytes 3932168 | tf_op jit(solution)/shard_map/ppermute | solution.py:935
  614.9 198.6 %reduce-scatter.11.cloned.1.call-start = ((), (), s32[]{:S(2)}) async-start(), calls=%async_computation.10 | async-start | bytes 6635520 | tf_op jit(solution)/shard_map/reduce_scatter | solution.py:1288
  614.9 56.3 %collective-permute-start.51 = (bf16[256,2560]{1,0:T(8,128)(2,1)}, bf16[256,2560]{1,0:T(8,128)(2,1)}, u32[]{:S(2)}, u32[]{:S(2)}) collective-permute-start(bf16[256,2560]{1,0:T(8,128)(2,1)} %fusion.2), channel_id=1, source_target_pairs={{0,1},{1,2},{2,3},{4,5},{5,6},{6,7},{8,9},{9,10},{10,11},{12,13},{... | collective-permute-start | bytes 3932168 | tf_op jit(solution)/shard_map/ppermute | solution.py:868
  620.2 67.1 %collective-permute-start.52 = (bf16[256,2560]{1,0:T(8,128)(2,1)}, bf16[256,2560]{1,0:T(8,128)(2,1)}, u32[]{:S(2)}, u32[]{:S(2)}) collective-permute-start(bf16[256,2560]{1,0:T(8,128)(2,1)} %fusion.2), channel_id=1, source_target_pairs={{1,0},{2,1},{3,2},{5,4},{6,5},{7,6},{9,8},{10,9},{11,10},{13,12},{... | collective-permute-start | bytes 3932168 | tf_op jit(solution)/shard_map/ppermute | solution.py:869
  737.7 29.7 %collective-permute-start.53 = (bf16[256,2560]{1,0:T(8,128)(2,1)}, bf16[256,2560]{1,0:T(8,128)(2,1)S(1)}, u32[]{:S(2)}, u32[]{:S(2)}) collective-permute-start(bf16[256,2560]{1,0:T(8,128)(2,1)} %collective-permute-done.51), channel_id=1, source_target_pairs={{1,2},{2,3},{5,6},{6,7},{9,10},{10,11},{13,14},{14,15},{17,18},{18... | collective-permute-start | bytes 3932168 | tf_op jit(solution)/shard_map/ppermute | solution.py:868
  738.5 34.1 %collective-permute-start.54 = (bf16[256,2560]{1,0:T(8,128)(2,1)}, bf16[256,2560]{1,0:T(8,128)(2,1)}, u32[]{:S(2)}, u32[]{:S(2)}) collective-permute-start(bf16[256,2560]{1,0:T(8,128)(2,1)} %collective-permute-done.52), channel_id=1, source_target_pairs={{1,0},{2,1},{5,4},{6,5},{9,8},{10,9},{13,12},{14,13},{17,16},{18,1... | collective-permute-start | bytes 3932168 | tf_op jit(solution)/shard_map/ppermute | solution.py:869
  764.4 10.2 %collective-permute-start.57 = (bf16[2,2,96,1056]{3,2,1,0:T(8,128)(2,1)S(1)}, bf16[2,2,96,1056]{3,2,1,0:T(8,128)(2,1)S(1)}, u32[]{:S(2)}, u32[]{:S(2)}) collective-permute-start(bf16[2,2,96,1056]{3,2,1,0:T(8,128)(2,1)S(1)} %fusion.15), channel_id=1, source_target_pairs={{0,4},{4,0},{8,12},{12,8},{16,20},{20,16},{24,28},{28,24},{1,5},{5... | collective-permute-start | bytes 2433032 | tf_op jit(solution)/shard_map/ppermute | solution.py:1000
  772.5 28.5 %collective-permute-start.55 = (bf16[256,2560]{1,0:T(8,128)(2,1)S(1)}, bf16[256,2560]{1,0:T(8,128)(2,1)S(1)}, u32[]{:S(2)}, u32[]{:S(2)}) collective-permute-start(bf16[256,2560]{1,0:T(8,128)(2,1)S(1)} %collective-permute-done.53), channel_id=1, source_target_pairs={{2,3},{6,7},{10,11},{14,15},{18,19},{22,23},{26,27},{30,31}} | collective-permute-start | bytes 3932168 | tf_op jit(solution)/shard_map/ppermute | solution.py:868
  773.3 31.7 %collective-permute-start.56 = (bf16[256,2560]{1,0:T(8,128)(2,1)}, bf16[256,2560]{1,0:T(8,128)(2,1)S(1)}, u32[]{:S(2)}, u32[]{:S(2)}) collective-permute-start(bf16[256,2560]{1,0:T(8,128)(2,1)} %collective-permute-done.54), channel_id=1, source_target_pairs={{1,0},{5,4},{9,8},{13,12},{17,16},{21,20},{25,24},{29,28}} | collective-permute-start | bytes 3932168 | tf_op jit(solution)/shard_map/ppermute | solution.py:869
  775.7 23.7 %collective-permute-start.58 = (bf16[2,96,1056]{2,1,0:T(8,128)(2,1)}, bf16[2,96,1056]{2,1,0:T(8,128)(2,1)S(1)}, u32[]{:S(2)}, u32[]{:S(2)}) collective-permute-start(bf16[2,96,1056]{2,1,0:T(8,128)(2,1)} %dynamic-slice_bitcast_fusion.2), channel_id=1, source_target_pairs={{0,8},{4,12},{8,0},{12,4},{16,24},{20,28},{24,16},{28,20},{1,9},{5... | collective-permute-start | bytes 1216520 | tf_op jit(solution)/shard_map/ppermute | solution.py:1000
  799.5 11.5 %collective-permute-start.59 = (bf16[96,1056]{1,0:T(8,128)(2,1)S(1)}, bf16[96,1056]{1,0:T(8,128)(2,1)S(1)}, u32[]{:S(2)}, u32[]{:S(2)}) collective-permute-start(bf16[96,1056]{1,0:T(8,128)(2,1)S(1)} %dynamic-slice_bitcast_fusion.3), channel_id=1, source_target_pairs={{0,16},{4,20},{8,24},{12,28},{16,0},{20,4},{24,8},{28,12},{1,17},{... | collective-permute-start | bytes 608264 | tf_op jit(solution)/shard_map/ppermute | solution.py:1000
  (57 other events, 584.2 us)
Sparse Core Ops, SparseCore 0:
  13.6 157.5 all-gather.2
  173.7 74.3 all-gather.4
  301.6 55.1 reduce-scatter.4
  358.9 65.6 reduce-scatter.6
  439.1 161.8 reduce-scatter.8
  615.0 119.6 all-reduce.4
  738.2 63.1 reduce-scatter.10

commit v3 on v2

--- a/solution.py
+++ b/solution.py
@@ -1243,11 +1243,13 @@
     seeds = heads_back(1)
     clock.tick(grad_rope[1])
     out_flow = Scatter(ffn_term, n_model)
-    clock.move(mid_flow[0], out_flow)
+    clock.move(mid_flow[0])
+    out_flow.advance(clock.gate)
     clock.tick()
-    clock.move(mid_flow[0], out_flow)
+    clock.move(mid_flow[0])
+    out_flow.advance(tie)
     clock.tick()
-    clock.move(out_flow)
+    out_flow.advance(tie)
     mixed_back(0)
     seeds = heads_back(0)
     part_latents = latent_back(
@@ -1284,7 +1286,12 @@
     ffn_late = after(ffn_sum, *arrived)
     gate_updates = adam_rows(ffn_gate, ffn_late, 0, ffn_gate_first, ffn_gate_second, ffn_rates[0])
     up_updates = adam_rows(ffn_up, ffn_late, 1, ffn_up_first, ffn_up_second, ffn_rates[1])
-    latents_sum = after(latents_sum, head_grads, gate_updates[2], up_updates[2])
+    down_updates = adam_rows(
+        ffn_down.T, ffn_late, 2, ffn_down_first.T, ffn_down_second.T, ffn_rates[2]
+    )
+    latents_sum = after(
+        latents_sum, head_grads, gate_updates[2], up_updates[2], down_updates[2]
+    )
     head_sum = lax.psum_scatter(
         after(head_grads, latents_sum).reshape(-1, up_width), "dp", scatter_dimension=0, tiled=True
     )
@@ -1328,13 +1335,7 @@
     clock.tick(input_grad)
     clock.move(down_flow)
     down_sum = wide(down_flow.result())
-    down_rate = ffn_rates[2]
-    down_part = ffn_sum.reshape(3, -1, hidden_dev)[2].T
-    ffn_updated = [
-        gate_updates,
-        up_updates,
-        adam_step(ffn_down, wide(down_part), ffn_down_first, ffn_down_second, down_rate),
-    ]
+    ffn_updated = [gate_updates, up_updates, [update.T for update in down_updates]]
     reduced = (
         down_sum[down_rows, :gain_count],
         down_sum[:down_rows, :QR],

time: 834 us -> 832 us (level)
  waiting for transfers between devices: 256 us -> 247 us
    psum x1, waiting for transfers between devices: 18.3 us -> 9.82 us  [local(): latents_sum = lax.psum(after(part_latents, ffn_sum), 'mp')]
    pallas_call x2 -> x3, Pallas kernels: 15.5 us -> 23.3 us  [adam_rows(): pl.pallas_call(functools.partial(adam_kernel, rate_pair), grid=(5,), in_s...]
  transfers between devices with their start and end apart: 67 -> 67, of which waited for: 23 -> 23; matrix products, arithmetic and copies ran while one was open for 13% -> 13% of each run, Pallas kernels for 39% -> 40%
where the time goes in v3:
time: 832 us; the launch traced here: 825 us
  Pallas kernels  333 us (40%)
  waiting for transfers between devices  247 us (30%)
  starting transfers between devices  96 us (12%)
  other arithmetic  72.4 us (9%)
  local copies, waits for them, and re-layouts  38.8 us (5%)
  matrix products  21.7 us (3%)
  between operations  16.4 us (2%)
    ppermute x18, waiting for transfers between devices, advance(): self.above.append(lax.ppermute(down, 'mp', downs))  88.9 us
    ppermute x18, waiting for transfers between devices, advance(): self.below.append(lax.ppermute(up, 'mp', ups))  51.8 us
    ppermute x12, waiting for transfers between devices, advance(): came.append(lax.ppermute(part, 'dp', pairs))  50.7 us
    pallas_call x4, Pallas kernels, ffn_back(): pl.pallas_call(functools.partial(back_kernel, count), grid=(2, tokens //...  48.7 us
    pallas_call x3, Pallas kernels, ffn_outer(): pl.pallas_call(functools.partial(outer_kernel, count), grid=(2,), in_spec...  44.4 us
    pallas_call x2, Pallas kernels, ffn_inner(): pl.pallas_call(inner_kernel, grid=(steps, 2, 2), in_specs=[pl.BlockSpec((...  39.1 us
    pallas_call x2, Pallas kernels, attend_backward(): pl.pallas_call(functools.partial(backward_kernel, half * size // BLK, hal...  36.2 us
    ppermute x18, starting transfers between devices, advance(): self.below.append(lax.ppermute(up, 'mp', ups))  29.3 us
  transfers between devices with their start and end apart: 67, of which 23 were waited for; matrix products, arithmetic and copies ran while one was open for 13% of the time, Pallas kernels for 40%

profile of v3, /device:TPU:0, one launch (start us, length us, event | category | flops | bytes accessed | tf_op | source)
XLA Modules:
  0.0 824.9 jit_solution(5112548318508983257)
XLA Ops:
  14.4 5.1 collective-permute-start.2
  20.8 3.8 collective-permute-done.2
  24.6 10.6 %collective-permute-done.1 = bf16[80,1056]{1,0:T(8,128)(2,1)S(1)} collective-permute-done((bf16[80,1056]{1,0:T(8,128)(2,1)S(1)}, bf16[80,1056]{1,0:T(8,128)(2,1)S(1)}, u32[]{:S(2)}, u32[]{:S(2)}) %collective-permute-start.1) | collective-permute-done | bytes 168992 | tf_op jit(solution)/shard_map/ppermute | solution.py:898
  39.7 2.8 collective-permute-start.7
  42.5 5.6 collective-permute-done.4
  49.5 13.8 %collective-permute-done.6 = bf16[1,160,1056]{2,1,0:T(8,128)(2,1)S(1)} collective-permute-done((bf16[1,160,1056]{2,1,0:T(8,128)(2,1)S(1)}, bf16[1,160,1056]{2,1,0:T(8,128)(2,1)S(1)}, u32[]{:S(2)}, u32[]{:S(2)}) %collective-permute-start.6) | collective-permute-done | bytes 337952 | tf_op jit(solution)/shard_map/ppermute | solution.py:964
  68.9 14.0 %collective-permute-done.9 = bf16[2,72,1280]{2,1,0:T(8,128)(2,1)} collective-permute-done((bf16[2,72,1280]{2,1,0:T(8,128)(2,1)S(1)}, bf16[2,72,1280]{2,1,0:T(8,128)(2,1)}, u32[]{:S(2)}, u32[]{:S(2)}) %collective-permute-start.9) | collective-permute-done | bytes 368672 | tf_op jit(solution)/shard_map/ppermute | solution.py:964
  83.5 15.8 %collective-permute-done.10 = bf16[2,72,1280]{2,1,0:T(8,128)(2,1)} collective-permute-done((bf16[2,72,1280]{2,1,0:T(8,128)(2,1)S(1)}, bf16[2,72,1280]{2,1,0:T(8,128)(2,1)}, u32[]{:S(2)}, u32[]{:S(2)}) %collective-permute-start.10) | collective-permute-done | bytes 368672 | tf_op jit(solution)/shard_map/ppermute | solution.py:964
  103.5 10.4 %collective-permute-done.28 = bf16[320,640]{1,0:T(8,128)(2,1)} collective-permute-done((bf16[320,640]{1,0:T(8,128)(2,1)}, bf16[320,640]{1,0:T(8,128)(2,1)}, u32[]{:S(2)}, u32[]{:S(2)}) %collective-permute-start.28) | collective-permute-done | bytes 409632 | tf_op jit(solution)/shard_map/ppermute | solution.py:869
  141.9 13.8 %latents_forward.1 = (bf16[1024,2560]{1,0:T(8,128)(2,1)}, f32[1024,1056]{1,0:T(8,128)}, bf16[1024,768]{1,0:T(8,128)(2,1)}, bf16[1024,256]{1,0:T(8,128)(2,1)}, bf16[32,1024]{1,0:T(8,128)(2,1)}) custom-call(bf16[1024,2560]{1,0:T(8,128)(2,1)} %inputs_ref.3, f32[1,2560]{1,0:T(1,128)} %broadcast_in_dim.45.gain_in.gain_ref, bf16[2560,1056]{1,0:T(8,128)(2,1)} %copy-done, ...), custom_call_target="tpu_custom_call" | custom-call | flops 27682 | bytes 1024 | tf_op jit(solution)/shard_map/latents_forward/pallas_call | solution.py:628
  155.7 6.9 heads_forward.1
  162.6 14.6 %attend_forward.2 = (bf16[10,64,512]{2,1,0:T(8,128)(2,1)}, f32[10,1,512]{2,1,0:T(1,128)}) custom-call(bf16[10,96,1024]{2,1,0:T(8,128)(2,1)} %get-tuple-element.187.q_ref.refs_0_, bf16[10,96,1024]{2,1,0:T(8,128)(2,1)} %get-tuple-element.184.k_ref.refs_1_, bf16[10,64,1024]{2,1,0:T(8,128)(2,1)} %get-tuple-element.185.v_ref.refs_2_), custom_call_target="tpu_custom_call" | custom-call | flops 73400 | bytes 1024 | tf_op jit(solution)/shard_map/attend_forward/pallas_call | solution.py:120
  179.8 10.3 %attend_forward.3 = (bf16[10,64,512]{2,1,0:T(8,128)(2,1)}, f32[10,1,512]{2,1,0:T(1,128)}) custom-call(bf16[10,96,1024]{2,1,0:T(8,128)(2,1)} %get-tuple-element.187.q_ref.refs_0_, bf16[10,96,1024]{2,1,0:T(8,128)(2,1)} %get-tuple-element.184.k_ref.refs_1_, bf16[10,64,1024]{2,1,0:T(8,128)(2,1)} %get-tuple-element.185.v_ref.refs_2_), custom_call_target="tpu_custom_call" | custom-call | flops 36700 | bytes 1024 | tf_op jit(solution)/shard_map/attend_forward/pallas_call | solution.py:120
  190.1 3.2 collective-permute-done.19
  193.3 4.0 collective-permute-done.20
  199.6 3.3 multiply_convert_fusion.grad_ref.refs_0_.refs_1_
  202.9 17.6 %hidden_back.1.grad_ref = f32[1024,1600]{1,0:T(8,128)} custom-call(bf16[1024,2560]{1,0:T(8,128)(2,1)} %multiply_convert_fusion.grad_ref.refs_0_.refs_1_, bf16[8,3,320,1600]{3,2,1,0:T(8,128)(2,1)} %all-gather.3.cloned.1.call-done.weight_ref.refs_2_.refs_1_), custom_call_target="tpu_custom_call" | custom-call | flops 83886 | bytes 1024 | tf_op jit(solution)/shard_map/hidden_back/pallas_call | solution.py:300
  222.4 17.5 %collective-permute-done.24 = bf16[640,512]{1,0:T(8,128)(2,1)S(1)} collective-permute-done((bf16[640,512]{1,0:T(8,128)(2,1)S(1)}, bf16[640,512]{1,0:T(8,128)(2,1)S(1)}, u32[]{:S(2)}, u32[]{:S(2)}) %collective-permute-start.24) | collective-permute-done | bytes 655392 | tf_op jit(solution)/shard_map/ppermute | solution.py:869
  245.1 3.0 all-gather.5.cloned.1.call-done
  248.1 10.8 %multiply_reduce_fusion.1 = (f32[512]{0:T(512)S(1)}, f32[512,2560]{1,0:T(8,128)S(1)}) fusion(bf16[2560,512]{1,0:T(8,128)(2,1)S(1)} %pad_maximum_fusion.5, bf16[2560,2560]{1,0:T(8,128)(2,1)} %all-gather.5.cloned.1.call-done, bf16[1024,2560]{1,0:T(8,128)(2,1)} %inputs_ref.3), kind=kOutput, calls=%fused_computation.9 | convolution fusion | flops 6717439488 | bytes 23595008 | tf_op jit(solution)/shard_map/ht,dh->td/dot_general | solution.py:52
  264.5 19.5 %ffn_inner.2 = (bf16[512,1600]{1,0:T(8,128)(2,1)}, bf16[512,1600]{1,0:T(8,128)(2,1)}, bf16[512,1600]{1,0:T(8,128)(2,1)}) custom-call(bf16[512,2560]{1,0:T(8,128)(2,1)} %multiply_convert_fusion.2.normed_ref.refs_0_, f32[1024,1600]{1,0:T(8,128)} %hidden_back.1.grad_ref, bf16[8,3,320,1600]{3,2,1,0:T(8,128)(2,1)} %all-gather.3.cloned.1.call-done.weight_ref.refs_2_.refs_1_), custom_call_target="tpu_custom_call" | custom-call | flops 83886 | bytes 1024 | tf_op jit(solution)/shard_map/ffn_inner/pallas_call | solution.py:348
  286.1 15.3 %ffn_back.4 = bf16[512,2560]{1,0:T(8,128)(2,1)} custom-call(bf16[512,1600]{1,0:T(8,128)(2,1)} %get-tuple-element.220.refs_0_.refs_2_, bf16[512,1600]{1,0:T(8,128)(2,1)} %get-tuple-element.219.refs_1_.refs_2_, bf16[8,3,320,1600]{3,2,1,0:T(8,128)(2,1)} %all-gather.3.cloned.1.call-done.weight_ref.refs_2_.refs_1_), custom_call_target="tpu_custom_call" | custom-call | flops 167772 | bytes 1024 | tf_op jit(solution)/shard_map/ffn_back/pallas_call | solution.py:382
  301.7 4.1 collective-permute-done.32
  307.6 10.9 %multiply_reduce_fusion = (f32[512]{0:T(512)S(1)}, f32[512,2560]{1,0:T(8,128)S(1)}) fusion(bf16[2560,512]{1,0:T(8,128)(2,1)S(1)} %pad_maximum_fusion.6, bf16[2560,2560]{1,0:T(8,128)(2,1)} %all-gather.5.cloned.1.call-done, bf16[1024,2560]{1,0:T(8,128)(2,1)} %inputs_ref.3), kind=kOutput, calls=%fused_computation.6 | convolution fusion | flops 6717439488 | bytes 23595008 | tf_op jit(solution)/shard_map/ht,dh->td/dot_general | solution.py:52
  322.8 19.6 %ffn_inner.3 = (bf16[512,1600]{1,0:T(8,128)(2,1)}, bf16[512,1600]{1,0:T(8,128)(2,1)}, bf16[512,1600]{1,0:T(8,128)(2,1)}) custom-call(bf16[512,2560]{1,0:T(8,128)(2,1)} %multiply_convert_fusion.1.normed_ref.refs_1_, f32[1024,1600]{1,0:T(8,128)} %hidden_back.1.grad_ref, bf16[8,3,320,1600]{3,2,1,0:T(8,128)(2,1)} %all-gather.3.cloned.1.call-done.weight_ref.refs_2_.refs_1_), custom_call_target="tpu_custom_call" | custom-call | flops 83886 | bytes 1024 | tf_op jit(solution)/shard_map/ffn_inner/pallas_call | solution.py:348
  342.4 15.4 %ffn_back.5 = bf16[512,2560]{1,0:T(8,128)(2,1)} custom-call(bf16[512,1600]{1,0:T(8,128)(2,1)} %get-tuple-element.215.refs_0_.refs_3_, bf16[512,1600]{1,0:T(8,128)(2,1)} %get-tuple-element.214.refs_1_.refs_3_, bf16[8,3,320,1600]{3,2,1,0:T(8,128)(2,1)} %all-gather.3.cloned.1.call-done.weight_ref.refs_2_.refs_1_), custom_call_target="tpu_custom_call" | custom-call | flops 167772 | bytes 1024 | tf_op jit(solution)/shard_map/ffn_back/pallas_call | solution.py:382
  358.4 3.2 middle_back.2
  361.6 3.4 collective-permute-start.33
  368.5 4.1 copy.75
  372.5 14.8 %ffn_outer.3 = (bf16[8,3,320,1600]{3,2,1,0:T(8,128)(2,1)}, f32[8,128]{1,0:T(8,128)}) custom-call(bf16[512,2560]{1,0:T(8,128)(2,1)} %multiply_convert_fusion.2.normed_ref.refs_0_, bf16[512,2560]{1,0:T(8,128)(2,1)} %multiply_convert_fusion.1.normed_ref.refs_1_, bf16[512,1600]{1,0:T(8,128)(2,1)} %get-tuple-element.220.refs_0_.refs_2_, ...), custom_call_target="tpu_custom_call" | custom-call | flops 167772 | bytes 1024 | tf_op jit(solution)/shard_map/ffn_outer/pallas_call | solution.py:412
  387.3 14.7 %ffn_outer.4 = (bf16[8,3,320,1600]{3,2,1,0:T(8,128)(2,1)}, f32[8,128]{1,0:T(8,128)}) custom-call(bf16[512,2560]{1,0:T(8,128)(2,1)} %multiply_convert_fusion.2.normed_ref.refs_0_, bf16[512,2560]{1,0:T(8,128)(2,1)} %multiply_convert_fusion.1.normed_ref.refs_1_, bf16[512,1600]{1,0:T(8,128)(2,1)} %get-tuple-element.219.refs_1_.refs_2_, ...), custom_call_target="tpu_custom_call", output_to_operand_aliasing={{0}: (4, {})} | custom-call | flops 167772 | bytes 1024 | tf_op jit(solution)/shard_map/ffn_outer/pallas_call | solution.py:412
  402.0 14.9 %ffn_outer.5 = (bf16[8,3,320,1600]{3,2,1,0:T(8,128)(2,1)}, f32[8,128]{1,0:T(8,128)}) custom-call(bf16[1024,2560]{1,0:T(8,128)(2,1)} %multiply_convert_fusion.grad_ref.refs_0_.refs_1_, bf16[1024,2560]{1,0:T(8,128)(2,1)} %multiply_convert_fusion.grad_ref.refs_0_.refs_1_, ...), custom_call_target="tpu_custom_call", output_to_operand_aliasing={{0}: (4, {})} | custom-call | flops 167772 | bytes 1024 | tf_op jit(solution)/shard_map/ffn_outer/pallas_call | solution.py:412
  419.1 9.1 %ffn_back.7 = bf16[512,2560]{1,0:T(8,128)(2,1)} custom-call(bf16[512,1600]{1,0:T(8,128)(2,1)} %get-tuple-element.229.refs_2_.refs_0_, bf16[8,3,320,1600]{3,2,1,0:T(8,128)(2,1)} %all-gather.3.cloned.1.call-done.weight_ref.refs_2_.refs_1_), custom_call_target="tpu_custom_call" | custom-call | flops 83886 | bytes 1024 | tf_op jit(solution)/shard_map/ffn_back/pallas_call | solution.py:382
  428.2 9.0 %ffn_back.6 = bf16[512,2560]{1,0:T(8,128)(2,1)} custom-call(bf16[512,1600]{1,0:T(8,128)(2,1)} %get-tuple-element.226.refs_3_.refs_0_, bf16[8,3,320,1600]{3,2,1,0:T(8,128)(2,1)} %all-gather.3.cloned.1.call-done.weight_ref.refs_2_.refs_1_), custom_call_target="tpu_custom_call" | custom-call | flops 83886 | bytes 1024 | tf_op jit(solution)/shard_map/ffn_back/pallas_call | solution.py:382
  447.3 3.7 middle_back.3
  451.0 8.9 %collective-permute-done.38 = bf16[128,2560]{1,0:T(8,128)(2,1)S(1)} collective-permute-done((bf16[128,2560]{1,0:T(8,128)(2,1)}, bf16[128,2560]{1,0:T(8,128)(2,1)S(1)}, u32[]{:S(2)}, u32[]{:S(2)}) %collective-permute-start.38) | collective-permute-done | bytes 655392 | tf_op jit(solution)/shard_map/ppermute | solution.py:869
  467.6 7.4 mixed_gradient.2
  475.0 22.4 %attend_backward.2 = (bf16[10,96,512]{2,1,0:T(8,128)(2,1)}, bf16[10,128,512]{2,1,0:T(8,128)(2,1)}, f32[32,512]{1,0:T(8,128)}, f32[10,96,512]{2,1,0:T(8,128)}, f32[10,64,512]{2,1,0:T(8,128)}) custom-call(bf16[10,96,1024]{2,1,0:T(8,128)(2,1)} %get-tuple-element.187.q_ref.refs_0_, bf16[10,96,1024]{2,1,0:T(8,128)(2,1)} %get-tuple-element.184.k_ref.refs_1_, ...), custom_call_target="tpu_custom_call" | custom-call | flops 157286 | bytes 1024 | tf_op jit(solution)/shard_map/attend_backward/pallas_call | solution.py:242
  497.4 5.6 collective-permute-start.41
  507.6 15.1 %collective-permute-done.48 = bf16[128,2560]{1,0:T(8,128)(2,1)} collective-permute-done((bf16[128,2560]{1,0:T(8,128)(2,1)S(1)}, bf16[128,2560]{1,0:T(8,128)(2,1)}, u32[]{:S(2)}, u32[]{:S(2)}) %collective-permute-start.48) | collective-permute-done | bytes 655392 | tf_op jit(solution)/shard_map/ppermute | solution.py:869
  524.7 3.8 collective-permute-done.41
  528.5 3.3 fusion.4
  531.8 4.7 collective-permute-start.43
  538.0 23.9 %collective-permute-done.43 = bf16[256,2560]{1,0:T(8,128)(2,1)S(1)} collective-permute-done((bf16[256,2560]{1,0:T(8,128)(2,1)S(1)}, bf16[256,2560]{1,0:T(8,128)(2,1)S(1)}, u32[]{:S(2)}, u32[]{:S(2)}) %collective-permute-start.43) | collective-permute-done | bytes 1310752 | tf_op jit(solution)/shard_map/ppermute | solution.py:933
  564.0 10.0 %collective-permute-start.45 = (bf16[256,2560]{1,0:T(8,128)(2,1)}, bf16[256,2560]{1,0:T(8,128)(2,1)}, u32[]{:S(2)}, u32[]{:S(2)}) collective-permute-start(bf16[256,2560]{1,0:T(8,128)(2,1)} %get-tuple-element.246), channel_id=1, source_target_pairs={{0,1},{1,2},{2,3},{4,5},{5,6},{6,7},{8,9},{9,10},{10,11},{12,13},{... | collective-permute-start | bytes 3932168 | tf_op jit(solution)/shard_map/ppermute | solution.py:933
  581.3 5.7 mixed_gradient.3
  587.0 13.7 %attend_backward.3 = (bf16[10,96,512]{2,1,0:T(8,128)(2,1)}, bf16[10,128,512]{2,1,0:T(8,128)(2,1)}, f32[32,512]{1,0:T(8,128)}) custom-call(bf16[10,96,1024]{2,1,0:T(8,128)(2,1)} %get-tuple-element.187.q_ref.refs_0_, bf16[10,96,1024]{2,1,0:T(8,128)(2,1)} %get-tuple-element.184.k_ref.refs_1_, bf16[10,64,1024]{2,1,0:T(8,128)(2,1)} %get-tuple-element.185.v_ref.refs_2_, ...), custom_call_target="tpu_custom_call" | custom-call | flops 78643 | bytes 1024 | tf_op jit(solution)/shard_map/attend_backward/pallas_call | solution.py:242
  600.7 7.0 latent_back.1
  607.7 4.0 fusion.2
  611.9 5.9 collective-permute-start.51
  619.1 48.6 %collective-permute-done.51 = bf16[256,2560]{1,0:T(8,128)(2,1)} collective-permute-done((bf16[256,2560]{1,0:T(8,128)(2,1)S(1)}, bf16[256,2560]{1,0:T(8,128)(2,1)}, u32[]{:S(2)}, u32[]{:S(2)}) %collective-permute-start.51) | collective-permute-done | bytes 1310752 | tf_op jit(solution)/shard_map/ppermute | solution.py:868
  667.7 16.4 %collective-permute-done.52 = bf16[256,2560]{1,0:T(8,128)(2,1)} collective-permute-done((bf16[256,2560]{1,0:T(8,128)(2,1)S(1)}, bf16[256,2560]{1,0:T(8,128)(2,1)}, u32[]{:S(2)}, u32[]{:S(2)}) %collective-permute-start.52) | collective-permute-done | bytes 1310752 | tf_op jit(solution)/shard_map/ppermute | solution.py:869
  684.1 13.7 %heads_outer.1 = bf16[8,288,1280]{2,1,0:T(8,128)(2,1)} custom-call(bf16[512,2560]{1,0:T(8,128)(2,1)} %get-tuple-element.271.refs_0_, bf16[512,2560]{1,0:T(8,128)(2,1)} %get-tuple-element.272.refs_1_, bf16[640,512]{1,0:T(8,128)(2,1)} %bitcast.206, bf16[640,512]{1,0:T(8,128)(2,1)} %bitcast.205, bf16[960,512]{1,0:T(8,128)(2,1)} %bitcast.200, ...), custom_call_target="tpu_custom_call" | custom-call | flops 67108 | bytes 1024 | tf_op jit(solution)/shard_map/heads_outer/pallas_call | solution.py:572
  697.8 7.8 adam_rows.4
  705.6 7.7 adam_rows.3
  713.3 7.8 adam_rows.5
  721.1 9.8 %all-reduce.5.cloned.1.call-done.total_ref = bf16[1040,1056]{1,0:T(8,128)(2,1)} async-done(((bf16[1040,1056]{1,0:T(8,128)(2,1)}), bf16[1040,1056]{1,0:T(8,128)(2,1)}) %all-reduce.5.cloned.1.call-update) | async-done | bytes 2196496 | tf_op jit(solution)/shard_map/psum | solution.py:1265
  736.3 6.4 latents_turned.1
  742.7 13.6 %down_outer.1 = (bf16[2560,1056]{1,0:T(8,128)(2,1)}, f32[2560,1]{1,0:T(8,128)}) custom-call(bf16[1024,2560]{1,0:T(8,128)(2,1)} %get-tuple-element.283.normed_ref, bf16[1024,1056]{1,0:T(8,128)(2,1)} %get-tuple-element.289.grad_ref, bf16[2560,1056]{1,0:T(8,128)(2,1)} %copy-done, f32[2560,1]{1,0:T(8,128)} %broadcast_in_dim.51.gain_ref), custom_call_target="tpu_custom_call" | custom-call | flops 110729 | bytes 1024 | tf_op jit(solution)/shard_map/down_outer/pallas_call | solution.py:445
  764.8 4.0 collective-permute-done.54
  775.6 17.6 %input_back.1 = f32[1024,2560]{1,0:T(8,128)} custom-call(bf16[1024,1056]{1,0:T(8,128)(2,1)} %get-tuple-element.289.grad_ref, bf16[2560,1056]{1,0:T(8,128)(2,1)} %copy-done, bf16[1024,2560]{1,0:T(8,128)(2,1)} %inputs_ref.3, bf16[1024,2560]{1,0:T(8,128)(2,1)} %cot_ref.5, bf16[1024,2560]{1,0:T(8,128)(2,1)} %constant_dynamic-update-slice_fusion.mid_ref, ...), custom_call_target="tpu_custom_call" | custom-call | flops 110729 | bytes 1024 | tf_op jit(solution)/shard_map/input_back/pallas_call | solution.py:478
  794.8 6.6 collective-permute-done.56
  801.4 3.2 select_select_fusion.3
  804.7 3.4 pad_maximum_fusion.1
  (350 shorter events, 152.1 us)
Async XLA Ops:
  7.2 195.6 %all-gather.3.cloned.1.call-start = ((), (), s32[]{:S(2)}) async-start(), calls=%async_computation.4 | async-start | bytes 28753920 | tf_op jit(solution)/shard_map/all_gather | solution.py:1115
  13.4 234.6 %all-gather.5.cloned.1.call-start = ((), (), s32[]{:S(2)}) async-start(), calls=%async_computation.5 | async-start | bytes 14745600 | tf_op jit(solution)/shard_map/all_gather | solution.py:1112
  14.4 10.2 %collective-permute-start.2 = (bf16[80,1056]{1,0:T(8,128)(2,1)S(1)}, bf16[80,1056]{1,0:T(8,128)(2,1)S(1)}, u32[]{:S(2)}, u32[]{:S(2)}) collective-permute-start(bf16[80,1056]{1,0:T(8,128)(2,1)S(1)} %pad_maximum_fusion.23), channel_id=1, source_target_pairs={{0,3},{1,0},{2,1},{3,2},{4,7},{5,4},{6,5},{7,6},{8,11},{9,8},{10,9... | collective-permute-start | bytes 506888 | tf_op jit(solution)/shard_map/ppermute | solution.py:898
  19.5 15.6 %collective-permute-start.1 = (bf16[80,1056]{1,0:T(8,128)(2,1)S(1)}, bf16[80,1056]{1,0:T(8,128)(2,1)S(1)}, u32[]{:S(2)}, u32[]{:S(2)}) collective-permute-start(bf16[80,1056]{1,0:T(8,128)(2,1)S(1)} %pad_maximum_fusion.23), channel_id=1, source_target_pairs={{0,2},{1,3},{2,0},{3,1},{4,6},{5,7},{6,4},{7,5},{8,10},{9,11},{10,... | collective-permute-start | bytes 506888 | tf_op jit(solution)/shard_map/ppermute | solution.py:898
  19.5 15.6 %collective-permute-start = (bf16[80,1056]{1,0:T(8,128)(2,1)S(1)}, bf16[80,1056]{1,0:T(8,128)(2,1)S(1)}, u32[]{:S(2)}, u32[]{:S(2)}) collective-permute-start(bf16[80,1056]{1,0:T(8,128)(2,1)S(1)} %pad_maximum_fusion.23), channel_id=1, source_target_pairs={{0,1},{1,2},{2,3},{3,0},{4,5},{5,6},{6,7},{7,4},{8,9},{9,10},{10,1... | collective-permute-start | bytes 506888 | tf_op jit(solution)/shard_map/ppermute | solution.py:898
  35.2 14.2 %collective-permute-start.3 = (bf16[1,72,1280]{2,1,0:T(8,128)(2,1)S(1)}, bf16[1,72,1280]{2,1,0:T(8,128)(2,1)S(1)}, u32[]{:S(2)}, u32[]{:S(2)}) collective-permute-start(bf16[1,72,1280]{2,1,0:T(8,128)(2,1)S(1)} %get-tuple-element.164), channel_id=1, source_target_pairs={{0,8},{4,12},{8,0},{12,4},{16,24},{20,28},{24,16},{28,20},{1,9},{5... | collective-permute-start | bytes 552968 | tf_op jit(solution)/shard_map/ppermute | solution.py:964
  36.7 11.4 %collective-permute-start.4 = (bf16[1,72,1280]{2,1,0:T(8,128)(2,1)S(1)}, bf16[1,72,1280]{2,1,0:T(8,128)(2,1)S(1)}, u32[]{:S(2)}, u32[]{:S(2)}) collective-permute-start(bf16[1,72,1280]{2,1,0:T(8,128)(2,1)S(1)} %get-tuple-element.165), channel_id=1, source_target_pairs={{0,16},{4,20},{8,24},{12,28},{16,0},{20,4},{24,8},{28,12},{1,17},{... | collective-permute-start | bytes 552968 | tf_op jit(solution)/shard_map/ppermute | solution.py:964
  38.6 24.8 %collective-permute-start.5 = (bf16[1,160,1056]{2,1,0:T(8,128)(2,1)S(1)}, bf16[1,160,1056]{2,1,0:T(8,128)(2,1)S(1)}, u32[]{:S(2)}, u32[]{:S(2)}) collective-permute-start(bf16[1,160,1056]{2,1,0:T(8,128)(2,1)S(1)} %get-tuple-element.166), channel_id=1, source_target_pairs={{0,8},{4,12},{8,0},{12,4},{16,24},{20,28},{24,16},{28,20},{1,9},{5... | collective-permute-start | bytes 1013768 | tf_op jit(solution)/shard_map/ppermute | solution.py:964
  39.2 24.1 %collective-permute-start.6 = (bf16[1,160,1056]{2,1,0:T(8,128)(2,1)S(1)}, bf16[1,160,1056]{2,1,0:T(8,128)(2,1)S(1)}, u32[]{:S(2)}, u32[]{:S(2)}) collective-permute-start(bf16[1,160,1056]{2,1,0:T(8,128)(2,1)S(1)} %get-tuple-element.167), channel_id=1, source_target_pairs={{0,16},{4,20},{8,24},{12,28},{16,0},{20,4},{24,8},{28,12},{1,17},{... | collective-permute-start | bytes 1013768 | tf_op jit(solution)/shard_map/ppermute | solution.py:964
  39.7 23.7 %collective-permute-start.7 = (bf16[320,640]{1,0:T(8,128)(2,1)S(1)}, bf16[320,640]{1,0:T(8,128)(2,1)S(1)}, u32[]{:S(2)}, u32[]{:S(2)}) collective-permute-start(bf16[320,640]{1,0:T(8,128)(2,1)S(1)} %convert_bitcast_fusion.3), channel_id=1, source_target_pairs={{0,1},{1,2},{2,3},{4,5},{5,6},{6,7},{8,9},{9,10},{10,11},{12,13},{... | collective-permute-start | bytes 1228808 | tf_op jit(solution)/shard_map/ppermute | solution.py:868
  48.1 15.3 %collective-permute-start.8 = (bf16[320,640]{1,0:T(8,128)(2,1)S(1)}, bf16[320,640]{1,0:T(8,128)(2,1)S(1)}, u32[]{:S(2)}, u32[]{:S(2)}) collective-permute-start(bf16[320,640]{1,0:T(8,128)(2,1)S(1)} %convert_bitcast_fusion.3), channel_id=1, source_target_pairs={{1,0},{2,1},{3,2},{5,4},{6,5},{7,6},{9,8},{10,9},{11,10},{13,12},{... | collective-permute-start | bytes 1228808 | tf_op jit(solution)/shard_map/ppermute | solution.py:869
  63.5 19.5 %collective-permute-start.9 = (bf16[2,72,1280]{2,1,0:T(8,128)(2,1)S(1)}, bf16[2,72,1280]{2,1,0:T(8,128)(2,1)}, u32[]{:S(2)}, u32[]{:S(2)}) collective-permute-start(bf16[2,72,1280]{2,1,0:T(8,128)(2,1)S(1)} %pad_maximum_fusion.19), channel_id=1, source_target_pairs={{0,16},{4,20},{8,24},{12,28},{16,0},{20,4},{24,8},{28,12},{1,17},{... | collective-permute-start | bytes 1105928 | tf_op jit(solution)/shard_map/ppermute | solution.py:964
  65.1 35.6 %collective-permute-start.11 = (bf16[2,160,1056]{2,1,0:T(8,128)(2,1)S(1)}, bf16[2,160,1056]{2,1,0:T(8,128)(2,1)}, u32[]{:S(2)}, u32[]{:S(2)}) collective-permute-start(bf16[2,160,1056]{2,1,0:T(8,128)(2,1)S(1)} %pad_maximum_fusion.16), channel_id=1, source_target_pairs={{0,16},{4,20},{8,24},{12,28},{16,0},{20,4},{24,8},{28,12},{1,17},{... | collective-permute-start | bytes 2027528 | tf_op jit(solution)/shard_map/ppermute | solution.py:964
  65.7 35.1 %collective-permute-start.12 = (bf16[2,160,1056]{2,1,0:T(8,128)(2,1)S(1)}, bf16[2,160,1056]{2,1,0:T(8,128)(2,1)}, u32[]{:S(2)}, u32[]{:S(2)}) collective-permute-start(bf16[2,160,1056]{2,1,0:T(8,128)(2,1)S(1)} %pad_maximum_fusion.17), channel_id=1, source_target_pairs={{0,8},{4,12},{8,0},{12,4},{16,24},{20,28},{24,16},{28,20},{1,9},{5... | collective-permute-start | bytes 2027528 | tf_op jit(solution)/shard_map/ppermute | solution.py:964
  66.2 33.0 %collective-permute-start.13 = (bf16[320,640]{1,0:T(8,128)(2,1)S(1)}, bf16[320,640]{1,0:T(8,128)(2,1)}, u32[]{:S(2)}, u32[]{:S(2)}) collective-permute-start(bf16[320,640]{1,0:T(8,128)(2,1)S(1)} %collective-permute-done.7), channel_id=1, source_target_pairs={{1,2},{2,3},{5,6},{6,7},{9,10},{10,11},{13,14},{14,15},{17,18},{18... | collective-permute-start | bytes 1228808 | tf_op jit(solution)/shard_map/ppermute | solution.py:868
  67.6 31.6 %collective-permute-start.14 = (bf16[320,640]{1,0:T(8,128)(2,1)S(1)}, bf16[320,640]{1,0:T(8,128)(2,1)}, u32[]{:S(2)}, u32[]{:S(2)}) collective-permute-start(bf16[320,640]{1,0:T(8,128)(2,1)S(1)} %collective-permute-done.8), channel_id=1, source_target_pairs={{1,0},{2,1},{5,4},{6,5},{9,8},{10,9},{13,12},{14,13},{17,16},{18,1... | collective-permute-start | bytes 1228808 | tf_op jit(solution)/shard_map/ppermute | solution.py:869
  82.9 16.3 %collective-permute-start.10 = (bf16[2,72,1280]{2,1,0:T(8,128)(2,1)S(1)}, bf16[2,72,1280]{2,1,0:T(8,128)(2,1)}, u32[]{:S(2)}, u32[]{:S(2)}) collective-permute-start(bf16[2,72,1280]{2,1,0:T(8,128)(2,1)S(1)} %pad_maximum_fusion.20), channel_id=1, source_target_pairs={{0,8},{4,12},{8,0},{12,4},{16,24},{20,28},{24,16},{28,20},{1,9},{5... | collective-permute-start | bytes 1105928 | tf_op jit(solution)/shard_map/ppermute | solution.py:964
  102.2 11.7 %collective-permute-start.28 = (bf16[320,640]{1,0:T(8,128)(2,1)}, bf16[320,640]{1,0:T(8,128)(2,1)}, u32[]{:S(2)}, u32[]{:S(2)}) collective-permute-start(bf16[320,640]{1,0:T(8,128)(2,1)} %collective-permute-done.14), channel_id=1, source_target_pairs={{1,0},{5,4},{9,8},{13,12},{17,16},{21,20},{25,24},{29,28}} | collective-permute-start | bytes 1228808 | tf_op jit(solution)/shard_map/ppermute | solution.py:869
  117.1 240.7 %reduce-scatter.5.cloned.1.call-start = ((), (), s32[]{:S(2)}) async-start(), calls=%async_computation.6 | async-start | bytes 3276800 | tf_op jit(solution)/shard_map/reduce_scatter | solution.py:1176
  119.7 6.9 collective-permute-start.15
  120.8 7.0 collective-permute-start.16
  126.1 8.7 %collective-permute-start.17 = (bf16[4,160,1056]{2,1,0:T(8,128)(2,1)}, bf16[4,160,1056]{2,1,0:T(8,128)(2,1)}, u32[]{:S(2)}, u32[]{:S(2)}) collective-permute-start(bf16[4,160,1056]{2,1,0:T(8,128)(2,1)} %pad_maximum_fusion.12), channel_id=1, source_target_pairs={{0,4},{4,0},{8,12},{12,8},{16,20},{20,16},{24,28},{28,24},{1,5},{5... | collective-permute-start | bytes 4055048 | tf_op jit(solution)/shard_map/ppermute | solution.py:964
  126.1 10.6 %collective-permute-start.18 = (bf16[4,160,1056]{2,1,0:T(8,128)(2,1)}, bf16[4,160,1056]{2,1,0:T(8,128)(2,1)}, u32[]{:S(2)}, u32[]{:S(2)}) collective-permute-start(bf16[4,160,1056]{2,1,0:T(8,128)(2,1)} %pad_maximum_fusion.13), channel_id=1, source_target_pairs={{0,4},{4,0},{8,12},{12,8},{16,20},{20,16},{24,28},{28,24},{1,5},{5... | collective-permute-start | bytes 4055048 | tf_op jit(solution)/shard_map/ppermute | solution.py:964
  177.2 16.0 %collective-permute-start.19 = (bf16[640,512]{1,0:T(8,128)(2,1)}, bf16[640,512]{1,0:T(8,128)(2,1)S(1)}, u32[]{:S(2)}, u32[]{:S(2)}) collective-permute-start(bf16[640,512]{1,0:T(8,128)(2,1)} %bitcast.203), channel_id=1, source_target_pairs={{0,1},{1,2},{2,3},{4,5},{5,6},{6,7},{8,9},{9,10},{10,11},{12,13},{... | collective-permute-start | bytes 1966088 | tf_op jit(solution)/shard_map/ppermute | solution.py:868
  178.5 18.8 %collective-permute-start.20 = (bf16[640,512]{1,0:T(8,128)(2,1)}, bf16[640,512]{1,0:T(8,128)(2,1)S(1)}, u32[]{:S(2)}, u32[]{:S(2)}) collective-permute-start(bf16[640,512]{1,0:T(8,128)(2,1)} %bitcast.204), channel_id=1, source_target_pairs={{1,0},{2,1},{3,2},{5,4},{6,5},{7,6},{9,8},{10,9},{11,10},{13,12},{... | collective-permute-start | bytes 1966088 | tf_op jit(solution)/shard_map/ppermute | solution.py:869
  197.3 23.1 %collective-permute-start.21 = (bf16[640,512]{1,0:T(8,128)(2,1)S(1)}, bf16[640,512]{1,0:T(8,128)(2,1)S(1)}, u32[]{:S(2)}, u32[]{:S(2)}) collective-permute-start(bf16[640,512]{1,0:T(8,128)(2,1)S(1)} %collective-permute-done.19), channel_id=1, source_target_pairs={{1,2},{2,3},{5,6},{6,7},{9,10},{10,11},{13,14},{14,15},{17,18},{18... | collective-permute-start | bytes 1966088 | tf_op jit(solution)/shard_map/ppermute | solution.py:868
  198.0 22.4 %collective-permute-start.22 = (bf16[640,512]{1,0:T(8,128)(2,1)S(1)}, bf16[640,512]{1,0:T(8,128)(2,1)S(1)}, u32[]{:S(2)}, u32[]{:S(2)}) collective-permute-start(bf16[640,512]{1,0:T(8,128)(2,1)S(1)} %collective-permute-done.20), channel_id=1, source_target_pairs={{1,0},{2,1},{5,4},{6,5},{9,8},{10,9},{13,12},{14,13},{17,16},{18,1... | collective-permute-start | bytes 1966088 | tf_op jit(solution)/shard_map/ppermute | solution.py:869
  221.1 18.8 %collective-permute-start.24 = (bf16[640,512]{1,0:T(8,128)(2,1)S(1)}, bf16[640,512]{1,0:T(8,128)(2,1)S(1)}, u32[]{:S(2)}, u32[]{:S(2)}) collective-permute-start(bf16[640,512]{1,0:T(8,128)(2,1)S(1)} %collective-permute-done.22), channel_id=1, source_target_pairs={{1,0},{5,4},{9,8},{13,12},{17,16},{21,20},{25,24},{29,28}} | collective-permute-start | bytes 1966088 | tf_op jit(solution)/shard_map/ppermute | solution.py:869
  241.5 20.6 %collective-permute-start.25 = (bf16[640,512]{1,0:T(8,128)(2,1)S(1)}, bf16[640,512]{1,0:T(8,128)(2,1)}, u32[]{:S(2)}, u32[]{:S(2)}) collective-permute-start(bf16[640,512]{1,0:T(8,128)(2,1)S(1)} %bitcast.207), channel_id=1, source_target_pairs={{0,1},{1,2},{2,3},{4,5},{5,6},{6,7},{8,9},{9,10},{10,11},{12,13},{... | collective-permute-start | bytes 1966088 | tf_op jit(solution)/shard_map/ppermute | solution.py:868
  243.8 18.2 %collective-permute-start.26 = (bf16[640,512]{1,0:T(8,128)(2,1)S(1)}, bf16[640,512]{1,0:T(8,128)(2,1)}, u32[]{:S(2)}, u32[]{:S(2)}) collective-permute-start(bf16[640,512]{1,0:T(8,128)(2,1)S(1)} %bitcast.208), channel_id=1, source_target_pairs={{1,0},{2,1},{3,2},{5,4},{6,5},{7,6},{9,8},{10,9},{11,10},{13,12},{... | collective-permute-start | bytes 1966088 | tf_op jit(solution)/shard_map/ppermute | solution.py:869
  262.1 22.0 %collective-permute-start.29 = (bf16[640,512]{1,0:T(8,128)(2,1)}, bf16[640,512]{1,0:T(8,128)(2,1)S(1)}, u32[]{:S(2)}, u32[]{:S(2)}) collective-permute-start(bf16[640,512]{1,0:T(8,128)(2,1)} %collective-permute-done.25), channel_id=1, source_target_pairs={{1,2},{2,3},{5,6},{6,7},{9,10},{10,11},{13,14},{14,15},{17,18},{18... | collective-permute-start | bytes 1966088 | tf_op jit(solution)/shard_map/ppermute | solution.py:868
  262.8 21.3 %collective-permute-start.30 = (bf16[640,512]{1,0:T(8,128)(2,1)}, bf16[640,512]{1,0:T(8,128)(2,1)S(1)}, u32[]{:S(2)}, u32[]{:S(2)}) collective-permute-start(bf16[640,512]{1,0:T(8,128)(2,1)} %collective-permute-done.26), channel_id=1, source_target_pairs={{1,0},{2,1},{5,4},{6,5},{9,8},{10,9},{13,12},{14,13},{17,16},{18,1... | collective-permute-start | bytes 1966088 | tf_op jit(solution)/shard_map/ppermute | solution.py:869
  284.1 17.6 %collective-permute-start.31 = (bf16[640,512]{1,0:T(8,128)(2,1)S(1)}, bf16[640,512]{1,0:T(8,128)(2,1)S(1)}, u32[]{:S(2)}, u32[]{:S(2)}) collective-permute-start(bf16[640,512]{1,0:T(8,128)(2,1)S(1)} %collective-permute-done.29), channel_id=1, source_target_pairs={{2,3},{6,7},{10,11},{14,15},{18,19},{22,23},{26,27},{30,31}} | collective-permute-start | bytes 1966088 | tf_op jit(solution)/shard_map/ppermute | solution.py:868
  284.8 21.0 %collective-permute-start.32 = (bf16[640,512]{1,0:T(8,128)(2,1)S(1)}, bf16[640,512]{1,0:T(8,128)(2,1)S(1)}, u32[]{:S(2)}, u32[]{:S(2)}) collective-permute-start(bf16[640,512]{1,0:T(8,128)(2,1)S(1)} %collective-permute-done.30), channel_id=1, source_target_pairs={{1,0},{5,4},{9,8},{13,12},{17,16},{21,20},{25,24},{29,28}} | collective-permute-start | bytes 1966088 | tf_op jit(solution)/shard_map/ppermute | solution.py:869
  301.4 137.5 %reduce-scatter.7.cloned.1.call-start = ((), (), s32[]{:S(2)}) async-start(), calls=%async_computation.7 | async-start | bytes 3276800 | tf_op jit(solution)/shard_map/reduce_scatter | solution.py:1176
  357.7 254.1 %reduce-scatter.9.cloned.1.call-start = ((), (), s32[]{:S(2)}) async-start(), calls=%async_computation.8 | async-start | bytes 28753920 | tf_op jit(solution)/shard_map/reduce_scatter | solution.py:1216
  361.6 55.4 %collective-permute-start.33 = (bf16[128,2560]{1,0:T(8,128)(2,1)}, bf16[128,2560]{1,0:T(8,128)(2,1)}, u32[]{:S(2)}, u32[]{:S(2)}) collective-permute-start(bf16[128,2560]{1,0:T(8,128)(2,1)} %get-tuple-element.217), channel_id=1, source_target_pairs={{0,1},{1,2},{2,3},{4,5},{5,6},{6,7},{8,9},{9,10},{10,11},{12,13},{... | collective-permute-start | bytes 1966088 | tf_op jit(solution)/shard_map/ppermute | solution.py:868
  365.0 52.0 %collective-permute-start.34 = (bf16[128,2560]{1,0:T(8,128)(2,1)}, bf16[128,2560]{1,0:T(8,128)(2,1)}, u32[]{:S(2)}, u32[]{:S(2)}) collective-permute-start(bf16[128,2560]{1,0:T(8,128)(2,1)} %get-tuple-element.217), channel_id=1, source_target_pairs={{1,0},{2,1},{3,2},{5,4},{6,5},{7,6},{9,8},{10,9},{11,10},{13,12},{... | collective-permute-start | bytes 1966088 | tf_op jit(solution)/shard_map/ppermute | solution.py:869
  417.0 20.2 %collective-permute-start.35 = (bf16[128,2560]{1,0:T(8,128)(2,1)}, bf16[128,2560]{1,0:T(8,128)(2,1)S(1)}, u32[]{:S(2)}, u32[]{:S(2)}) collective-permute-start(bf16[128,2560]{1,0:T(8,128)(2,1)} %collective-permute-done.33), channel_id=1, source_target_pairs={{1,2},{2,3},{5,6},{6,7},{9,10},{10,11},{13,14},{14,15},{17,18},{18... | collective-permute-start | bytes 1966088 | tf_op jit(solution)/shard_map/ppermute | solution.py:868
  417.8 21.1 %collective-permute-start.36 = (bf16[128,2560]{1,0:T(8,128)(2,1)}, bf16[128,2560]{1,0:T(8,128)(2,1)}, u32[]{:S(2)}, u32[]{:S(2)}) collective-permute-start(bf16[128,2560]{1,0:T(8,128)(2,1)} %collective-permute-done.34), channel_id=1, source_target_pairs={{1,0},{2,1},{5,4},{6,5},{9,8},{10,9},{13,12},{14,13},{17,16},{18,1... | collective-permute-start | bytes 1966088 | tf_op jit(solution)/shard_map/ppermute | solution.py:869
  439.0 291.9 %all-reduce.5.cloned.1.call-start = ((), (), s32[]{:S(2)}) async-start(), calls=%async_computation.9 | async-start | bytes 4792320 | tf_op jit(solution)/shard_map/psum | solution.py:1265
  439.0 11.9 %collective-permute-start.37 = (bf16[128,2560]{1,0:T(8,128)(2,1)S(1)}, bf16[128,2560]{1,0:T(8,128)(2,1)S(1)}, u32[]{:S(2)}, u32[]{:S(2)}) collective-permute-start(bf16[128,2560]{1,0:T(8,128)(2,1)S(1)} %collective-permute-done.35), channel_id=1, source_target_pairs={{2,3},{6,7},{10,11},{14,15},{18,19},{22,23},{26,27},{30,31}} | collective-permute-start | bytes 1966088 | tf_op jit(solution)/shard_map/ppermute | solution.py:868
  439.9 20.0 %collective-permute-start.38 = (bf16[128,2560]{1,0:T(8,128)(2,1)}, bf16[128,2560]{1,0:T(8,128)(2,1)S(1)}, u32[]{:S(2)}, u32[]{:S(2)}) collective-permute-start(bf16[128,2560]{1,0:T(8,128)(2,1)} %collective-permute-done.36), channel_id=1, source_target_pairs={{1,0},{5,4},{9,8},{13,12},{17,16},{21,20},{25,24},{29,28}} | collective-permute-start | bytes 1966088 | tf_op jit(solution)/shard_map/ppermute | solution.py:869
  459.9 37.6 %collective-permute-start.39 = (bf16[128,2560]{1,0:T(8,128)(2,1)}, bf16[128,2560]{1,0:T(8,128)(2,1)S(1)}, u32[]{:S(2)}, u32[]{:S(2)}) collective-permute-start(bf16[128,2560]{1,0:T(8,128)(2,1)} %get-tuple-element.237), channel_id=1, source_target_pairs={{0,1},{1,2},{2,3},{4,5},{5,6},{6,7},{8,9},{9,10},{10,11},{12,13},{... | collective-permute-start | bytes 1966088 | tf_op jit(solution)/shard_map/ppermute | solution.py:868
  461.5 36.0 %collective-permute-start.40 = (bf16[128,2560]{1,0:T(8,128)(2,1)}, bf16[128,2560]{1,0:T(8,128)(2,1)S(1)}, u32[]{:S(2)}, u32[]{:S(2)}) collective-permute-start(bf16[128,2560]{1,0:T(8,128)(2,1)} %get-tuple-element.237), channel_id=1, source_target_pairs={{1,0},{2,1},{3,2},{5,4},{6,5},{7,6},{9,8},{10,9},{11,10},{13,12},{... | collective-permute-start | bytes 1966088 | tf_op jit(solution)/shard_map/ppermute | solution.py:869
  497.4 31.1 %collective-permute-start.41 = (bf16[256,2560]{1,0:T(8,128)(2,1)}, bf16[256,2560]{1,0:T(8,128)(2,1)}, u32[]{:S(2)}, u32[]{:S(2)}) collective-permute-start(bf16[256,2560]{1,0:T(8,128)(2,1)} %get-tuple-element.242), channel_id=1, source_target_pairs={{0,1},{4,5},{8,9},{12,13},{16,17},{20,21},{24,25},{28,29}} | collective-permute-start | bytes 3932168 | tf_op jit(solution)/shard_map/ppermute | solution.py:933
  503.1 25.4 %collective-permute-start.42 = (bf16[256,2560]{1,0:T(8,128)(2,1)}, bf16[256,2560]{1,0:T(8,128)(2,1)}, u32[]{:S(2)}, u32[]{:S(2)}) collective-permute-start(bf16[256,2560]{1,0:T(8,128)(2,1)} %get-tuple-element.243), channel_id=1, source_target_pairs={{3,2},{7,6},{11,10},{15,14},{19,18},{23,22},{27,26},{31,30}} | collective-permute-start | bytes 3932168 | tf_op jit(solution)/shard_map/ppermute | solution.py:935
  506.3 16.4 %collective-permute-start.48 = (bf16[128,2560]{1,0:T(8,128)(2,1)S(1)}, bf16[128,2560]{1,0:T(8,128)(2,1)}, u32[]{:S(2)}, u32[]{:S(2)}) collective-permute-start(bf16[128,2560]{1,0:T(8,128)(2,1)S(1)} %collective-permute-done.40), channel_id=1, source_target_pairs={{1,0},{2,1},{5,4},{6,5},{9,8},{10,9},{13,12},{14,13},{17,16},{18,1... | collective-permute-start | bytes 1966088 | tf_op jit(solution)/shard_map/ppermute | solution.py:869
  522.7 14.6 %collective-permute-start.49 = (bf16[128,2560]{1,0:T(8,128)(2,1)}, bf16[128,2560]{1,0:T(8,128)(2,1)S(1)}, u32[]{:S(2)}, u32[]{:S(2)}) collective-permute-start(bf16[128,2560]{1,0:T(8,128)(2,1)} %collective-permute-done.47), channel_id=1, source_target_pairs={{2,3},{6,7},{10,11},{14,15},{18,19},{22,23},{26,27},{30,31}} | collective-permute-start | bytes 1966088 | tf_op jit(solution)/shard_map/ppermute | solution.py:868
  523.4 53.6 %collective-permute-start.50 = (bf16[128,2560]{1,0:T(8,128)(2,1)}, bf16[128,2560]{1,0:T(8,128)(2,1)S(1)}, u32[]{:S(2)}, u32[]{:S(2)}) collective-permute-start(bf16[128,2560]{1,0:T(8,128)(2,1)} %collective-permute-done.48), channel_id=1, source_target_pairs={{1,0},{5,4},{9,8},{13,12},{17,16},{21,20},{25,24},{29,28}} | collective-permute-start | bytes 1966088 | tf_op jit(solution)/shard_map/ppermute | solution.py:869
  531.8 30.1 %collective-permute-start.43 = (bf16[256,2560]{1,0:T(8,128)(2,1)S(1)}, bf16[256,2560]{1,0:T(8,128)(2,1)S(1)}, u32[]{:S(2)}, u32[]{:S(2)}) collective-permute-start(bf16[256,2560]{1,0:T(8,128)(2,1)S(1)} %get-tuple-element.244), channel_id=1, source_target_pairs={{0,1},{1,2},{4,5},{5,6},{8,9},{9,10},{12,13},{13,14},{16,17},{17,1... | collective-permute-start | bytes 3932168 | tf_op jit(solution)/shard_map/ppermute | solution.py:933
  536.5 25.4 %collective-permute-start.44 = (bf16[256,2560]{1,0:T(8,128)(2,1)S(1)}, bf16[256,2560]{1,0:T(8,128)(2,1)S(1)}, u32[]{:S(2)}, u32[]{:S(2)}) collective-permute-start(bf16[256,2560]{1,0:T(8,128)(2,1)S(1)} %get-tuple-element.245), channel_id=1, source_target_pairs={{3,2},{2,1},{7,6},{6,5},{11,10},{10,9},{15,14},{14,13},{19,18},{18... | collective-permute-start | bytes 3932168 | tf_op jit(solution)/shard_map/ppermute | solution.py:935
  564.0 43.7 %collective-permute-start.45 = (bf16[256,2560]{1,0:T(8,128)(2,1)}, bf16[256,2560]{1,0:T(8,128)(2,1)}, u32[]{:S(2)}, u32[]{:S(2)}) collective-permute-start(bf16[256,2560]{1,0:T(8,128)(2,1)} %get-tuple-element.246), channel_id=1, source_target_pairs={{0,1},{1,2},{2,3},{4,5},{5,6},{6,7},{8,9},{9,10},{10,11},{12,13},{... | collective-permute-start | bytes 3932168 | tf_op jit(solution)/shard_map/ppermute | solution.py:933
  574.0 33.7 %collective-permute-start.46 = (bf16[256,2560]{1,0:T(8,128)(2,1)}, bf16[256,2560]{1,0:T(8,128)(2,1)}, u32[]{:S(2)}, u32[]{:S(2)}) collective-permute-start(bf16[256,2560]{1,0:T(8,128)(2,1)} %get-tuple-element.247), channel_id=1, source_target_pairs={{3,2},{2,1},{1,0},{7,6},{6,5},{5,4},{11,10},{10,9},{9,8},{15,14},{... | collective-permute-start | bytes 3932168 | tf_op jit(solution)/shard_map/ppermute | solution.py:935
  611.8 198.8 %reduce-scatter.11.cloned.1.call-start = ((), (), s32[]{:S(2)}) async-start(), calls=%async_computation.10 | async-start | bytes 6635520 | tf_op jit(solution)/shard_map/reduce_scatter | solution.py:1295
  611.9 55.8 %collective-permute-start.51 = (bf16[256,2560]{1,0:T(8,128)(2,1)S(1)}, bf16[256,2560]{1,0:T(8,128)(2,1)}, u32[]{:S(2)}, u32[]{:S(2)}) collective-permute-start(bf16[256,2560]{1,0:T(8,128)(2,1)S(1)} %fusion.2), channel_id=1, source_target_pairs={{0,1},{1,2},{2,3},{4,5},{5,6},{6,7},{8,9},{9,10},{10,11},{12,13},{... | collective-permute-start | bytes 3932168 | tf_op jit(solution)/shard_map/ppermute | solution.py:868
  617.8 66.4 %collective-permute-start.52 = (bf16[256,2560]{1,0:T(8,128)(2,1)S(1)}, bf16[256,2560]{1,0:T(8,128)(2,1)}, u32[]{:S(2)}, u32[]{:S(2)}) collective-permute-start(bf16[256,2560]{1,0:T(8,128)(2,1)S(1)} %fusion.2), channel_id=1, source_target_pairs={{1,0},{2,1},{3,2},{5,4},{6,5},{7,6},{9,8},{10,9},{11,10},{13,12},{... | collective-permute-start | bytes 3932168 | tf_op jit(solution)/shard_map/ppermute | solution.py:869
  733.1 31.7 %collective-permute-start.53 = (bf16[256,2560]{1,0:T(8,128)(2,1)}, bf16[256,2560]{1,0:T(8,128)(2,1)}, u32[]{:S(2)}, u32[]{:S(2)}) collective-permute-start(bf16[256,2560]{1,0:T(8,128)(2,1)} %collective-permute-done.51), channel_id=1, source_target_pairs={{1,2},{2,3},{5,6},{6,7},{9,10},{10,11},{13,14},{14,15},{17,18},{18... | collective-permute-start | bytes 3932168 | tf_op jit(solution)/shard_map/ppermute | solution.py:868
  734.8 34.0 %collective-permute-start.54 = (bf16[256,2560]{1,0:T(8,128)(2,1)}, bf16[256,2560]{1,0:T(8,128)(2,1)}, u32[]{:S(2)}, u32[]{:S(2)}) collective-permute-start(bf16[256,2560]{1,0:T(8,128)(2,1)} %collective-permute-done.52), channel_id=1, source_target_pairs={{1,0},{2,1},{5,4},{6,5},{9,8},{10,9},{13,12},{14,13},{17,16},{18,1... | collective-permute-start | bytes 3932168 | tf_op jit(solution)/shard_map/ppermute | solution.py:869
  761.7 9.2 %collective-permute-start.57 = (bf16[2,2,96,1056]{3,2,1,0:T(8,128)(2,1)}, bf16[2,2,96,1056]{3,2,1,0:T(8,128)(2,1)}, u32[]{:S(2)}, u32[]{:S(2)}) collective-permute-start(bf16[2,2,96,1056]{3,2,1,0:T(8,128)(2,1)} %fusion.13), channel_id=1, source_target_pairs={{0,4},{4,0},{8,12},{12,8},{16,20},{20,16},{24,28},{28,24},{1,5},{5... | collective-permute-start | bytes 2433032 | tf_op jit(solution)/shard_map/ppermute | solution.py:1000
  768.8 26.0 %collective-permute-start.55 = (bf16[256,2560]{1,0:T(8,128)(2,1)}, bf16[256,2560]{1,0:T(8,128)(2,1)S(1)}, u32[]{:S(2)}, u32[]{:S(2)}) collective-permute-start(bf16[256,2560]{1,0:T(8,128)(2,1)} %collective-permute-done.53), channel_id=1, source_target_pairs={{2,3},{6,7},{10,11},{14,15},{18,19},{22,23},{26,27},{30,31}} | collective-permute-start | bytes 3932168 | tf_op jit(solution)/shard_map/ppermute | solution.py:868
  769.6 31.9 %collective-permute-start.56 = (bf16[256,2560]{1,0:T(8,128)(2,1)}, bf16[256,2560]{1,0:T(8,128)(2,1)}, u32[]{:S(2)}, u32[]{:S(2)}) collective-permute-start(bf16[256,2560]{1,0:T(8,128)(2,1)} %collective-permute-done.54), channel_id=1, source_target_pairs={{1,0},{5,4},{9,8},{13,12},{17,16},{21,20},{25,24},{29,28}} | collective-permute-start | bytes 3932168 | tf_op jit(solution)/shard_map/ppermute | solution.py:869
  772.3 20.9 %collective-permute-start.58 = (bf16[2,96,1056]{2,1,0:T(8,128)(2,1)S(1)}, bf16[2,96,1056]{2,1,0:T(8,128)(2,1)S(1)}, u32[]{:S(2)}, u32[]{:S(2)}) collective-permute-start(bf16[2,96,1056]{2,1,0:T(8,128)(2,1)S(1)} %dynamic-slice_bitcast_fusion.2), channel_id=1, source_target_pairs={{0,8},{4,12},{8,0},{12,4},{16,24},{20,28},{24,16},{28,20},{1,9},{5... | collective-permute-start | bytes 1216520 | tf_op jit(solution)/shard_map/ppermute | solution.py:1000
  793.3 14.8 %collective-permute-start.59 = (bf16[96,1056]{1,0:T(8,128)(2,1)S(1)}, bf16[96,1056]{1,0:T(8,128)(2,1)S(1)}, u32[]{:S(2)}, u32[]{:S(2)}) collective-permute-start(bf16[96,1056]{1,0:T(8,128)(2,1)S(1)} %dynamic-slice_bitcast_fusion.3), channel_id=1, source_target_pairs={{0,16},{4,20},{8,24},{12,28},{16,0},{20,4},{24,8},{28,12},{1,17},{... | collective-permute-start | bytes 608264 | tf_op jit(solution)/shard_map/ppermute | solution.py:1000
  (57 other events, 660.3 us)
Sparse Core Ops, SparseCore 0:
  13.6 157.5 all-gather.2
  173.7 74.3 all-gather.4
  301.6 55.1 reduce-scatter.4
  358.9 65.6 reduce-scatter.6
  439.1 161.8 reduce-scatter.8
  612.0 118.8 all-reduce.4
  734.4 63.1 reduce-scatter.10
